TPU v7x, 512 devices: a whole 4x8x8 slice. The times are simulated.
512 devices in a mesh: row: 16 (over z, core), col: 32 (over x, y).
Axes of the slice: x: 4, y: 8, z: 8, core: 2. Of those that a mesh axis runs over, the one named last changes fastest.
Arguments:
- noise: bfloat16 [4096, 8192], P('row', 'col'), as said below
- data: bfloat16 [8192, 8192], P('col'), as said below
Outputs:
- noise_potential: float32 [4096], P('row')
- data_potential: float32 [8192], P('col')
- targets: bfloat16 [4096, 8192], P('row', 'col')
Inputs may be any that keep to these rules, and one draw needn't show every extreme that they name: noise latents, rows of different scales. data latents, rows of different scales.
All inputs are finite; a program needn't handle non-finite values.
Results may differ from a plain program's by a relative error of at most 0.02.
Values may be sent and summed in bfloat16 or wider, within the bound.
No kernel may reach another device: no remote copies, remote signals or barrier semaphores. Data moves between devices by JAX's collectives and lax.ppermute only.
A program may use at most 64 MiB of HBM per device.

v0:
```python
import jax
import jax.numpy as jnp
from jax import lax
from jax.sharding import PartitionSpec as P

F = 8192
ITERS = 4


EPSILON = 0.01


def row_totals(scores):
    local_top = jnp.max(scores, axis=1)
    top = lax.pmax(local_top, "col")
    total = lax.psum(jnp.sum(jnp.exp(scores - top[:, None]), axis=1), "col")
    return (top, total)


def col_totals(scores):
    local_top = jnp.max(scores, axis=0)
    top = lax.pmax(local_top, "row")
    total = lax.psum(jnp.sum(jnp.exp(scores - top[None, :]), axis=0), "row")
    return (top, total)


def shards(noise, data):
    rows = noise.shape[0]
    cols = data.shape[0]
    data_sq = jnp.einsum("jf,jf->j", data, data, preferred_element_type=jnp.float32)
    gathered = lax.all_gather(noise, "col", axis=1, tiled=True)
    inner = lax.dot_general(
        gathered, data, (((1,), (1,)), ((), ())), preferred_element_type=jnp.float32
    )
    noise_sq = jnp.einsum("if,if->i", gathered, gathered, preferred_element_type=jnp.float32)
    cost = (noise_sq[:, None] + data_sq[None, :] - 2.0 * inner) / F
    log_rows = jnp.log(jnp.float32(rows * lax.axis_size("row")))
    log_cols = jnp.log(jnp.float32(cols * lax.axis_size("col")))
    data_potential = jnp.zeros((cols,), jnp.float32)
    for step in range(ITERS):
        top, total = row_totals((data_potential[None, :] - cost) / EPSILON)
        noise_potential = -EPSILON * (log_rows + top + jnp.log(total))
        top, total = col_totals((noise_potential[:, None] - cost) / EPSILON)
        data_potential = -EPSILON * (log_cols + top + jnp.log(total))
    scores = (data_potential[None, :] - cost) / EPSILON
    top, total = row_totals(scores)
    noise_potential = -EPSILON * (log_rows + top + jnp.log(total))
    weights = (jnp.exp(scores - top[:, None]) / total[:, None]).astype(jnp.bfloat16)
    term = jnp.dot(weights, data, preferred_element_type=jnp.float32)
    targets = lax.psum_scatter(term.astype(jnp.bfloat16), "col", scatter_dimension=1, tiled=True)
    return (noise_potential, data_potential, targets)


def solution(mesh):
    placed = (P("row", "col"), P("col", None))
    return jax.shard_map(
        shards,
        mesh=mesh,
        in_specs=placed,
        out_specs=(P("row"), P("col"), P("row", "col")),
        check_vma=False,
    )
```

profile of v0, /device:TPU:1, one launch (start us, length us, event | category | flops | bytes accessed | tf_op | source)
XLA Modules:
  0.0 1243.4 jit_solution(9124337941990601860)
XLA Ops:
  7.2 0.0 all-gather.2.cloned.1.call-start
  7.2 0.7 all-gather.2.cloned.1.call-update
  7.9 0.0 reduce-scatter.2.cloned.1.call-start
  7.9 3.1 fusion
  11.0 90.7 %all-gather.2.cloned.1.call-done = bf16[256,8192]{1,0:T(8,128)(2,1)} async-done(((bf16[256,256]{1,0:T(8,128)(2,1)}), bf16[256,8192]{1,0:T(8,128)(2,1)}) %all-gather.2.cloned.1.call-update) | async-done | bytes 4194320 | tf_op jit(solution)/shard_map/all_gather | solution.py:31
  101.8 3.3 fusion.1
  105.0 0.2 copy-done
  105.2 3.5 fusion.4
  108.7 59.4 %pmax.63 = f32[256]{0:T(256)S(1)} all-reduce(f32[256]{0:T(256)S(1)} %get-tuple-element.3), channel_id=1, replica_groups=mesh['row'=16,'col'=32] {'col'}, use_global_device_ids=true, to_apply=%region_1.0 | all-reduce | flops 256 | bytes 2048 | tf_op jit(solution)/shard_map/pmax | solution.py:15
  168.1 0.1 exponential_reduce_fusion.7
  168.2 56.0 %psum.63 = f32[256]{0:T(256)S(1)} all-reduce(f32[256]{0:T(256)S(1)} %exponential_reduce_fusion.7), channel_id=1, replica_groups=mesh['row'=16,'col'=32] {'col'}, use_global_device_ids=true, to_apply=%region_3.0 | all-reduce | flops 256 | bytes 2048 | tf_op jit(solution)/shard_map/psum | solution.py:16
  224.2 0.1 fusion.5
  224.3 57.6 %pmax.64 = f32[256]{0:T(256)S(1)} all-reduce(f32[256]{0:T(256)S(1)} %fusion.5), channel_id=1, replica_groups=mesh['row'=16,'col'=32] {'row'}, use_global_device_ids=true, to_apply=%region_5.0 | all-reduce | flops 256 | bytes 2048 | tf_op jit(solution)/shard_map/pmax | solution.py:22
  282.0 0.2 exponential_reduce_fusion.6
  282.2 23.1 %psum.64 = f32[256]{0:T(256)S(1)} all-reduce(f32[256]{0:T(256)S(1)} %exponential_reduce_fusion.6), channel_id=1, replica_groups=mesh['row'=16,'col'=32] {'row'}, use_global_device_ids=true, to_apply=%region_7.0 | all-reduce | flops 256 | bytes 2048 | tf_op jit(solution)/shard_map/psum | solution.py:23
  305.2 0.1 fusion.6
  305.4 57.7 %pmax.65 = f32[256]{0:T(256)S(1)} all-reduce(f32[256]{0:T(256)S(1)} %fusion.6), channel_id=1, replica_groups=mesh['row'=16,'col'=32] {'col'}, use_global_device_ids=true, to_apply=%region_9.0 | all-reduce | flops 256 | bytes 2048 | tf_op jit(solution)/shard_map/pmax | solution.py:15
  363.0 0.1 exponential_reduce_fusion.5
  363.1 56.2 %psum.65 = f32[256]{0:T(256)S(1)} all-reduce(f32[256]{0:T(256)S(1)} %exponential_reduce_fusion.5), channel_id=1, replica_groups=mesh['row'=16,'col'=32] {'col'}, use_global_device_ids=true, to_apply=%region_11.0 | all-reduce | flops 256 | bytes 2048 | tf_op jit(solution)/shard_map/psum | solution.py:16
  419.4 0.1 fusion.7
  419.5 51.3 %pmax.66 = f32[256]{0:T(256)S(1)} all-reduce(f32[256]{0:T(256)S(1)} %fusion.7), channel_id=1, replica_groups=mesh['row'=16,'col'=32] {'row'}, use_global_device_ids=true, to_apply=%region_13.0 | all-reduce | flops 256 | bytes 2048 | tf_op jit(solution)/shard_map/pmax | solution.py:22
  470.8 0.2 exponential_reduce_fusion.4
  471.0 23.5 %psum.66 = f32[256]{0:T(256)S(1)} all-reduce(f32[256]{0:T(256)S(1)} %exponential_reduce_fusion.4), channel_id=1, replica_groups=mesh['row'=16,'col'=32] {'row'}, use_global_device_ids=true, to_apply=%region_15.0 | all-reduce | flops 256 | bytes 2048 | tf_op jit(solution)/shard_map/psum | solution.py:23
  494.6 0.1 fusion.8
  494.7 57.4 %pmax.67 = f32[256]{0:T(256)S(1)} all-reduce(f32[256]{0:T(256)S(1)} %fusion.8), channel_id=1, replica_groups=mesh['row'=16,'col'=32] {'col'}, use_global_device_ids=true, to_apply=%region_17.0 | all-reduce | flops 256 | bytes 2048 | tf_op jit(solution)/shard_map/pmax | solution.py:15
  552.1 0.1 exponential_reduce_fusion.3
  552.3 56.1 %psum.67 = f32[256]{0:T(256)S(1)} all-reduce(f32[256]{0:T(256)S(1)} %exponential_reduce_fusion.3), channel_id=1, replica_groups=mesh['row'=16,'col'=32] {'col'}, use_global_device_ids=true, to_apply=%region_19.0 | all-reduce | flops 256 | bytes 2048 | tf_op jit(solution)/shard_map/psum | solution.py:16
  608.4 0.1 fusion.9
  608.5 51.3 %pmax.68 = f32[256]{0:T(256)S(1)} all-reduce(f32[256]{0:T(256)S(1)} %fusion.9), channel_id=1, replica_groups=mesh['row'=16,'col'=32] {'row'}, use_global_device_ids=true, to_apply=%region_21.0 | all-reduce | flops 256 | bytes 2048 | tf_op jit(solution)/shard_map/pmax | solution.py:22
  659.8 0.2 exponential_reduce_fusion.2
  660.0 23.5 %psum.68 = f32[256]{0:T(256)S(1)} all-reduce(f32[256]{0:T(256)S(1)} %exponential_reduce_fusion.2), channel_id=1, replica_groups=mesh['row'=16,'col'=32] {'row'}, use_global_device_ids=true, to_apply=%region_23.0 | all-reduce | flops 256 | bytes 2048 | tf_op jit(solution)/shard_map/psum | solution.py:23
  683.5 0.1 fusion.10
  683.6 57.4 %pmax.69 = f32[256]{0:T(256)S(1)} all-reduce(f32[256]{0:T(256)S(1)} %fusion.10), channel_id=1, replica_groups=mesh['row'=16,'col'=32] {'col'}, use_global_device_ids=true, to_apply=%region_25.0 | all-reduce | flops 256 | bytes 2048 | tf_op jit(solution)/shard_map/pmax | solution.py:15
  741.1 0.1 exponential_reduce_fusion.1
  741.2 56.1 %psum.69 = f32[256]{0:T(256)S(1)} all-reduce(f32[256]{0:T(256)S(1)} %exponential_reduce_fusion.1), channel_id=1, replica_groups=mesh['row'=16,'col'=32] {'col'}, use_global_device_ids=true, to_apply=%region_27.0 | all-reduce | flops 256 | bytes 2048 | tf_op jit(solution)/shard_map/psum | solution.py:16
  797.3 0.1 fusion.11
  797.4 51.3 %pmax.70 = f32[256]{0:T(256)S(1)} all-reduce(f32[256]{0:T(256)S(1)} %fusion.11), channel_id=1, replica_groups=mesh['row'=16,'col'=32] {'row'}, use_global_device_ids=true, to_apply=%region_29.0 | all-reduce | flops 256 | bytes 2048 | tf_op jit(solution)/shard_map/pmax | solution.py:22
  848.7 0.2 exponential_reduce_fusion
  848.9 23.5 %psum.70 = f32[256]{0:T(256)S(1)} all-reduce(f32[256]{0:T(256)S(1)} %exponential_reduce_fusion), channel_id=1, replica_groups=mesh['row'=16,'col'=32] {'row'}, use_global_device_ids=true, to_apply=%region_31.0 | all-reduce | flops 256 | bytes 2048 | tf_op jit(solution)/shard_map/psum | solution.py:23
  872.5 0.1 fusion.12
  872.6 57.4 %pmax.71 = f32[256]{0:T(256)S(1)} all-reduce(f32[256]{0:T(256)S(1)} %fusion.12), channel_id=1, replica_groups=mesh['row'=16,'col'=32] {'col'}, use_global_device_ids=true, to_apply=%region_33.0 | all-reduce | flops 256 | bytes 2048 | tf_op jit(solution)/shard_map/pmax | solution.py:15
  930.0 0.1 fusion.13
  930.2 56.1 %psum.71 = f32[256]{0:T(256)S(1)} all-reduce(f32[256]{0:T(256)S(1)} %fusion.13), channel_id=1, replica_groups=mesh['row'=16,'col'=32] {'col'}, use_global_device_ids=true, to_apply=%region_35.0 | all-reduce | flops 256 | bytes 2048 | tf_op jit(solution)/shard_map/psum | solution.py:16
  986.3 5.5 convolution_convert_fusion
  991.8 0.0 copy-done.1
  991.8 0.0 reduce-scatter.2.cloned.1.call-update
  991.8 0.6 add_multiply_fusion
  992.4 244.2 %reduce-scatter.2.cloned.1.call-done = bf16[256,256]{1,0:T(8,128)(2,1)} async-done(((bf16[256,8192]{1,0:T(8,128)(2,1)}), bf16[256,256]{1,0:T(8,128)(2,1)}) %reduce-scatter.2.cloned.1.call-update) | async-done | bytes 131088 | tf_op jit(solution)/shard_map/reduce_scatter | solution.py:50
  (10 shorter events, 0.1 us)
Async XLA Ops:
  7.2 94.6 %all-gather.2.cloned.1.call-start = ((), (), s32[]{:S(2)}) async-start(), calls=%async_computation.1 | async-start | bytes 4325376 | tf_op jit(solution)/shard_map/all_gather | solution.py:31
  7.9 1228.7 %reduce-scatter.2.cloned.1.call-start = ((), (), s32[]{:S(2)}) async-start(), calls=%async_computation.2 | async-start | bytes 4325376 | tf_op jit(solution)/shard_map/reduce_scatter | solution.py:50
  101.8 3.4 copy-start
  872.5 119.3 %copy-start.1 = (f32[256]{0:T(256)}, f32[256]{0:T(256)S(1)}, u32[]{:S(2)}) copy-start(f32[256]{0:T(256)S(1)} %add_multiply_fusion.1) | copy-start | bytes 3076
Sparse Core Ops, SparseCore 0:
  11.0 90.6 all-gather.1
  991.9 244.6 reduce-scatter.1
where the time goes:
time: 1250 us; the launch traced here: 1240 us
  blocking collectives  875 us (70%)
  waiting for transfers between devices  336 us (27%)
  between operations  14.1 us (1%)
    pmax x5, blocking collectives, row_totals(): top = lax.pmax(local_top, 'col')  289 us
    psum x5, blocking collectives, row_totals(): total = lax.psum(jnp.sum(jnp.exp(scores - top[:, None]), axis=1), 'col')  280 us
    reduce_scatter x1, waiting for transfers between devices, shards(): lax.psum_scatter(term.astype(jnp.bfloat16), 'col', scatter_dimension=1, t...  244 us
    pmax x4, blocking collectives, col_totals(): top = lax.pmax(local_top, 'row')  211 us
    psum x4, blocking collectives, col_totals(): total = lax.psum(jnp.sum(jnp.exp(scores - top[None, :]), axis=0), 'row')  93.7 us
    all_gather x1, waiting for transfers between devices, shards(): gathered = lax.all_gather(noise, 'col', axis=1, tiled=True)  90.7 us
  transfers between devices with their start and end apart: 2, of which 2 were waited for; matrix products, arithmetic and copies ran while one was open for 0% of the time, Pallas kernels for 0%

commit v1 on v0

v1 whole, which is shorter than its diff:
```python
import jax
import jax.numpy as jnp
from jax import lax
from jax.sharding import Mesh, PartitionSpec as P

ITERS = 4
EPSILON = 0.01
ROW = ("z", "core")
COL = ("x", "y")


def spread(values, axes):
    members = lax.axis_size(axes)
    sent = jnp.broadcast_to(values.reshape(1, -1, 128), (members, values.size // 128, 128))
    return lax.all_to_all(sent, axes, 0, 0).reshape(members, values.size)


def lse(scores, axis):
    top = jnp.max(scores, axis=axis, keepdims=True)
    total = jnp.sum(jnp.exp(scores - top), axis=axis, keepdims=True)
    return jnp.squeeze(top + jnp.log(total), axis)


def shards(noise, data):
    rows, width = noise.shape
    cols, features = data.shape
    nx, ny = lax.axis_size("x"), lax.axis_size("y")
    log_rows = jnp.log(jnp.float32(rows * lax.axis_size(ROW)))
    log_cols = jnp.log(jnp.float32(cols * lax.axis_size(COL)))

    part = lax.all_gather(noise, "x", axis=1, tiled=True)
    gathered = lax.all_gather(part, "y", axis=1, tiled=True)
    by_y = data.reshape(cols, nx, ny, width).transpose(0, 2, 1, 3).reshape(cols, features)

    noise_sq = jnp.sum(jnp.square(noise.astype(jnp.float32)), axis=1)
    data_sq = jnp.sum(jnp.square(data.astype(jnp.float32)), axis=1)
    noise_sq = jnp.sum(spread(noise_sq, COL), axis=0)

    inner = lax.dot_general(
        gathered, by_y, (((1,), (1,)), ((), ())), preferred_element_type=jnp.float32
    )
    scaled = inner * (2.0 / (features * EPSILON))
    col_pot = data_sq * (-1.0 / (features * EPSILON))
    for step in range(ITERS):
        row_lse = lse(spread(lse(col_pot[None, :] + scaled, 1), COL), 0)
        row_pot = -(log_rows + row_lse)
        col_lse = lse(spread(lse(row_pot[:, None] + scaled, 0), ROW), 0)
        col_pot = -(log_cols + col_lse)
    scores = col_pot[None, :] + scaled
    row_lse = lse(spread(lse(scores, 1), COL), 0)
    noise_potential = noise_sq / features - EPSILON * (log_rows + row_lse)
    data_potential = data_sq / features + EPSILON * col_pot
    weights = jnp.exp(scores - row_lse[:, None]).astype(jnp.bfloat16)
    term = jnp.dot(weights, data, preferred_element_type=jnp.float32).astype(jnp.bfloat16)
    part = lax.psum_scatter(term, "x", scatter_dimension=1, tiled=True)
    targets = lax.psum_scatter(part, "y", scatter_dimension=1, tiled=True)
    return (noise_potential, data_potential, targets)


def solution(mesh):
    devices = mesh.devices.reshape(8, 2, 4, 8)
    return jax.shard_map(
        shards,
        mesh=Mesh(devices, ("z", "core", "x", "y")),
        in_specs=(P(ROW, COL), P(COL, None)),
        out_specs=(P(ROW), P(COL), P(ROW, COL)),
        check_vma=False,
    )
```

time: 1250 us -> 322 us (0.26)
  blocking collectives: 875 us -> 103 us
  waiting for transfers between devices: 336 us -> 158 us
  local copies, waits for them, and re-layouts: 0.2 us -> 13 us
  starting transfers between devices: 0.08 us -> 12.6 us
    pmax x9 -> x0, blocking collectives: 501 us -> none  [the longest x5 289 us: row_totals(): top = lax.pmax(local_top, 'col')]
    psum x9 -> x0, blocking collectives: 374 us -> none  [the longest x5 280 us: row_totals(): total = lax.psum(jnp.sum(jnp.exp(scores - top[:, None]), axis=1), 'col')]
    reduce_scatter x1 -> x2, waiting for transfers between devices: 244 us -> 83.7 us  [the longest x1 43.7 us: shards(): part = lax.psum_scatter(term, 'x', scatter_dimension=1, tiled=True)]
    all_to_all x0 -> x7, blocking collectives: none -> 89.9 us  [spread(): return lax.all_to_all(sent, axes, 0, 0).reshape(members, values.size)]
    all_gather x1, waiting for transfers between devices: 90.7 us -> 50.9 us  [shards(): gathered = lax.all_gather(part, 'y', axis=1, tiled=True)]
    all_to_all x0 -> x3, waiting for transfers between devices: none -> 23.8 us  [spread(): return lax.all_to_all(sent, axes, 0, 0).reshape(members, values.size)]
    all_gather x0 -> x1, blocking collectives: none -> 13.3 us  [shards(): part = lax.all_gather(noise, 'x', axis=1, tiled=True)]
  transfers between devices with their start and end apart: 2 -> 6, of which waited for: 2 -> 6; matrix products, arithmetic and copies ran while one was open for 0% -> 4% of each run, Pallas kernels for 0% -> 0%
where the time goes in v1:
time: 322 us; the launch traced here: 317 us
  waiting for transfers between devices  158 us (49%)
  blocking collectives  103 us (32%)
  between operations  14 us (4%)
  local copies, waits for them, and re-layouts  13 us (4%)
  starting transfers between devices  12.6 us (4%)
  matrix products  10.7 us (3%)
  other arithmetic  5.34 us (2%)
    all_to_all x7, blocking collectives, spread(): return lax.all_to_all(sent, axes, 0, 0).reshape(members, values.size)  89.9 us
    all_gather x1, waiting for transfers between devices, shards(): gathered = lax.all_gather(part, 'y', axis=1, tiled=True)  50.9 us
    reduce_scatter x1, waiting for transfers between devices, shards(): part = lax.psum_scatter(term, 'x', scatter_dimension=1, tiled=True)  43.7 us
    reduce_scatter x1, waiting for transfers between devices, shards(): targets = lax.psum_scatter(part, 'y', scatter_dimension=1, tiled=True)  40 us
    all_to_all x3, waiting for transfers between devices, spread(): return lax.all_to_all(sent, axes, 0, 0).reshape(members, values.size)  23.8 us
    all_gather x1, blocking collectives, shards(): part = lax.all_gather(noise, 'x', axis=1, tiled=True)  13.3 us
    all_to_all x3, starting transfers between devices, spread(): return lax.all_to_all(sent, axes, 0, 0).reshape(members, values.size)  12.5 us
  transfers between devices with their start and end apart: 6, of which 6 were waited for; matrix products, arithmetic and copies ran while one was open for 4% of the time, Pallas kernels for 0%

profile of v1, /device:TPU:1, one launch (start us, length us, event | category | flops | bytes accessed | tf_op | source)
XLA Modules:
  0.0 317.4 jit_solution(8713451814744850804)
XLA Ops:
  7.2 0.0 all-gather.2.cloned.1.call-start
  7.2 13.3 %all_gather.6 = bf16[256,1024]{1,0:T(8,128)(2,1)} all-gather(bf16[256,256]{1,0:T(8,128)(2,1)} %param.2), channel_id=1, replica_groups=mesh['z'=8,'core'=2,'x'=4,'y'=8] {'x'}, dimensions={1}, use_global_device_ids=true | all-gather | bytes 655360 | tf_op jit(solution)/shard_map/all_gather | solution.py:31
  20.6 6.4 %copy.31 = bf16[256,8192]{0,1:T(8,128)(2,1)} copy(bf16[256,8192]{1,0:T(8,128)(2,1)} %param.3) | data formatting | bytes 8388608 | tf_op args[1]
  26.9 4.7 %copy.32 = bf16[256,8,4,256]{0,3,2,1:T(8,128)(2,1)} copy(bf16[256,8,4,256]{0,3,1,2:T(8,128)(2,1)} %bitcast.49) | data formatting | bytes 8388608 | tf_op jit(solution)/shard_map/transpose | solution.py:33
  31.7 0.9 multiply_reduce_fusion
  32.6 50.9 %all-gather.2.cloned.1.call-done = bf16[256,8192]{1,0:T(8,128)(2,1)} async-done(((bf16[256,1024]{1,0:T(8,128)(2,1)}), bf16[256,8192]{1,0:T(8,128)(2,1)}) %all-gather.2.cloned.1.call-update) | async-done | bytes 4194320 | tf_op jit(solution)/shard_map/all_gather | solution.py:32
  83.5 5.2 %add_reduce_fusion.7 = (f32[256]{0:T(256)S(1)}, f32[256,256]{0,1:T(8,128)S(1)}) fusion(f32[256]{0:T(256)S(1)} %broadcast_multiply_fusion, bf16[256,8192]{1,0:T(8,128)(2,1)} %all-gather.2.cloned.1.call-done, bf16[256,8192]{0,1:T(8,128)(2,1)} %bitcast.48), kind=kOutput, calls=%fused_computation.21 | convolution fusion | flops 1073938176 | bytes 8652800 | tf_op jit(solution)/shard_map/dot_general | solution.py:39
  88.7 0.1 exponential_reduce_fusion.8
  88.9 15.6 %all_to_all.50 = f32[32,2,128]{2,1,0:T(2,128)S(1)} all-to-all(f32[32,2,128]{2,1,0:T(2,128)S(1)} %broadcast_in_dim.24), channel_id=1, replica_groups=mesh['z'=8,'core'=2,'x'=4,'y'=8] {'x','y'}, dimensions={0} | all-to-all | bytes 65536 | tf_op jit(solution)/shard_map/all_to_all | solution.py:15
  104.6 0.1 add_reduce_fusion.6
  104.7 0.2 exponential_reduce_fusion.7
  104.9 16.6 %all_to_all.51 = f32[16,2,128]{2,1,0:T(2,128)S(1)} all-to-all(f32[16,2,128]{2,1,0:T(2,128)S(1)} %broadcast_in_dim.25), channel_id=1, replica_groups=mesh['z'=8,'core'=2,'x'=4,'y'=8] {'z','core'}, dimensions={0} | all-to-all | bytes 32768 | tf_op jit(solution)/shard_map/all_to_all | solution.py:15
  121.6 0.1 add_reduce_fusion.5
  121.7 0.1 exponential_reduce_fusion.6
  121.9 11.7 %all_to_all.52 = f32[32,2,128]{2,1,0:T(2,128)S(1)} all-to-all(f32[32,2,128]{2,1,0:T(2,128)S(1)} %broadcast_in_dim.26), channel_id=1, replica_groups=mesh['z'=8,'core'=2,'x'=4,'y'=8] {'x','y'}, dimensions={0} | all-to-all | bytes 65536 | tf_op jit(solution)/shard_map/all_to_all | solution.py:15
  133.7 0.1 add_reduce_fusion.4
  133.8 0.2 exponential_reduce_fusion.5
  134.0 11.3 %all_to_all.53 = f32[16,2,128]{2,1,0:T(2,128)S(1)} all-to-all(f32[16,2,128]{2,1,0:T(2,128)S(1)} %broadcast_in_dim.27), channel_id=1, replica_groups=mesh['z'=8,'core'=2,'x'=4,'y'=8] {'z','core'}, dimensions={0} | all-to-all | bytes 32768 | tf_op jit(solution)/shard_map/all_to_all | solution.py:15
  145.4 0.1 add_reduce_fusion.3
  145.5 0.1 exponential_reduce_fusion.4
  145.7 11.7 %all_to_all.54 = f32[32,2,128]{2,1,0:T(2,128)S(1)} all-to-all(f32[32,2,128]{2,1,0:T(2,128)S(1)} %broadcast_in_dim.28), channel_id=1, replica_groups=mesh['z'=8,'core'=2,'x'=4,'y'=8] {'x','y'}, dimensions={0} | all-to-all | bytes 65536 | tf_op jit(solution)/shard_map/all_to_all | solution.py:15
  157.5 0.1 add_reduce_fusion.2
  157.6 0.2 exponential_reduce_fusion.3
  157.8 11.3 %all_to_all.55 = f32[16,2,128]{2,1,0:T(2,128)S(1)} all-to-all(f32[16,2,128]{2,1,0:T(2,128)S(1)} %broadcast_in_dim.29), channel_id=1, replica_groups=mesh['z'=8,'core'=2,'x'=4,'y'=8] {'z','core'}, dimensions={0} | all-to-all | bytes 32768 | tf_op jit(solution)/shard_map/all_to_all | solution.py:15
  169.2 0.1 add_reduce_fusion.1
  169.3 0.1 exponential_reduce_fusion.2
  169.5 11.7 %all_to_all.56 = f32[32,2,128]{2,1,0:T(2,128)S(1)} all-to-all(f32[32,2,128]{2,1,0:T(2,128)S(1)} %broadcast_in_dim.30), channel_id=1, replica_groups=mesh['z'=8,'core'=2,'x'=4,'y'=8] {'x','y'}, dimensions={0} | all-to-all | bytes 65536 | tf_op jit(solution)/shard_map/all_to_all | solution.py:15
  181.3 0.1 add_reduce_fusion
  181.4 0.2 exponential_reduce_fusion.1
  181.6 0.6 broadcast_in_dim.31
  182.2 4.7 %all-to-all-start.8 = ((f32[16,2,128]{2,1,0:T(2,128)}), f32[16,2,128]{2,1,0:T(2,128)S(1)}, u32[]{:S(2)}, u32[]{:S(2)}) async-start(f32[16,2,128]{2,1,0:T(2,128)} %broadcast_in_dim.31), calls=%async_computation.8 | async-start | bytes 32768 | tf_op jit(solution)/shard_map/all_to_all | solution.py:15
  187.0 0.1 multiply_reduce_fusion.1
  187.1 7.3 %all-to-all-done.8 = f32[16,2,128]{2,1,0:T(2,128)S(1)} async-done(((f32[16,2,128]{2,1,0:T(2,128)}), f32[16,2,128]{2,1,0:T(2,128)S(1)}, u32[]{:S(2)}, u32[]{:S(2)}) %all-to-all-start.8) | async-done | bytes 16416 | tf_op jit(solution)/shard_map/all_to_all | solution.py:15
  194.4 0.6 broadcast_in_dim.23
  195.0 3.9 %all-to-all-start = ((f32[32,2,128]{2,1,0:T(2,128)}), f32[32,2,128]{2,1,0:T(2,128)S(1)}, u32[]{:S(2)}, u32[]{:S(2)}) async-start(f32[32,2,128]{2,1,0:T(2,128)} %broadcast_in_dim.23), calls=%async_computation | async-start | bytes 65536 | tf_op jit(solution)/shard_map/all_to_all | solution.py:15
  199.0 0.6 multiply_add_fusion
  199.5 0.1 add_reduce_fusion.8
  199.6 0.1 exponential_reduce_fusion
  199.8 7.9 %all-to-all-done = f32[32,2,128]{2,1,0:T(2,128)S(1)} async-done(((f32[32,2,128]{2,1,0:T(2,128)}), f32[32,2,128]{2,1,0:T(2,128)S(1)}, u32[]{:S(2)}, u32[]{:S(2)}) %all-to-all-start) | async-done | bytes 32800 | tf_op jit(solution)/shard_map/all_to_all | solution.py:15
  207.7 0.6 broadcast_in_dim.32
  208.3 3.9 %all-to-all-start.9 = ((f32[32,2,128]{2,1,0:T(2,128)}), f32[32,2,128]{2,1,0:T(2,128)S(1)}, u32[]{:S(2)}, u32[]{:S(2)}) async-start(f32[32,2,128]{2,1,0:T(2,128)} %broadcast_in_dim.32), calls=%async_computation.9 | async-start | bytes 65536 | tf_op jit(solution)/shard_map/all_to_all | solution.py:15
  212.2 0.0 reduce-scatter.3.cloned.1.call-start
  212.3 8.6 %all-to-all-done.9 = f32[32,2,128]{2,1,0:T(2,128)S(1)} async-done(((f32[32,2,128]{2,1,0:T(2,128)}), f32[32,2,128]{2,1,0:T(2,128)S(1)}, u32[]{:S(2)}, u32[]{:S(2)}) %all-to-all-start.9) | async-done | bytes 32800 | tf_op jit(solution)/shard_map/all_to_all | solution.py:15
  220.9 0.6 bitcast_subtract_fusion
  221.5 5.5 %convolution_convert_fusion = bf16[256,8192]{1,0:T(8,128)(2,1)} fusion(bf16[256,8192]{1,0:T(8,128)(2,1)} %param.3, f32[256,256]{0,1:T(8,128)S(1)} %get-tuple-element.8, f32[256]{0:T(256)S(1)} %get-tuple-element.6, f32[256]{0:T(256)S(1)} %get-tuple-element.4), kind=kOutput, calls=%fused_computation | convolution fusion | flops 1076035584 | bytes 8652800 | tf_op jit(solution)/shard_map/dot_general | solution.py:54
  227.0 0.0 reduce-scatter.5.cloned.1.call-start
  227.1 43.7 %reduce-scatter.3.cloned.1.call-done = bf16[256,2048]{1,0:T(8,128)(2,1)} async-done(((bf16[256,8192]{1,0:T(8,128)(2,1)}), bf16[256,2048]{1,0:T(8,128)(2,1)}) %reduce-scatter.3.cloned.1.call-update) | async-done | bytes 1048592 | tf_op jit(solution)/shard_map/reduce_scatter | solution.py:55
  270.8 40.0 %reduce-scatter.5.cloned.1.call-done = bf16[256,256]{1,0:T(8,128)(2,1)} async-done(((bf16[256,2048]{1,0:T(8,128)(2,1)}), bf16[256,256]{1,0:T(8,128)(2,1)}) %reduce-scatter.5.cloned.1.call-update) | async-done | bytes 131088 | tf_op jit(solution)/shard_map/reduce_scatter | solution.py:56
  (50 shorter events, 0.9 us)
Async XLA Ops:
  7.2 76.3 %all-gather.2.cloned.1.call-start = ((), (), s32[]{:S(2)}) async-start(), calls=%async_computation.12 | async-start | bytes 4718592 | tf_op jit(solution)/shard_map/all_gather | solution.py:32
  26.9 4.7 %copy-start = (bf16[256,8192]{1,0:T(8,128)(2,1)S(1)}, bf16[256,8192]{1,0:T(8,128)(2,1)}, u32[]{:S(2)}) copy-start(bf16[256,8192]{1,0:T(8,128)(2,1)} %param.3) | copy-start | bytes 12582916
  88.7 98.3 %copy-start.1 = (bf16[256,256]{1,0:T(8,128)(2,1)S(1)}, bf16[256,256]{1,0:T(8,128)(2,1)}, u32[]{:S(2)}) copy-start(bf16[256,256]{1,0:T(8,128)(2,1)} %param.2) | copy-start | bytes 393220
  182.2 12.2 %all-to-all-start.8 = ((f32[16,2,128]{2,1,0:T(2,128)}), f32[16,2,128]{2,1,0:T(2,128)S(1)}, u32[]{:S(2)}, u32[]{:S(2)}) async-start(f32[16,2,128]{2,1,0:T(2,128)} %broadcast_in_dim.31), calls=%async_computation.8 | async-start | bytes 32768 | tf_op jit(solution)/shard_map/all_to_all | solution.py:15
  195.0 12.6 %all-to-all-start = ((f32[32,2,128]{2,1,0:T(2,128)}), f32[32,2,128]{2,1,0:T(2,128)S(1)}, u32[]{:S(2)}, u32[]{:S(2)}) async-start(f32[32,2,128]{2,1,0:T(2,128)} %broadcast_in_dim.23), calls=%async_computation | async-start | bytes 65536 | tf_op jit(solution)/shard_map/all_to_all | solution.py:15
  208.3 12.6 %all-to-all-start.9 = ((f32[32,2,128]{2,1,0:T(2,128)}), f32[32,2,128]{2,1,0:T(2,128)S(1)}, u32[]{:S(2)}, u32[]{:S(2)}) async-start(f32[32,2,128]{2,1,0:T(2,128)} %broadcast_in_dim.32), calls=%async_computation.9 | async-start | bytes 65536 | tf_op jit(solution)/shard_map/all_to_all | solution.py:15
  212.2 58.6 %reduce-scatter.3.cloned.1.call-start = ((), (), s32[]{:S(2)}) async-start(), calls=%async_computation.13 | async-start | bytes 5242880 | tf_op jit(solution)/shard_map/reduce_scatter | solution.py:55
  227.0 83.8 %reduce-scatter.5.cloned.1.call-start = ((), (), s32[]{:S(2)}) async-start(), calls=%async_computation.14 | async-start | bytes 1179648 | tf_op jit(solution)/shard_map/reduce_scatter | solution.py:56
Sparse Core Ops, SparseCore 0:
  20.7 62.7 all-gather.1
  227.1 43.5 reduce-scatter.2
  274.4 36.3 reduce-scatter.4

commit v2 on v1

v2 whole, which is shorter than its diff:
```python
import jax
import jax.numpy as jnp
from jax import lax
from jax.sharding import Mesh, PartitionSpec as P

ITERS = 4
EPSILON = 0.01
ROW = ("z", "core")
COL = ("x", "y")


def spread(values, axes):
    members = lax.axis_size(axes)
    sent = jnp.broadcast_to(values.reshape(1, -1, 128), (members, values.size // 128, 128))
    return lax.all_to_all(sent, axes, 0, 0).reshape(members, *values.shape)


def lse(scores, axis):
    top = jnp.max(scores, axis=axis, keepdims=True)
    total = jnp.sum(jnp.exp(scores - top), axis=axis, keepdims=True)
    return jnp.squeeze(top + jnp.log(total), axis)


def parts_of(values):
    first = lax.reduce_precision(values, 8, 7)
    second = lax.reduce_precision(values - first, 8, 7)
    third = values - first - second
    return jnp.stack([first, second, third]).astype(jnp.bfloat16)


def shards(noise, data):
    rows, width = noise.shape
    cols, features = data.shape
    nx, ny, nrow = lax.axis_size("x"), lax.axis_size("y"), lax.axis_size(ROW)
    log_rows = jnp.log(jnp.float32(rows * nrow))
    log_cols = jnp.log(jnp.float32(cols * nx * ny))

    part = lax.all_gather(noise, "x", axis=1, tiled=True)
    gathered = lax.all_gather(part, "y", axis=1, tiled=True)
    by_y = data.reshape(cols, nx, ny, width).transpose(0, 2, 1, 3).reshape(cols, features)

    share = cols // nrow
    piece = lax.dynamic_slice_in_dim(by_y, lax.axis_index(ROW) * share, share, 0)
    piece = piece.reshape(share, ny, nx * width).transpose(1, 0, 2)
    piece = lax.all_to_all(piece, "y", 0, 0)
    mine = lax.all_gather(piece, ROW, axis=1, tiled=True).reshape(ny * cols, nx * width)

    noise_sq = jnp.sum(jnp.square(noise.astype(jnp.float32)), axis=1)
    data_sq = jnp.sum(jnp.square(data.astype(jnp.float32)), axis=1)

    inner = lax.dot_general(
        gathered, by_y, (((1,), (1,)), ((), ())), preferred_element_type=jnp.float32
    )
    scaled = inner * (2.0 / (features * EPSILON))
    wide = lax.all_gather(scaled, "y", axis=1, tiled=True)

    col_pot = data_sq * (-1.0 / (features * EPSILON))
    for step in range(ITERS):
        local = lse(col_pot[None, :] + scaled, 1)
        if step == 0:
            got = spread(jnp.stack([local, noise_sq]), COL)
            noise_sq = jnp.sum(got[:, 1], axis=0)
            row_lse = lse(got[:, 0], 0)
        else:
            row_lse = lse(spread(local, COL), 0)
        row_pot = -(log_rows + row_lse)
        block = wide if step == ITERS - 1 else scaled
        col_pot = -(log_cols + lse(spread(lse(row_pot[:, None] + block, 0), ROW), 0))
    own = lax.dynamic_slice_in_dim(col_pot, lax.axis_index("y") * cols, cols, 0)
    data_potential = data_sq / features + EPSILON * own

    scores = col_pot[None, :] + wide
    top = jnp.max(scores, axis=1, keepdims=True)
    weights = jnp.exp(scores - top)
    total = jnp.sum(weights, axis=1, keepdims=True)
    term = jnp.dot(weights.astype(jnp.bfloat16), mine, preferred_element_type=jnp.float32)
    term = (term / total).astype(jnp.bfloat16).reshape(rows, nx, width).transpose(1, 0, 2)
    local = (top + jnp.log(total))[:, 0]
    extra = jnp.pad(parts_of(local), ((0, 13), (0, 0)))
    extra = jnp.broadcast_to(extra[None], (nx, 16, rows))
    got = lax.all_to_all(jnp.concatenate([term, extra], axis=1), "x", 0, 0)
    locals_ = jnp.sum(got[:, rows : rows + 3].astype(jnp.float32), axis=1)
    row_lse = lse(locals_, 0)
    scale = jnp.exp(locals_ - row_lse[None])
    targets = jnp.sum(scale[:, :, None] * got[:, :rows].astype(jnp.float32), axis=0)
    noise_potential = noise_sq / features - EPSILON * (log_rows + row_lse)
    return (noise_potential, data_potential, targets.astype(jnp.bfloat16))


def solution(mesh):
    devices = mesh.devices.reshape(8, 2, 4, 8)
    return jax.shard_map(
        shards,
        mesh=Mesh(devices, ("z", "core", "x", "y")),
        in_specs=(P(ROW, COL), P(COL, None)),
        out_specs=(P(ROW), P(COL), P(ROW, COL)),
        check_vma=False,
    )
```

time: 322 us -> 246 us (0.76); the launches traced: 317 us -> 245 us
  waiting for transfers between devices: 158 us -> 63.2 us
  blocking collectives: 103 us -> 118 us
  local copies, waits for them, and re-layouts: 13 us -> 23.8 us
  other arithmetic: 5.34 us -> 10.2 us
  starting transfers between devices: 12.6 us -> 8.36 us
  matrix products: 10.7 us -> 7.41 us
    reduce_scatter x2 -> x0, waiting for transfers between devices: 83.7 us -> none  [the longest x1 43.7 us: shards(): part = lax.psum_scatter(term, 'x', scatter_dimension=1, tiled=True)]
    all_to_all x7 -> x8, blocking collectives: 89.9 us -> 105 us  [the longest x7 90.4 us: spread(): return lax.all_to_all(sent, axes, 0, 0).reshape(members, *values.shape)]
    all_to_all x3 -> x2, waiting for transfers between devices: 23.8 us -> 12.3 us  [the longest x1 9.54 us: shards(): got = lax.all_to_all(jnp.concatenate([term, extra], axis=1), 'x', 0, 0)]
    all_gather x0 -> x1, local copies, waits for them, and re-layouts: none -> 6.48 us  [shards(): lax.all_gather(piece, ROW, axis=1, tiled=True)]
    all_to_all x3 -> x2, starting transfers between devices: 12.5 us -> 8.24 us  [the longest x1 4.77 us: spread(): return lax.all_to_all(sent, axes, 0, 0).reshape(members, *values.shape)]
    dot_general x1, matrix products: 5.49 us -> 1.45 us  [shards(): jnp.dot(weights.astype(jnp.bfloat16), mine, preferred_element_type=jnp.fl...]
    unnamed x5 -> x11, local copies, waits for them, and re-layouts: 6.37 us -> 7.88 us
  transfers between devices with their start and end apart: 6 -> 5, of which waited for: 6 -> 3; matrix products, arithmetic and copies ran while one was open for 4% -> 12% of each run, Pallas kernels for 0% -> 0%
where the time goes in v2:
time: 246 us; the launch traced here: 245 us
  blocking collectives  118 us (48%)
  waiting for transfers between devices  63.2 us (26%)
  local copies, waits for them, and re-layouts  23.8 us (10%)
  between operations  14.1 us (6%)
  other arithmetic  10.2 us (4%)
  starting transfers between devices  8.36 us (3%)
  matrix products  7.41 us (3%)
    all_to_all x7, blocking collectives, spread(): return lax.all_to_all(sent, axes, 0, 0).reshape(members, *values.shape)  90.4 us
    all_gather x1, waiting for transfers between devices, shards(): gathered = lax.all_gather(part, 'y', axis=1, tiled=True)  50.8 us
    all_to_all x1, blocking collectives, shards(): piece = lax.all_to_all(piece, 'y', 0, 0)  14.3 us
    all_gather x1, blocking collectives, shards(): part = lax.all_gather(noise, 'x', axis=1, tiled=True)  13.3 us
    all_to_all x1, waiting for transfers between devices, shards(): got = lax.all_to_all(jnp.concatenate([term, extra], axis=1), 'x', 0, 0)  9.54 us
    unnamed x11, local copies, waits for them, and re-layouts  7.88 us
    all_gather x1, local copies, waits for them, and re-layouts, shards(): lax.all_gather(piece, ROW, axis=1, tiled=True)  6.48 us
    dot_general x1, matrix products, shards(): lax.dot_general(gathered, by_y, (((1,), (1,)), ((), ())), preferred_eleme...  5.96 us
  transfers between devices with their start and end apart: 5, of which 3 were waited for; matrix products, arithmetic and copies ran while one was open for 12% of the time, Pallas kernels for 0%

profile of v2, /device:TPU:1, one launch (start us, length us, event | category | flops | bytes accessed | tf_op | source)
XLA Modules:
  0.0 245.1 jit_solution(16787207837518185352)
XLA Ops:
  7.2 13.3 %all_gather.12 = bf16[256,1024]{1,0:T(8,128)(2,1)} all-gather(bf16[256,256]{1,0:T(8,128)(2,1)} %param.2), channel_id=1, replica_groups=mesh['z'=8,'core'=2,'x'=4,'y'=8] {'x'}, dimensions={1}, use_global_device_ids=true | all-gather | bytes 655360 | tf_op jit(solution)/shard_map/all_gather | solution.py:38
  20.6 6.4 %copy.57 = bf16[256,8192]{0,1:T(8,128)(2,1)} copy(bf16[256,8192]{1,0:T(8,128)(2,1)} %param.3) | data formatting | bytes 8388608 | tf_op args[1]
  27.0 4.7 %copy.58 = bf16[256,8,4,256]{0,3,2,1:T(8,128)(2,1)} copy(bf16[256,8,4,256]{0,3,1,2:T(8,128)(2,1)} %bitcast.58) | data formatting | bytes 8388608 | tf_op jit(solution)/shard_map/transpose | solution.py:40
  31.7 0.9 multiply_reduce_fusion
  32.7 50.8 %all-gather.4.cloned.1.call-done = bf16[256,8192]{1,0:T(8,128)(2,1)} async-done(((bf16[256,1024]{1,0:T(8,128)(2,1)}), bf16[256,8192]{1,0:T(8,128)(2,1)}) %all-gather.4.cloned.1.call-update) | async-done | bytes 4194320 | tf_op jit(solution)/shard_map/all_gather | solution.py:39
  83.5 6.0 %add_reduce_fusion.8 = (f32[256]{0:T(256)S(1)}, f32[256,256]{0,1:T(8,128)}) fusion(f32[256]{0:T(256)S(1)} %broadcast_multiply_fusion, bf16[256,8192]{1,0:T(8,128)(2,1)} %all-gather.4.cloned.1.call-done, bf16[256,8192]{0,1:T(8,128)(2,1)} %bitcast.56), kind=kOutput, calls=%fused_computation.29 | convolution fusion | flops 1073938176 | bytes 8652800 | tf_op jit(solution)/shard_map/dot_general | solution.py:51
  89.5 2.2 constant_dynamic-slice_fusion
  91.8 0.8 copy.74
  92.6 14.3 %all_to_all.50 = bf16[8,16,1024]{2,1,0:T(8,128)(2,1)S(1)} all-to-all(bf16[8,16,1024]{2,1,0:T(8,128)(2,1)S(1)} %copy.74), channel_id=1, replica_groups=mesh['z'=8,'core'=2,'x'=4,'y'=8] {'y'}, dimensions={0} | all-to-all | bytes 524288 | tf_op jit(solution)/shard_map/all_to_all | solution.py:45
  106.9 0.8 copy.75
  107.8 0.1 multiply_reduce_fusion.2
  107.9 0.1 exponential_reduce_fusion.7
  108.1 14.5 %all_to_all.51 = f32[32,4,128]{2,1,0:T(4,128)S(1)} all-to-all(f32[32,4,128]{2,1,0:T(4,128)S(1)} %broadcast_in_dim.21), channel_id=1, replica_groups=mesh['z'=8,'core'=2,'x'=4,'y'=8] {'x','y'}, dimensions={0} | all-to-all | bytes 131072 | tf_op jit(solution)/shard_map/all_to_all | solution.py:15
  122.8 0.1 add_reduce_fusion.7
  122.9 0.2 exponential_reduce_fusion.6
  123.2 17.9 %all_to_all.52 = f32[16,2,128]{2,1,0:T(2,128)S(1)} all-to-all(f32[16,2,128]{2,1,0:T(2,128)S(1)} %broadcast_in_dim.22), channel_id=1, replica_groups=mesh['z'=8,'core'=2,'x'=4,'y'=8] {'z','core'}, dimensions={0} | all-to-all | bytes 32768 | tf_op jit(solution)/shard_map/all_to_all | solution.py:15
  141.1 0.1 add_reduce_fusion.6
  141.2 0.1 exponential_reduce_fusion.5
  141.4 11.7 %all_to_all.53 = f32[32,2,128]{2,1,0:T(2,128)S(1)} all-to-all(f32[32,2,128]{2,1,0:T(2,128)S(1)} %broadcast_in_dim.23), channel_id=1, replica_groups=mesh['z'=8,'core'=2,'x'=4,'y'=8] {'x','y'}, dimensions={0} | all-to-all | bytes 65536 | tf_op jit(solution)/shard_map/all_to_all | solution.py:15
  153.1 0.1 add_reduce_fusion.5
  153.2 0.2 exponential_reduce_fusion.4
  153.5 11.6 %all_to_all.54 = f32[16,2,128]{2,1,0:T(2,128)S(1)} all-to-all(f32[16,2,128]{2,1,0:T(2,128)S(1)} %broadcast_in_dim.24), channel_id=1, replica_groups=mesh['z'=8,'core'=2,'x'=4,'y'=8] {'z','core'}, dimensions={0} | all-to-all | bytes 32768 | tf_op jit(solution)/shard_map/all_to_all | solution.py:15
  165.2 0.1 add_reduce_fusion.4
  165.3 0.1 exponential_reduce_fusion.3
  165.5 11.7 %all_to_all.55 = f32[32,2,128]{2,1,0:T(2,128)S(1)} all-to-all(f32[32,2,128]{2,1,0:T(2,128)S(1)} %broadcast_in_dim.25), channel_id=1, replica_groups=mesh['z'=8,'core'=2,'x'=4,'y'=8] {'x','y'}, dimensions={0} | all-to-all | bytes 65536 | tf_op jit(solution)/shard_map/all_to_all | solution.py:15
  177.3 0.1 add_reduce_fusion.3
  177.4 0.2 exponential_reduce_fusion.2
  177.6 11.3 %all_to_all.56 = f32[16,2,128]{2,1,0:T(2,128)S(1)} all-to-all(f32[16,2,128]{2,1,0:T(2,128)S(1)} %broadcast_in_dim.26), channel_id=1, replica_groups=mesh['z'=8,'core'=2,'x'=4,'y'=8] {'z','core'}, dimensions={0} | all-to-all | bytes 32768 | tf_op jit(solution)/shard_map/all_to_all | solution.py:15
  189.0 0.1 add_reduce_fusion.2
  189.1 0.1 exponential_reduce_fusion.1
  189.3 11.7 %all_to_all.57 = f32[32,2,128]{2,1,0:T(2,128)S(1)} all-to-all(f32[32,2,128]{2,1,0:T(2,128)S(1)} %broadcast_in_dim.27), channel_id=1, replica_groups=mesh['z'=8,'core'=2,'x'=4,'y'=8] {'x','y'}, dimensions={0} | all-to-all | bytes 65536 | tf_op jit(solution)/shard_map/all_to_all | solution.py:15
  201.1 2.1 add_reduce_fusion.1
  203.2 0.1 copy-done.1
  203.3 0.8 exponential_reduce_fusion
  204.1 0.7 broadcast_in_dim.28
  204.8 4.8 %all-to-all-start.7 = ((f32[16,16,128]{2,1,0:T(8,128)}), f32[16,16,128]{2,1,0:T(8,128)S(1)}, u32[]{:S(2)}, u32[]{:S(2)}) async-start(f32[16,16,128]{2,1,0:T(8,128)} %broadcast_in_dim.28), calls=%async_computation.7 | async-start | bytes 262144 | tf_op jit(solution)/shard_map/all_to_all | solution.py:15
  209.6 6.5 %copy.76 = bf16[8,256,1024]{2,1,0:T(8,128)(2,1)} copy(bf16[8,256,1024]{2,0,1:T(8,128)(2,1)} %all-gather.8.cloned.1.call-done) | data formatting | bytes 8388608 | tf_op jit(solution)/shard_map/all_gather | solution.py:46
  216.1 2.7 %all-to-all-done.7 = f32[16,16,128]{2,1,0:T(8,128)S(1)} async-done(((f32[16,16,128]{2,1,0:T(8,128)}), f32[16,16,128]{2,1,0:T(8,128)S(1)}, u32[]{:S(2)}, u32[]{:S(2)}) %all-to-all-start.7) | async-done | bytes 131104 | tf_op jit(solution)/shard_map/all_to_all | solution.py:15
  218.9 0.4 add_reduce_fusion
  219.2 0.4 fusion
  219.7 1.4 copy-done.3
  221.1 1.4 fusion.2
  222.6 0.8 pad_maximum_fusion
  223.4 3.5 %all-to-all-start.9 = ((bf16[4,272,256]{2,1,0:T(8,128)(2,1)}), bf16[4,272,256]{2,1,0:T(8,128)(2,1)S(1)}, u32[]{:S(2)}, u32[]{:S(2)}) async-start(bf16[4,272,256]{2,1,0:T(8,128)(2,1)} %pad_maximum_fusion), calls=%async_computation.9 | async-start | bytes 1114112 | tf_op jit(solution)/shard_map/all_to_all | solution.py:81
  226.9 0.6 multiply_add_fusion
  227.5 9.5 %all-to-all-done.9 = bf16[4,272,256]{2,1,0:T(8,128)(2,1)S(1)} async-done(((bf16[4,272,256]{2,1,0:T(8,128)(2,1)}), bf16[4,272,256]{2,1,0:T(8,128)(2,1)S(1)}, u32[]{:S(2)}, u32[]{:S(2)}) %all-to-all-start.9) | async-done | bytes 557088 | tf_op jit(solution)/shard_map/all_to_all | solution.py:81
  237.2 0.6 multiply_subtract_fusion
  237.8 0.9 multiply_reduce_fusion.1
  (69 shorter events, 1.2 us)
Async XLA Ops:
  7.2 76.3 %all-gather.4.cloned.1.call-start = ((), (), s32[]{:S(2)}) async-start(), calls=%async_computation.10 | async-start | bytes 4718592 | tf_op jit(solution)/shard_map/all_gather | solution.py:39
  20.6 180.6 %all-gather.6.cloned.1.call-start = ((), (), s32[]{:S(2)}) async-start(), calls=%async_computation.11 | async-start | bytes 2359296 | tf_op jit(solution)/shard_map/all_gather | solution.py:55
  27.0 4.7 %copy-start.2 = (bf16[256,8192]{1,0:T(8,128)(2,1)S(1)}, bf16[256,8192]{1,0:T(8,128)(2,1)}, u32[]{:S(2)}) copy-start(bf16[256,8192]{1,0:T(8,128)(2,1)} %param.3) | copy-start | bytes 12582916
  89.5 120.1 %all-gather.8.cloned.1.call-start = ((), (), s32[]{:S(2)}) async-start(), calls=%async_computation.12 | async-start | bytes 4456448 | tf_op jit(solution)/shard_map/all_gather | solution.py:46
  91.8 16.0 %copy-start.4 = (bf16[256,256]{1,0:T(8,128)(2,1)S(1)}, bf16[256,256]{1,0:T(8,128)(2,1)}, u32[]{:S(2)}) copy-start(bf16[256,256]{1,0:T(8,128)(2,1)} %param.2) | copy-start | bytes 393220
  91.8 16.1 %copy-start = (f32[256,256]{0,1:T(8,128)S(1)}, f32[256,256]{0,1:T(8,128)}, u32[]{:S(2)}) copy-start(f32[256,256]{0,1:T(8,128)} %get-tuple-element.12) | copy-start | bytes 786436
  201.1 2.2 copy-start.1
  204.8 14.0 %all-to-all-start.7 = ((f32[16,16,128]{2,1,0:T(8,128)}), f32[16,16,128]{2,1,0:T(8,128)S(1)}, u32[]{:S(2)}, u32[]{:S(2)}) async-start(f32[16,16,128]{2,1,0:T(8,128)} %broadcast_in_dim.28), calls=%async_computation.7 | async-start | bytes 262144 | tf_op jit(solution)/shard_map/all_to_all | solution.py:15
  218.9 2.2 copy-start.3
  223.4 13.7 %all-to-all-start.9 = ((bf16[4,272,256]{2,1,0:T(8,128)(2,1)}), bf16[4,272,256]{2,1,0:T(8,128)(2,1)S(1)}, u32[]{:S(2)}, u32[]{:S(2)}) async-start(bf16[4,272,256]{2,1,0:T(8,128)(2,1)} %pad_maximum_fusion), calls=%async_computation.9 | async-start | bytes 1114112 | tf_op jit(solution)/shard_map/all_to_all | solution.py:81
Sparse Core Ops, SparseCore 0:
  20.7 62.7 all-gather.3
  89.6 40.3 all-gather.5
  132.1 47.7 all-gather.7

commit v3 on v1

v3 whole, which is shorter than its diff:
```python
import functools

import jax
import jax.numpy as jnp
import numpy as np
from jax import lax
from jax.experimental import pallas as pl
from jax.experimental.pallas import tpu as pltpu
from jax.sharding import Mesh, PartitionSpec as P

ITERS = 4
EPSILON = 0.01
ROW = ("z", "core")
COL = ("x", "y")
LANES = 128
FIRST_ROWS = 160
VMEM = pl.BlockSpec(memory_space=pltpu.VMEM)
ANY = pl.BlockSpec(memory_space=pl.ANY)
PARAMS = pltpu.CompilerParams(vmem_limit_bytes=40 * 2**20)


def spread(values, axes):
    members = lax.axis_size(axes)
    sent = jnp.broadcast_to(values.reshape(1, -1, LANES), (members, values.size // LANES, LANES))
    return lax.all_to_all(sent, axes, 0, 0).reshape(members, *values.shape)


def lse(scores, axis):
    top = jnp.max(scores, axis=axis, keepdims=True)
    total = jnp.sum(jnp.exp(scores - top), axis=axis, keepdims=True)
    return jnp.squeeze(top + jnp.log(total), axis)


def as_column(values):
    return jnp.broadcast_to(values, (LANES, values.shape[1])).T


def as_rows(column):
    return jnp.broadcast_to(column, (column.shape[0], LANES)).T


def joined(got_ref):
    got = got_ref[...]
    top = jnp.max(got, axis=0)
    return top + jnp.log(jnp.sum(jnp.exp(got - top[None]), axis=0))


def inner_kernel(scale, nx, steps, first_ref, second_ref, *rest):
    data_refs, (out_ref, total) = rest[:nx], rest[nx:]
    step = pl.program_id(0)
    width = data_refs[0].shape[1]
    split = first_ref.shape[0]
    dims = (((1,), (1,)), ((), ()))
    upper, lower = None, None
    for x in range(nx):
        block = data_refs[x][...]
        one = lax.dot_general(
            first_ref[:, x * width : (x + 1) * width], block, dims, preferred_element_type=jnp.float32
        )
        two = lax.dot_general(second_ref[x, 0], block, dims, preferred_element_type=jnp.float32)
        upper = one if upper is None else upper + one
        lower = two if lower is None else lower + two

    @pl.when(step == 0)
    def _():
        total[:split] = upper
        total[split:] = lower

    @pl.when(step > 0)
    def _():
        total[:split] += upper
        total[split:] += lower

    @pl.when(step == steps - 1)
    def _():
        out_ref[...] = total[...] * scale


def inner_product(first, second, data, scale):
    nx, ny, low, width = second.shape
    high, cols = first.shape[0], data.shape[0]
    at = lambda x: pl.BlockSpec((cols, width), lambda y: (0, x * ny + y))
    return pl.pallas_call(
        functools.partial(inner_kernel, scale, nx, ny),
        grid=(ny,),
        out_shape=jax.ShapeDtypeStruct((high + low, cols), jnp.float32),
        in_specs=[
            pl.BlockSpec((high, nx * width), lambda y: (0, y)),
            pl.BlockSpec((nx, 1, low, width), lambda y: (0, y, 0, 0)),
        ]
        + [at(x) for x in range(nx)],
        out_specs=pl.BlockSpec((high + low, cols), lambda y: (0, 0)),
        scratch_shapes=[pltpu.VMEM((high + low, cols), jnp.float32)],
        compiler_params=PARAMS,
        name="inner_product",
    )(first, second, *([data] * nx))


def wide_cols_kernel(pot_ref, wide_ref, out_ref):
    pot = as_column(pot_ref[...])
    members = out_ref.shape[0]
    for k in range(wide_ref.shape[1] // LANES):
        scores = wide_ref[:, k * LANES : (k + 1) * LANES] + pot
        top = jnp.max(scores, axis=0, keepdims=True)
        local = top + jnp.log(jnp.sum(jnp.exp(scores - top), axis=0, keepdims=True))
        out_ref[:, k, :] = jnp.broadcast_to(local, (members, LANES))


def wide_cols(pot, wide, members):
    return pl.pallas_call(
        wide_cols_kernel,
        out_shape=jax.ShapeDtypeStruct((members, wide.shape[1] // LANES, LANES), jnp.float32),
        in_specs=[VMEM, VMEM],
        out_specs=VMEM,
        compiler_params=PARAMS,
        name="wide_cols",
    )(pot.reshape(1, -1), wide)


def row_top(wide_ref, pot):
    top = None
    for k in range(pot.shape[0]):
        scores = wide_ref[:, k * LANES : (k + 1) * LANES] + pot[k : k + 1]
        top = scores if top is None else jnp.maximum(top, scores)
    return jnp.max(top, axis=1, keepdims=True)


def wide_rows_kernel(log_cols, got_ref, wide_ref, out_ref):
    pot = -(log_cols + joined(got_ref))
    top = row_top(wide_ref, pot)
    total = None
    for k in range(pot.shape[0]):
        part = jnp.exp(wide_ref[:, k * LANES : (k + 1) * LANES] + pot[k : k + 1] - top)
        total = part if total is None else total + part
    local = as_rows(top + jnp.log(jnp.sum(total, axis=1, keepdims=True)))[:1]
    for k in range(out_ref.shape[1]):
        out_ref[:, k, :] = jnp.broadcast_to(local[:, k * LANES : (k + 1) * LANES], (out_ref.shape[0], LANES))


def wide_rows(got, wide, members, log_cols):
    return pl.pallas_call(
        functools.partial(wide_rows_kernel, log_cols),
        out_shape=jax.ShapeDtypeStruct((members, wide.shape[0] // LANES, LANES), jnp.float32),
        in_specs=[VMEM, VMEM],
        out_specs=VMEM,
        compiler_params=PARAMS,
        name="wide_rows",
    )(got, wide)


def rounded(values):
    return values.astype(jnp.bfloat16).astype(jnp.float32)


def final_kernel(log_cols, got_ref, wide_ref, data_ref, out_ref, pot_ref, weights):
    pot = -(log_cols + joined(got_ref))
    pot_ref[...] = pot
    ny, nx, cols, width = data_ref.shape
    rows = wide_ref.shape[0]
    top = row_top(wide_ref, pot)
    total = None
    for k in range(pot.shape[0]):
        lanes = slice(k * LANES, (k + 1) * LANES)
        part = jnp.exp(wide_ref[:, lanes] + pot[k : k + 1] - top)
        weights[:, lanes] = part.astype(jnp.bfloat16)
        total = part if total is None else total + part
    total = jnp.sum(total, axis=1, keepdims=True)
    inverse = 1.0 / total
    for x in range(nx):
        term = None
        for y in range(ny):
            one = jnp.dot(
                weights[:, y * cols : (y + 1) * cols], data_ref[y, x], preferred_element_type=jnp.float32
            )
            term = one if term is None else term + one
        out_ref[x, :rows, :] = (term * inverse).astype(jnp.bfloat16)
    local = as_rows(top + jnp.log(total))[:16]
    first = rounded(local)
    second = rounded(local - first)
    third = local - first - second
    place = lax.broadcasted_iota(jnp.int32, local.shape, 0)
    extra = jnp.where(place == 0, first, jnp.where(place == 1, second, third))
    extra = jnp.where(place < 3, extra, 0.0).astype(jnp.bfloat16)
    for x in range(nx):
        out_ref[x, rows:, :] = extra


def final_terms(got, wide, data, log_cols):
    ny, nx, cols, width = data.shape
    rows = wide.shape[0]
    return pl.pallas_call(
        functools.partial(final_kernel, log_cols),
        out_shape=(
            jax.ShapeDtypeStruct((nx, rows + 16, width), jnp.bfloat16),
            jax.ShapeDtypeStruct(got.shape[1:], jnp.float32),
        ),
        in_specs=[VMEM] * 3,
        out_specs=(VMEM, VMEM),
        scratch_shapes=[pltpu.VMEM(wide.shape, jnp.bfloat16)],
        compiler_params=PARAMS,
        name="final_terms",
    )(got, wide, data)


def combine_kernel(log_rows, features, got_ref, sq_ref, out_ref, pot_ref):
    nx, rows = got_ref.shape[0], out_ref.shape[0]
    locals_ = [
        jnp.sum(got_ref[x, rows:, :].astype(jnp.float32), axis=0, keepdims=True) for x in range(nx)
    ]
    top = functools.reduce(jnp.maximum, locals_)
    whole = top + jnp.log(functools.reduce(jnp.add, [jnp.exp(v - top) for v in locals_]))
    pot_ref[...] = sq_ref[...] * (1.0 / features) - EPSILON * (log_rows + whole)
    scales = [as_column(jnp.exp(v - whole)) for v in locals_]
    for k in range(out_ref.shape[1] // LANES):
        lanes = slice(k * LANES, (k + 1) * LANES)
        parts = [scales[x] * got_ref[x, :rows, lanes].astype(jnp.float32) for x in range(nx)]
        out_ref[:, lanes] = functools.reduce(jnp.add, parts).astype(jnp.bfloat16)


def combine(got, noise_sq, features, log_rows):
    nx, held, width = got.shape
    rows = held - 16
    return pl.pallas_call(
        functools.partial(combine_kernel, log_rows, features),
        out_shape=(
            jax.ShapeDtypeStruct((rows, width), jnp.bfloat16),
            jax.ShapeDtypeStruct((1, rows), jnp.float32),
        ),
        in_specs=[VMEM, VMEM],
        out_specs=(VMEM, VMEM),
        compiler_params=PARAMS,
        name="combine",
    )(got, noise_sq.reshape(1, -1))


def shards(noise, data):
    rows, width = noise.shape
    cols, features = data.shape
    nx, ny, nrow = lax.axis_size("x"), lax.axis_size("y"), lax.axis_size(ROW)
    log_rows = _log(rows * nrow)
    log_cols = _log(cols * nx * ny)

    part = lax.all_gather(noise[:FIRST_ROWS], "x", axis=1, tiled=True)
    first = lax.all_gather(part, "y", axis=1, tiled=True)
    low = rows - FIRST_ROWS
    share = cols // nrow
    piece = lax.dynamic_slice_in_dim(data, lax.axis_index(ROW) * share, share, 0)
    piece = piece.reshape(share, nx, ny, width).transpose(2, 1, 0, 3).reshape(ny, nx * share, width)
    sent = jnp.broadcast_to(noise[None, FIRST_ROWS:], (ny, low, width))
    sent = jnp.concatenate([sent, piece], axis=1)
    part, sent = lax.optimization_barrier((part, sent))
    got = lax.all_to_all(sent, "y", 0, 0)
    second = jnp.broadcast_to(got[None, :, :low], (nx, ny, low, width))
    second = lax.all_to_all(second, "x", 0, 0)
    piece = got[:, low:].reshape(ny, nx, share, width)

    noise_sq = jnp.sum(jnp.square(noise.astype(jnp.float32)), axis=1)
    data_sq = jnp.sum(jnp.square(data.astype(jnp.float32)), axis=1)

    scaled = inner_product(first, second, data, 2.0 / (features * EPSILON))
    wide = lax.all_gather(scaled, "y", axis=1, tiled=True)

    col_pot = data_sq * (-1.0 / (features * EPSILON))
    for step in range(ITERS - 1):
        local = lse(col_pot[None, :] + scaled, 1)
        if step == 0:
            got = spread(jnp.stack([local, noise_sq]), COL)
            noise_sq = jnp.sum(got[:, 1], axis=0)
            row_lse = lse(got[:, 0], 0)
            row_lse, piece = lax.optimization_barrier((row_lse, piece))
            mine = lax.all_gather(piece, ROW, axis=2, tiled=True)
        else:
            row_lse = lse(spread(local, COL), 0)
        row_pot = -(log_rows + row_lse)
        if step < ITERS - 2:
            local = lse(row_pot[:, None] + scaled, 0)
            col_pot = -(log_cols + lse(spread(local, ROW), 0))
    got = lax.all_to_all(wide_cols(row_pot, wide, nrow), ROW, 0, 0)
    got = lax.all_to_all(wide_rows(got, wide, nx, log_cols), "x", 0, 0)
    row_pot = -(log_rows + lse(got.reshape(nx, rows), 0))
    got = lax.all_to_all(wide_cols(row_pot, wide, nrow), ROW, 0, 0)
    terms, col_pot = final_terms(got, wide, mine, log_cols)
    own = lax.dynamic_slice_in_dim(col_pot, lax.axis_index("y") * (cols // LANES), cols // LANES, 0)
    data_potential = data_sq / features + EPSILON * own.reshape(cols)
    got = lax.all_to_all(terms, "x", 0, 0)
    targets, noise_potential = combine(got, noise_sq, features, log_rows)
    return (noise_potential.reshape(rows), data_potential, targets)


def _log(count):
    return float(np.log(np.float32(count)))


def solution(mesh):
    devices = mesh.devices.reshape(8, 2, 4, 8)
    return jax.shard_map(
        shards,
        mesh=Mesh(devices, ("z", "core", "x", "y")),
        in_specs=(P(ROW, COL), P(COL, None)),
        out_specs=(P(ROW), P(COL), P(ROW, COL)),
        check_vma=False,
    )
```

time: 322 us -> 232 us (0.72)
  waiting for transfers between devices: 158 us -> 27.5 us
  blocking collectives: 103 us -> 142 us
  Pallas kernels: 0 us -> 11.3 us
  matrix products: 10.7 us -> 0 us
  other arithmetic: 5.34 us -> 15.3 us
  starting transfers between devices: 12.6 us -> 9.16 us
    reduce_scatter x2 -> x0, waiting for transfers between devices: 83.7 us -> none  [the longest x1 43.7 us: shards(): part = lax.psum_scatter(term, 'x', scatter_dimension=1, tiled=True)]
    all_gather x1 -> x3, waiting for transfers between devices: 50.9 us -> 9.75 us  [the longest x1 9.73 us: shards(): first = lax.all_gather(part, 'y', axis=1, tiled=True)]
    all_to_all x7 -> x9, blocking collectives: 89.9 us -> 130 us  [the longest x4 57.5 us: spread(): return lax.all_to_all(sent, axes, 0, 0).reshape(members, *values.shape)]
    pallas_call x0 -> x6, Pallas kernels: none -> 11.3 us  [the longest x1 5.82 us: inner_product(): pl.pallas_call(functools.partial(inner_kernel, scale, nx, ny), grid=(ny,)...]
    dot_general x2 -> x0, matrix products: 10.7 us -> none  [the longest x1 5.49 us: shards(): jnp.dot(weights, data, preferred_element_type=jnp.float32)]
    all_to_all x3 -> x2, waiting for transfers between devices: 23.8 us -> 17.7 us  [the longest x1 9.64 us: shards(): got = lax.all_to_all(terms, 'x', 0, 0)]
    transpose x1, local copies, waits for them, and re-layouts: 4.74 us -> 0.15 us  [shards(): piece.reshape(share, nx, ny, width).transpose(2, 1, 0, 3)]
    reduce_max x17 -> x10, other arithmetic: 1.28 us -> 5.49 us  [lse(): top = jnp.max(scores, axis=axis, keepdims=True)]
  transfers between devices with their start and end apart: 6 -> 5, of which waited for: 6 -> 3; matrix products, arithmetic and copies ran while one was open for 4% -> 8% of each run, Pallas kernels for 0% -> 1%
where the time goes in v3:
time: 232 us; the launch traced here: 230 us
  blocking collectives  142 us (61%)
  waiting for transfers between devices  27.5 us (12%)
  other arithmetic  15.3 us (7%)
  between operations  14 us (6%)
  local copies, waits for them, and re-layouts  11.5 us (5%)
  Pallas kernels  11.3 us (5%)
  starting transfers between devices  9.16 us (4%)
    all_to_all x4, blocking collectives, spread(): return lax.all_to_all(sent, axes, 0, 0).reshape(members, *values.shape)  57.5 us
    all_to_all x2, blocking collectives, shards(): got = lax.all_to_all(wide_cols(row_pot, wide, nrow), ROW, 0, 0)  26.1 us
    all_to_all x1, blocking collectives, shards(): got = lax.all_to_all(sent, 'y', 0, 0)  23.6 us
    all_to_all x1, blocking collectives, shards(): second = lax.all_to_all(second, 'x', 0, 0)  16.7 us
    all_gather x1, blocking collectives, shards(): part = lax.all_gather(noise[:FIRST_ROWS], 'x', axis=1, tiled=True)  11.4 us
    all_gather x1, waiting for transfers between devices, shards(): first = lax.all_gather(part, 'y', axis=1, tiled=True)  9.73 us
    all_to_all x1, waiting for transfers between devices, shards(): got = lax.all_to_all(terms, 'x', 0, 0)  9.64 us
    all_to_all x1, waiting for transfers between devices, spread(): return lax.all_to_all(sent, axes, 0, 0).reshape(members, *values.shape)  8.09 us
  transfers between devices with their start and end apart: 5, of which 3 were waited for; matrix products, arithmetic and copies ran while one was open for 8% of the time, Pallas kernels for 1%

profile of v3, /device:TPU:1, one launch (start us, length us, event | category | flops | bytes accessed | tf_op | source)
XLA Modules:
  0.0 230.4 jit_solution(5675637564676276304)
XLA Ops:
  7.2 0.9 slice.18
  8.1 11.4 %all_gather.12 = bf16[160,1024]{1,0:T(8,128)(2,1)} all-gather(bf16[160,256]{1,0:T(8,128)(2,1)S(1)} %slice.18), channel_id=1, replica_groups=mesh['z'=8,'core'=2,'x'=4,'y'=8] {'x'}, dimensions={1}, use_global_device_ids=true | all-gather | bytes 409600 | tf_op jit(solution)/shard_map/all_gather | solution.py:243
  19.6 0.0 all-gather.6.cloned.1.call-start
  19.6 1.0 constant_dynamic-slice_fusion
  20.6 0.2 copy.21
  20.9 23.6 %all_to_all.55 = bf16[8,160,256]{2,1,0:T(8,128)(2,1)S(1)} all-to-all(bf16[8,160,256]{2,1,0:T(8,128)(2,1)S(1)} %pad_maximum_fusion), channel_id=1, replica_groups=mesh['z'=8,'core'=2,'x'=4,'y'=8] {'y'}, dimensions={0} | all-to-all | bytes 1310720 | tf_op jit(solution)/shard_map/all_to_all | solution.py:252
  44.5 0.2 broadcast_in_dim.17
  44.7 16.7 %all_to_all.56.second_ref = bf16[4,8,96,256]{3,2,1,0:T(8,128)(2,1)S(1)} all-to-all(bf16[4,8,96,256]{3,2,1,0:T(8,128)(2,1)S(1)} %broadcast_in_dim.17), channel_id=1, replica_groups=mesh['z'=8,'core'=2,'x'=4,'y'=8] {'x'}, dimensions={0} | all-to-all | bytes 3145728 | tf_op jit(solution)/shard_map/all_to_all | solution.py:254
  61.3 9.7 %all-gather.4.cloned.1.call-done.first_ref = bf16[160,8192]{1,0:T(8,128)(2,1)} async-done(((bf16[160,1024]{1,0:T(8,128)(2,1)}), bf16[160,8192]{1,0:T(8,128)(2,1)}) %all-gather.4.cloned.1.call-update) | async-done | bytes 2621456 | tf_op jit(solution)/shard_map/all_gather | solution.py:244
  71.1 2.2 copy-done
  73.2 1.7 copy-done.4
  75.0 5.8 %inner_product.1 = f32[256,256]{1,0:T(8,128)} custom-call(bf16[160,8192]{1,0:T(8,128)(2,1)S(1)} %copy-done.4, bf16[4,8,96,256]{3,2,1,0:T(8,128)(2,1)S(1)} %all_to_all.56.second_ref, bf16[256,8192]{1,0:T(8,128)(2,1)S(1)} %copy-done, bf16[256,8192]{1,0:T(8,128)(2,1)S(1)} %copy-done, bf16[256,8192]{1,0:T(8,128)(2,1)S(1)} %copy-done, bf16[256,8192]{1,0:T(8,128)(2,1)S(1)} %copy-done), custom_call_target="tpu_custom_call" | custom-call | tf_op jit(solution)/shard_map/inner_product/pallas_call | solution.py:83
  80.8 0.1 multiply_reduce_fusion.1
  81.0 3.1 %multiply_reduce_fusion = f32[256]{0:T(256)S(1)} fusion(bf16[256,8192]{1,0:T(8,128)(2,1)} %rest_3_.1), kind=kLoop, calls=%fused_computation | loop fusion | flops 6291200 | bytes 4195328 | tf_op jit(solution)/shard_map/reduce_sum | solution.py:258
  84.1 1.1 add_reduce_fusion.4
  85.1 1.1 exponential_reduce_fusion.4
  86.3 0.6 broadcast_in_dim.19
  87.0 5.6 %all-to-all-start.2 = ((f32[32,4,128]{2,1,0:T(4,128)}), f32[32,4,128]{2,1,0:T(4,128)S(1)}, u32[]{:S(2)}, u32[]{:S(2)}) async-start(f32[32,4,128]{2,1,0:T(4,128)} %broadcast_in_dim.19), calls=%async_computation.2 | async-start | bytes 131072 | tf_op jit(solution)/shard_map/all_to_all | solution.py:25
  92.5 0.0 all-gather.8.cloned.1.call-start
  92.6 0.7 slice.26
  93.3 8.1 %all-to-all-done.2 = f32[32,4,128]{2,1,0:T(4,128)S(1)} async-done(((f32[32,4,128]{2,1,0:T(4,128)}), f32[32,4,128]{2,1,0:T(4,128)S(1)}, u32[]{:S(2)}, u32[]{:S(2)}) %all-to-all-start.2) | async-done | bytes 65568 | tf_op jit(solution)/shard_map/all_to_all | solution.py:25
  101.4 0.1 reshape.326
  101.5 0.1 slice_reduce_fusion
  101.6 1.1 add_reduce_fusion.3
  102.7 1.1 exponential_reduce_fusion.3
  103.8 22.4 %all_to_all.57 = f32[16,2,128]{2,1,0:T(2,128)S(1)} all-to-all(f32[16,2,128]{2,1,0:T(2,128)S(1)} %broadcast_in_dim.20), channel_id=1, replica_groups=mesh['z'=8,'core'=2,'x'=4,'y'=8] {'z','core'}, dimensions={0} | all-to-all | bytes 32768 | tf_op jit(solution)/shard_map/all_to_all | solution.py:25
  126.3 1.1 add_reduce_fusion.2
  127.4 1.1 exponential_reduce_fusion.2
  128.6 11.8 %all_to_all.58 = f32[32,2,128]{2,1,0:T(2,128)S(1)} all-to-all(f32[32,2,128]{2,1,0:T(2,128)S(1)} %broadcast_in_dim.21), channel_id=1, replica_groups=mesh['z'=8,'core'=2,'x'=4,'y'=8] {'x','y'}, dimensions={0} | all-to-all | bytes 65536 | tf_op jit(solution)/shard_map/all_to_all | solution.py:25
  140.5 1.1 add_reduce_fusion.1
  141.6 1.1 exponential_reduce_fusion.1
  142.7 11.6 %all_to_all.59 = f32[16,2,128]{2,1,0:T(2,128)S(1)} all-to-all(f32[16,2,128]{2,1,0:T(2,128)S(1)} %broadcast_in_dim.22), channel_id=1, replica_groups=mesh['z'=8,'core'=2,'x'=4,'y'=8] {'z','core'}, dimensions={0} | all-to-all | bytes 32768 | tf_op jit(solution)/shard_map/all_to_all | solution.py:25
  154.3 1.1 add_reduce_fusion
  155.4 1.1 exponential_reduce_fusion
  156.5 11.7 %all_to_all.60 = f32[32,2,128]{2,1,0:T(2,128)S(1)} all-to-all(f32[32,2,128]{2,1,0:T(2,128)S(1)} %broadcast_in_dim.23), channel_id=1, replica_groups=mesh['z'=8,'core'=2,'x'=4,'y'=8] {'x','y'}, dimensions={0} | all-to-all | bytes 65536 | tf_op jit(solution)/shard_map/all_to_all | solution.py:25
  168.3 1.6 copy-done.1
  169.9 0.7 wide_cols.2
  170.6 13.3 %all_to_all.61.got_ref = f32[16,16,128]{2,1,0:T(8,128)S(1)} all-to-all(f32[16,16,128]{2,1,0:T(8,128)S(1)} %wide_cols.2), channel_id=1, replica_groups=mesh['z'=8,'core'=2,'x'=4,'y'=8] {'z','core'}, dimensions={0} | all-to-all | bytes 262144 | tf_op jit(solution)/shard_map/all_to_all | solution.py:278
  183.9 0.6 wide_rows.1
  184.5 6.5 %all_to_all.62 = f32[4,2,128]{2,1,0:T(2,128)S(1)} all-to-all(f32[4,2,128]{2,1,0:T(2,128)S(1)} %wide_rows.1), channel_id=1, replica_groups=mesh['z'=8,'core'=2,'x'=4,'y'=8] {'x'}, dimensions={0} | all-to-all | bytes 8192 | tf_op jit(solution)/shard_map/all_to_all | solution.py:279
  191.1 0.7 wide_cols.3
  191.8 12.7 %all_to_all.63.got_ref = f32[16,16,128]{2,1,0:T(8,128)S(1)} all-to-all(f32[16,16,128]{2,1,0:T(8,128)S(1)} %wide_cols.3), channel_id=1, replica_groups=mesh['z'=8,'core'=2,'x'=4,'y'=8] {'z','core'}, dimensions={0} | all-to-all | bytes 262144 | tf_op jit(solution)/shard_map/all_to_all | solution.py:281
  204.5 2.2 copy-done.3
  206.7 2.6 %final_terms.1 = (bf16[4,272,256]{2,1,0:T(8,128)(2,1)}, f32[16,128]{1,0:T(8,128)S(1)}) custom-call(f32[16,16,128]{2,1,0:T(8,128)S(1)} %all_to_all.63.got_ref, f32[256,2048]{1,0:T(8,128)S(1)} %copy-done.2, bf16[8,4,256,256]{3,2,1,0:T(8,128)(2,1)S(1)} %copy-done.3), custom_call_target="tpu_custom_call" | custom-call | tf_op jit(solution)/shard_map/final_terms/pallas_call | solution.py:191
  209.3 3.5 %all-to-all-start.10 = ((bf16[4,272,256]{2,1,0:T(8,128)(2,1)}), bf16[4,272,256]{2,1,0:T(8,128)(2,1)S(1)}, u32[]{:S(2)}, u32[]{:S(2)}) async-start(bf16[4,272,256]{2,1,0:T(8,128)(2,1)} %get-tuple-element.13), calls=%async_computation.10 | async-start | bytes 1114112 | tf_op jit(solution)/shard_map/all_to_all | solution.py:285
  212.7 0.6 bitcast_add_fusion
  213.3 9.6 %all-to-all-done.10.got_ref = bf16[4,272,256]{2,1,0:T(8,128)(2,1)S(1)} async-done(((bf16[4,272,256]{2,1,0:T(8,128)(2,1)}), bf16[4,272,256]{2,1,0:T(8,128)(2,1)S(1)}, u32[]{:S(2)}, u32[]{:S(2)}) %all-to-all-start.10) | async-done | bytes 557088 | tf_op jit(solution)/shard_map/all_to_all | solution.py:285
  223.0 0.9 combine.1
  (50 shorter events, 0.8 us)
Async XLA Ops:
  7.2 13.6 %slice-start = ((bf16[256,256]{1,0:T(8,128)(2,1)}), bf16[96,256]{1,0:T(8,128)(2,1)S(1)}, s32[]{:S(2)}) async-start(bf16[256,256]{1,0:T(8,128)(2,1)} %param.2), calls=%async_computation.14 | async-start | bytes 98304 | tf_op jit(solution)/shard_map/slice | solution.py:249
  7.2 63.9 %all-gather.4.cloned.1.call-start = ((), (), s32[]{:S(2)}) async-start(), calls=%async_computation.11 | async-start | bytes 2949120 | tf_op jit(solution)/shard_map/all_gather | solution.py:244
  19.6 148.8 %all-gather.6.cloned.1.call-start = ((), (), s32[]{:S(2)}) async-start(), calls=%async_computation.12 | async-start | bytes 2359296 | tf_op jit(solution)/shard_map/all_gather | solution.py:261
  71.0 2.2 copy-start
  73.2 1.7 copy-start.4
  75.0 5.8 %copy-start.5 = (bf16[256,256]{1,0:T(8,128)(2,1)S(1)}, bf16[256,256]{1,0:T(8,128)(2,1)}, u32[]{:S(2)}) copy-start(bf16[256,256]{1,0:T(8,128)(2,1)} %param.2) | copy-start | bytes 393220
  87.0 14.4 %all-to-all-start.2 = ((f32[32,4,128]{2,1,0:T(4,128)}), f32[32,4,128]{2,1,0:T(4,128)S(1)}, u32[]{:S(2)}, u32[]{:S(2)}) async-start(f32[32,4,128]{2,1,0:T(4,128)} %broadcast_in_dim.19), calls=%async_computation.2 | async-start | bytes 131072 | tf_op jit(solution)/shard_map/all_to_all | solution.py:25
  92.5 112.0 %all-gather.8.cloned.1.call-start = ((), (), s32[]{:S(2)}) async-start(), calls=%async_computation.13 | async-start | bytes 4456448 | tf_op jit(solution)/shard_map/all_gather | solution.py:271
  168.3 1.6 copy-start.1
  169.9 21.1 %copy-start.2 = (f32[256,2048]{1,0:T(8,128)S(1)}, f32[256,2048]{1,0:T(8,128)}, u32[]{:S(2)}) copy-start(f32[256,2048]{1,0:T(8,128)} %all-gather.6.cloned.1.call-done.wide_ref) | copy-start | bytes 6291460
  204.5 2.2 copy-start.3
  209.3 13.7 %all-to-all-start.10 = ((bf16[4,272,256]{2,1,0:T(8,128)(2,1)}), bf16[4,272,256]{2,1,0:T(8,128)(2,1)S(1)}, u32[]{:S(2)}, u32[]{:S(2)}) async-start(bf16[4,272,256]{2,1,0:T(8,128)(2,1)} %get-tuple-element.13), calls=%async_computation.10 | async-start | bytes 1114112 | tf_op jit(solution)/shard_map/all_to_all | solution.py:285
Sparse Core Ops, SparseCore 0:
  19.7 51.3 all-gather.3
  80.9 42.9 all-gather.5
  126.1 48.7 all-gather.7

commit v4 on v1

v4 whole, which is shorter than its diff:
```python
import functools

import jax
import jax.numpy as jnp
import numpy as np
from jax import lax
from jax.experimental import pallas as pl
from jax.experimental.pallas import tpu as pltpu
from jax.sharding import Mesh, PartitionSpec as P

ITERS = 4
EPSILON = 0.01
ROW = ("z", "core")
COL = ("x", "y")
LANES = 128
FIRST_ROWS = 160
WIDE_FROM = 1
VMEM = pl.BlockSpec(memory_space=pltpu.VMEM)
HBM = pl.BlockSpec(memory_space=pltpu.HBM)
MIB = 2**20
F32, BF16 = jnp.float32, jnp.bfloat16


def call(kernel, name, out_shape, in_specs, out_specs, *args, scratch_shapes=(), vmem=40):
    return pl.pallas_call(
        kernel,
        out_shape=out_shape,
        in_specs=in_specs,
        out_specs=out_specs,
        scratch_shapes=scratch_shapes,
        compiler_params=pltpu.CompilerParams(vmem_limit_bytes=vmem * MIB),
        name=name,
    )(*args)


def shape(dims, dtype=F32):
    return jax.ShapeDtypeStruct(dims, dtype)


def lanes(k):
    return slice(k * LANES, (k + 1) * LANES)


def as_column(values):
    return jnp.broadcast_to(values, (LANES, values.shape[1])).T


def as_rows(column):
    return jnp.broadcast_to(column, (column.shape[0], LANES)).T


def joined(got):
    top = jnp.max(got, axis=0)
    return top + jnp.log(jnp.sum(jnp.exp(got - top[None]), axis=0))


def products(read, data_ref, nx, ny, width):
    total = None
    for y in range(ny):
        left = jnp.concatenate([read(y, x) for x in range(nx)], axis=1)
        right = jnp.concatenate(
            [data_ref[:, (x * ny + y) * width : (x * ny + y + 1) * width] for x in range(nx)], axis=1
        )
        one = lax.dot_general(left, right, (((1,), (1,)), ((), ())), preferred_element_type=F32)
        total = one if total is None else total + one
    return total


def second_kernel(scale, second_ref, data_ref, out_ref):
    nx, ny, _, width = second_ref.shape
    out_ref[...] = products(lambda y, x: second_ref[x, y], data_ref, nx, ny, width) * scale


def first_kernel(scale, first_ref, data_ref, low_ref, pot_ref, sq_ref, out_ref, copy_ref, send_ref, held, sems):
    ny, nx, high, width = first_ref.shape
    copies = [pltpu.make_async_copy(first_ref.at[y], held.at[y], sems.at[y]) for y in range(ny)]
    for copy in copies:
        copy.start()

    def read(y, x):
        if x == 0:
            copies[y].wait()
        return held[y, x]

    out_ref[:high] = products(read, data_ref, nx, ny, width) * scale
    out_ref[high:] = low_ref[...]
    out = pltpu.make_async_copy(out_ref, copy_ref, sems.at[ny])
    out.start()
    local = local_rows(out_ref, pot_ref[...])
    chunks = local.shape[1] // LANES
    members = send_ref.shape[0]
    for k in range(chunks):
        send_ref[:, k, :] = jnp.broadcast_to(local[:, lanes(k)], (members, LANES))
        send_ref[:, chunks + k, :] = jnp.broadcast_to(sq_ref[k : k + 1], (members, LANES))
    out.wait()


def row_top(block_ref, pot):
    top = None
    for k in range(pot.shape[0]):
        scores = block_ref[:, lanes(k)] + pot[k : k + 1]
        top = scores if top is None else jnp.maximum(top, scores)
    return jnp.max(top, axis=1, keepdims=True)


def local_rows(block_ref, pot):
    top = row_top(block_ref, pot)
    total = None
    for k in range(pot.shape[0]):
        part = jnp.exp(block_ref[:, lanes(k)] + pot[k : k + 1] - top)
        total = part if total is None else total + part
    return as_rows(top + jnp.log(jnp.sum(total, axis=1, keepdims=True)))[:1]


def rows_kernel(log_cols, got_ref, block_ref, out_ref):
    local = local_rows(block_ref, -(log_cols + joined(got_ref[...])))
    for k in range(out_ref.shape[1]):
        out_ref[:, k, :] = jnp.broadcast_to(local[:, lanes(k)], (out_ref.shape[0], LANES))


def half_rows(got, block, members, log_cols):
    out = shape((members, block.shape[0] // LANES, LANES))
    return call(functools.partial(rows_kernel, log_cols), "half_rows", out, [VMEM, VMEM], VMEM, got, block)


def cols_kernel(log_rows, got_ref, block_ref, out_ref):
    chunks = block_ref.shape[0] // LANES
    pot = -(log_rows + joined(got_ref[:, :chunks, :]))
    pot = jnp.concatenate([as_column(pot[k : k + 1]) for k in range(chunks)], axis=0)
    members = out_ref.shape[0]
    for k in range(out_ref.shape[1]):
        scores = block_ref[:, lanes(k)] + pot
        top = jnp.max(scores, axis=0, keepdims=True)
        local = top + jnp.log(jnp.sum(jnp.exp(scores - top), axis=0, keepdims=True))
        out_ref[:, k, :] = jnp.broadcast_to(local, (members, LANES))


def half_cols(got, block, members, log_rows):
    out = shape((members, block.shape[1] // LANES, LANES))
    return call(functools.partial(cols_kernel, log_rows), "half_cols", out, [VMEM, VMEM], VMEM, got, block)


def rounded(values):
    return values.astype(BF16).astype(F32)


def final_kernel(log_cols, got_ref, wide_ref, data_ref, out_ref, pot_ref, weights, held, sems):
    ny, nx, cols, width = data_ref.shape
    rows = wide_ref.shape[0]
    copies = [pltpu.make_async_copy(data_ref.at[y], held.at[y], sems.at[y]) for y in range(ny)]
    for copy in copies:
        copy.start()
    pot = -(log_cols + joined(got_ref[...]))
    pot_ref[...] = pot
    top = row_top(wide_ref, pot)
    total = None
    for k in range(pot.shape[0]):
        part = jnp.exp(wide_ref[:, lanes(k)] + pot[k : k + 1] - top)
        weights[:, lanes(k)] = part.astype(BF16)
        total = part if total is None else total + part
    total = jnp.sum(total, axis=1, keepdims=True)
    inverse = 1.0 / total
    local = as_rows(top + jnp.log(total))[:16]
    first = rounded(local)
    second = rounded(local - first)
    third = local - first - second
    place = lax.broadcasted_iota(jnp.int32, local.shape, 0)
    extra = jnp.where(place == 0, first, jnp.where(place == 1, second, third))
    extra = jnp.where(place < 3, extra, 0.0).astype(BF16)
    for copy in copies:
        copy.wait()
    for x in range(nx):
        right = jnp.concatenate([held[y, x] for y in range(ny)], axis=0)
        term = jnp.dot(weights[...], right, preferred_element_type=F32)
        out_ref[x, :rows, :] = (term * inverse).astype(BF16)
        out_ref[x, rows:, :] = extra


def final_terms(got, wide, data, log_cols):
    ny, nx, cols, width = data.shape
    rows = wide.shape[0]
    return call(
        functools.partial(final_kernel, log_cols),
        "final_terms",
        (shape((nx, rows + 16, width), BF16), shape(got.shape[1:])),
        [VMEM, VMEM, HBM],
        (VMEM, VMEM),
        got,
        wide,
        data,
        scratch_shapes=[
            pltpu.VMEM(wide.shape, BF16),
            pltpu.VMEM(data.shape, BF16),
            pltpu.SemaphoreType.DMA((ny,)),
        ],
        vmem=52,
    )


def combine_kernel(log_rows, features, got_ref, began_ref, out_ref, pot_ref):
    nx, rows = got_ref.shape[0], out_ref.shape[0]
    chunks = rows // LANES
    locals_ = [jnp.sum(got_ref[x, rows:, :].astype(F32), axis=0, keepdims=True) for x in range(nx)]
    top = functools.reduce(jnp.maximum, locals_)
    whole = top + jnp.log(functools.reduce(jnp.add, [jnp.exp(v - top) for v in locals_]))
    noise_sq = jnp.sum(began_ref[:, chunks:, :], axis=0)
    for k in range(chunks):
        pot_ref[k : k + 1, :] = noise_sq[k : k + 1] * (1.0 / features) - EPSILON * (log_rows + whole[:, lanes(k)])
    scales = [as_column(jnp.exp(v - whole)) for v in locals_]
    for k in range(out_ref.shape[1] // LANES):
        parts = [scales[x] * got_ref[x, :rows, lanes(k)].astype(F32) for x in range(nx)]
        out_ref[:, lanes(k)] = functools.reduce(jnp.add, parts).astype(BF16)


def shards(noise, data):
    rows, width = noise.shape
    cols, features = data.shape
    nx, ny, nrow, ncol = (lax.axis_size(axes) for axes in ("x", "y", ROW, COL))
    log_rows, log_cols = _log(rows * nrow), _log(cols * ncol)
    chunks = rows // LANES

    sent = jnp.broadcast_to(noise[None, :FIRST_ROWS], (nx, FIRST_ROWS, width))
    part = lax.all_to_all(sent, "x", 0, 0)
    first = lax.all_gather(part, "y")
    low = rows - FIRST_ROWS
    share = cols // nrow
    piece = lax.dynamic_slice_in_dim(data, lax.axis_index(ROW) * share, share, 0)
    piece = piece.reshape(share, nx, ny, width).transpose(2, 1, 0, 3).reshape(ny, nx * share, width)
    sent = jnp.broadcast_to(noise[None, FIRST_ROWS:], (ny, low, width))
    sent = jnp.concatenate([sent, piece], axis=1)
    part, sent = lax.optimization_barrier((part, sent))
    got = lax.all_to_all(sent, "y", 0, 0)
    second = jnp.broadcast_to(got[None, :, :low], (nx, ny, low, width))
    second = lax.all_to_all(second, "x", 0, 0)
    piece = got[:, low:].reshape(ny, nx, share, width)

    noise_sq = jnp.sum(jnp.square(noise.astype(F32)), axis=1)
    data_sq = jnp.sum(jnp.square(data.astype(F32)), axis=1)
    col_pot = (data_sq * (-1.0 / (features * EPSILON))).reshape(-1, LANES)
    scale = 2.0 / (features * EPSILON)
    lower = call(
        functools.partial(second_kernel, scale), "second_rows", shape((low, cols)), [VMEM, VMEM], VMEM, second, data
    )
    scaled, copied, sent = call(
        functools.partial(first_kernel, scale),
        "first_rows",
        (shape((rows, cols)), shape((rows, cols)), shape((ncol, 2 * chunks, LANES))),
        [HBM, VMEM, VMEM, VMEM, VMEM],
        (VMEM, HBM, VMEM),
        first,
        data,
        lower,
        col_pot,
        noise_sq.reshape(-1, LANES),
        scratch_shapes=[
            pltpu.VMEM((ny, nx, FIRST_ROWS, width), BF16),
            pltpu.SemaphoreType.DMA((ny + 1,)),
        ],
        vmem=52,
    )
    wide = lax.all_gather(copied, "y", axis=1, tiled=True)

    began = None
    for step in range(ITERS):
        got = lax.all_to_all(sent, "x" if step > WIDE_FROM else COL, 0, 0)
        if step == 0:
            began, piece = lax.optimization_barrier((got, piece))
            mine = lax.all_gather(piece, ROW, axis=2, tiled=True)
        sent = half_cols(got, wide if step >= WIDE_FROM else scaled, nrow, log_rows)
        got = lax.all_to_all(sent, ROW, 0, 0)
        if step < WIDE_FROM:
            sent = half_rows(got, scaled, ncol, log_cols)
        elif step < ITERS - 1:
            sent = half_rows(got, wide, nx, log_cols)
    terms, col_pot = final_terms(got, wide, mine, log_cols)
    own = lax.dynamic_slice_in_dim(col_pot, lax.axis_index("y") * (cols // LANES), cols // LANES, 0)
    data_potential = data_sq / features + EPSILON * own.reshape(cols)
    got = lax.all_to_all(terms, "x", 0, 0)
    targets, noise_potential = call(
        functools.partial(combine_kernel, log_rows, features),
        "combine",
        (shape((rows, width), BF16), shape((chunks, LANES))),
        [VMEM, VMEM],
        (VMEM, VMEM),
        got,
        began,
    )
    return (noise_potential.reshape(rows), data_potential, targets)


def _log(count):
    return float(np.log(np.float32(count)))


def solution(mesh):
    devices = mesh.devices.reshape(8, 2, 4, 8)
    return jax.shard_map(
        shards,
        mesh=Mesh(devices, ("z", "core", "x", "y")),
        in_specs=(P(ROW, COL), P(COL, None)),
        out_specs=(P(ROW), P(COL), P(ROW, COL)),
        check_vma=False,
    )
```

time: 322 us -> 219 us (0.68); the launches traced: 317 us -> 218 us
  waiting for transfers between devices: 158 us -> 30.4 us
  blocking collectives: 103 us -> 130 us
  Pallas kernels: 0 us -> 19.5 us
  matrix products: 10.7 us -> 0 us
  local copies, waits for them, and re-layouts: 13 us -> 8.07 us
    reduce_scatter x2 -> x0, waiting for transfers between devices: 83.7 us -> none  [the longest x1 43.7 us: shards(): part = lax.psum_scatter(term, 'x', scatter_dimension=1, tiled=True)]
    all_gather x1 -> x3, waiting for transfers between devices: 50.9 us -> 2.15 us  [the longest x1 2.15 us: shards(): first = lax.all_gather(part, 'y')]
    all_to_all x7 -> x9, blocking collectives: 89.9 us -> 130 us  [the longest x4 67.7 us: shards(): got = lax.all_to_all(sent, ROW, 0, 0)]
    pallas_call x0 -> x11, Pallas kernels: none -> 19.5 us  [call(): pl.pallas_call(kernel, out_shape=out_shape, in_specs=in_specs, out_specs=...]
    all_gather x1 -> x0, blocking collectives: 13.3 us -> none  [shards(): part = lax.all_gather(noise, 'x', axis=1, tiled=True)]
    dot_general x2 -> x0, matrix products: 10.7 us -> none  [the longest x1 5.49 us: shards(): jnp.dot(weights, data, preferred_element_type=jnp.float32)]
    transpose x1, local copies, waits for them, and re-layouts: 4.74 us -> 0.15 us  [shards(): piece.reshape(share, nx, ny, width).transpose(2, 1, 0, 3)]
    all_to_all x3, waiting for transfers between devices: 23.8 us -> 28.2 us  [the longest x1 10.5 us: shards(): second = lax.all_to_all(second, 'x', 0, 0)]
  transfers between devices with their start and end apart: 6 -> 6, of which waited for: 6 -> 4; matrix products, arithmetic and copies ran while one was open for 4% -> 3% of each run, Pallas kernels for 0% -> 2%
where the time goes in v4:
time: 219 us; the launch traced here: 218 us
  blocking collectives  130 us (59%)
  waiting for transfers between devices  30.4 us (14%)
  Pallas kernels  19.5 us (9%)
  between operations  13.9 us (6%)
  starting transfers between devices  12.6 us (6%)
  local copies, waits for them, and re-layouts  8.07 us (4%)
  other arithmetic  3.87 us (2%)
    all_to_all x4, blocking collectives, shards(): got = lax.all_to_all(sent, ROW, 0, 0)  67.7 us
    all_to_all x3, blocking collectives, shards(): got = lax.all_to_all(sent, 'x' if step > WIDE_FROM else COL, 0, 0)  26.4 us
    all_to_all x1, blocking collectives, shards(): got = lax.all_to_all(sent, 'y', 0, 0)  24.9 us
    pallas_call x11, Pallas kernels, call(): pl.pallas_call(kernel, out_shape=out_shape, in_specs=in_specs, out_specs=...  19.5 us
    all_to_all x1, blocking collectives, shards(): part = lax.all_to_all(sent, 'x', 0, 0)  10.6 us
    all_to_all x1, waiting for transfers between devices, shards(): second = lax.all_to_all(second, 'x', 0, 0)  10.5 us
    all_to_all x1, waiting for transfers between devices, shards(): got = lax.all_to_all(terms, 'x', 0, 0)  9.61 us
    all_to_all x1, waiting for transfers between devices, shards(): got = lax.all_to_all(sent, 'x' if step > WIDE_FROM else COL, 0, 0)  8.08 us
  transfers between devices with their start and end apart: 6, of which 4 were waited for; matrix products, arithmetic and copies ran while one was open for 3% of the time, Pallas kernels for 2%

profile of v4, /device:TPU:1, one launch (start us, length us, event | category | flops | bytes accessed | tf_op | source)
XLA Modules:
  0.0 218.1 jit_solution(13428203562382955098)
XLA Ops:
  7.2 0.0 slice-start
  7.2 0.0 all-gather.9.cloned.1.call-start
  7.2 0.9 slice.12
  8.1 10.6 %all_to_all.60 = bf16[4,160,256]{2,1,0:T(8,128)(2,1)} all-to-all(bf16[4,160,256]{2,1,0:T(8,128)(2,1)S(1)} %broadcast_in_dim.6), channel_id=1, replica_groups=mesh['z'=8,'core'=2,'x'=4,'y'=8] {'x'}, dimensions={0} | all-to-all | bytes 655360 | tf_op jit(solution)/shard_map/all_to_all | solution.py:223
  18.8 0.0 all-gather.9.cloned.1.call-update
  18.8 1.0 constant_dynamic-slice_fusion
  19.8 0.2 copy.6
  20.0 0.0 slice-done
  20.1 24.9 %all_to_all.61 = bf16[8,160,256]{2,1,0:T(8,128)(2,1)S(1)} all-to-all(bf16[8,160,256]{2,1,0:T(8,128)(2,1)S(1)} %pad_maximum_fusion), channel_id=1, replica_groups=mesh['z'=8,'core'=2,'x'=4,'y'=8] {'y'}, dimensions={0} | all-to-all | bytes 1310720 | tf_op jit(solution)/shard_map/all_to_all | solution.py:232
  45.1 0.0 copy-start.3
  45.1 1.3 broadcast_in_dim.8
  46.4 3.6 %all-to-all-start.2 = ((bf16[4,8,96,256]{3,2,1,0:T(8,128)(2,1)}), bf16[4,8,96,256]{3,2,1,0:T(8,128)(2,1)S(1)}, u32[]{:S(2)}, u32[]{:S(2)}) async-start(bf16[4,8,96,256]{3,2,1,0:T(8,128)(2,1)} %broadcast_in_dim.8), calls=%async_computation.2 | async-start | bytes 3145728 | tf_op jit(solution)/shard_map/all_to_all | solution.py:234
  50.0 0.0 all-gather.5.cloned.1.call-start
  50.0 0.0 copy-done.3
  50.0 0.1 multiply_reduce_fusion.1
  50.2 3.1 %multiply_reduce_fusion = f32[256]{0:T(256)S(1)} fusion(bf16[256,8192]{1,0:T(8,128)(2,1)} %data_ref.3), kind=kLoop, calls=%fused_computation | loop fusion | flops 6291200 | bytes 4195328 | tf_op jit(solution)/shard_map/reduce_sum | solution.py:238
  53.3 10.5 %all-to-all-done.2.second_ref = bf16[4,8,96,256]{3,2,1,0:T(8,128)(2,1)S(1)} async-done(((bf16[4,8,96,256]{3,2,1,0:T(8,128)(2,1)}), bf16[4,8,96,256]{3,2,1,0:T(8,128)(2,1)S(1)}, u32[]{:S(2)}, u32[]{:S(2)}) %all-to-all-start.2) | async-done | bytes 1572896 | tf_op jit(solution)/shard_map/all_to_all | solution.py:234
  63.8 2.2 %copy-done.2 = bf16[256,8192]{1,0:T(8,128)(2,1)S(1)} copy-done((bf16[256,8192]{1,0:T(8,128)(2,1)S(1)}, bf16[256,8192]{1,0:T(8,128)(2,1)}, u32[]{:S(2)}) %copy-start.2) | copy-done | bytes 4194328
  66.1 1.4 second_rows.1.low_ref
  67.5 2.1 all-gather.9.cloned.1.call-done
  69.6 7.4 %first_rows.1 = (f32[256,256]{1,0:T(8,128)S(1)}, f32[256,256]{1,0:T(8,128)}, f32[32,4,128]{2,1,0:T(4,128)}) custom-call(bf16[8,4,160,256]{3,2,1,0:T(8,128)(2,1)} %bitcast.15, bf16[256,8192]{1,0:T(8,128)(2,1)} %data_ref.3, f32[96,256]{1,0:T(8,128)S(1)} %second_rows.1.low_ref, f32[2,128]{1,0:T(2,128)S(1)} %multiply_bitcast_fusion.pot_ref, f32[2,128]{1,0:T(2,128)S(1)} %bitcast.14), custom_call_target="tpu_custom_call" | custom-call | tf_op jit(solution)/shard_map/first_rows/pallas_call | solution.py:25
  77.1 0.0 all-gather.5.cloned.1.call-update
  77.1 5.4 %all-to-all-start.3 = ((f32[32,4,128]{2,1,0:T(4,128)}), f32[32,4,128]{2,1,0:T(4,128)S(1)}, u32[]{:S(2)}, u32[]{:S(2)}) async-start(f32[32,4,128]{2,1,0:T(4,128)} %get-tuple-element.14), calls=%async_computation.3 | async-start | bytes 131072 | tf_op jit(solution)/shard_map/all_to_all | solution.py:265
  82.5 0.0 all-gather.7.cloned.1.call-start
  82.6 0.7 slice.17
  83.3 8.1 %all-to-all-done.3.got_ref.began_ref = f32[32,4,128]{2,1,0:T(4,128)S(1)} async-done(((f32[32,4,128]{2,1,0:T(4,128)}), f32[32,4,128]{2,1,0:T(4,128)S(1)}, u32[]{:S(2)}, u32[]{:S(2)}) %all-to-all-start.3) | async-done | bytes 65568 | tf_op jit(solution)/shard_map/all_to_all | solution.py:265
  91.4 0.0 all-gather.7.cloned.1.call-update
  91.4 0.2 half_cols.4
  91.7 25.7 %all_to_all.62.got_ref = f32[16,2,128]{2,1,0:T(2,128)S(1)} all-to-all(f32[16,2,128]{2,1,0:T(2,128)S(1)} %half_cols.4), channel_id=1, replica_groups=mesh['z'=8,'core'=2,'x'=4,'y'=8] {'z','core'}, dimensions={0} | all-to-all | bytes 32768 | tf_op jit(solution)/shard_map/all_to_all | solution.py:270
  117.4 0.3 half_rows.3
  117.7 11.9 %all_to_all.63.got_ref = f32[32,2,128]{2,1,0:T(2,128)S(1)} all-to-all(f32[32,2,128]{2,1,0:T(2,128)S(1)} %half_rows.3), channel_id=1, replica_groups=mesh['z'=8,'core'=2,'x'=4,'y'=8] {'x','y'}, dimensions={0} | all-to-all | bytes 65536 | tf_op jit(solution)/shard_map/all_to_all | solution.py:265
  129.5 1.6 copy-done
  131.1 0.7 half_cols.5
  131.9 14.5 %all_to_all.64.got_ref = f32[16,16,128]{2,1,0:T(8,128)S(1)} all-to-all(f32[16,16,128]{2,1,0:T(8,128)S(1)} %half_cols.5), channel_id=1, replica_groups=mesh['z'=8,'core'=2,'x'=4,'y'=8] {'z','core'}, dimensions={0} | all-to-all | bytes 262144 | tf_op jit(solution)/shard_map/all_to_all | solution.py:270
  146.4 0.0 copy-done.1
  146.4 0.6 half_rows.4
  147.0 8.1 %all_to_all.65.got_ref = f32[4,2,128]{2,1,0:T(2,128)S(1)} all-to-all(f32[4,2,128]{2,1,0:T(2,128)S(1)} %half_rows.4), channel_id=1, replica_groups=mesh['z'=8,'core'=2,'x'=4,'y'=8] {'x'}, dimensions={0} | all-to-all | bytes 8192 | tf_op jit(solution)/shard_map/all_to_all | solution.py:265
  155.0 0.7 half_cols.6
  155.7 14.3 %all_to_all.66.got_ref = f32[16,16,128]{2,1,0:T(8,128)S(1)} all-to-all(f32[16,16,128]{2,1,0:T(8,128)S(1)} %half_cols.6), channel_id=1, replica_groups=mesh['z'=8,'core'=2,'x'=4,'y'=8] {'z','core'}, dimensions={0} | all-to-all | bytes 262144 | tf_op jit(solution)/shard_map/all_to_all | solution.py:270
  170.1 0.6 half_rows.5
  170.7 6.5 %all_to_all.67.got_ref = f32[4,2,128]{2,1,0:T(2,128)S(1)} all-to-all(f32[4,2,128]{2,1,0:T(2,128)S(1)} %half_rows.5), channel_id=1, replica_groups=mesh['z'=8,'core'=2,'x'=4,'y'=8] {'x'}, dimensions={0} | all-to-all | bytes 8192 | tf_op jit(solution)/shard_map/all_to_all | solution.py:265
  177.1 0.7 half_cols.7
  177.9 13.2 %all_to_all.68.got_ref = f32[16,16,128]{2,1,0:T(8,128)S(1)} all-to-all(f32[16,16,128]{2,1,0:T(8,128)S(1)} %half_cols.7), channel_id=1, replica_groups=mesh['z'=8,'core'=2,'x'=4,'y'=8] {'z','core'}, dimensions={0} | all-to-all | bytes 262144 | tf_op jit(solution)/shard_map/all_to_all | solution.py:270
  191.0 5.9 %final_terms.1 = (bf16[4,272,256]{2,1,0:T(8,128)(2,1)}, f32[16,128]{1,0:T(8,128)S(1)}) custom-call(f32[16,16,128]{2,1,0:T(8,128)S(1)} %all_to_all.68.got_ref, f32[256,2048]{1,0:T(8,128)} %all-gather.5.cloned.1.call-done.block_ref.wide_ref, bf16[8,4,256,256]{3,2,1,0:T(8,128)(2,1)} %all-gather.7.cloned.1.call-done.data_ref), custom_call_target="tpu_custom_call" | custom-call | tf_op jit(solution)/shard_map/final_terms/pallas_call | solution.py:25
  196.9 3.5 %all-to-all-start.11 = ((bf16[4,272,256]{2,1,0:T(8,128)(2,1)}), bf16[4,272,256]{2,1,0:T(8,128)(2,1)S(1)}, u32[]{:S(2)}, u32[]{:S(2)}) async-start(bf16[4,272,256]{2,1,0:T(8,128)(2,1)} %get-tuple-element.18), calls=%async_computation.11 | async-start | bytes 1114112 | tf_op jit(solution)/shard_map/all_to_all | solution.py:278
  200.4 0.6 bitcast_add_fusion
  201.0 9.6 %all-to-all-done.11.got_ref = bf16[4,272,256]{2,1,0:T(8,128)(2,1)S(1)} async-done(((bf16[4,272,256]{2,1,0:T(8,128)(2,1)}), bf16[4,272,256]{2,1,0:T(8,128)(2,1)S(1)}, u32[]{:S(2)}, u32[]{:S(2)}) %all-to-all-start.11) | async-done | bytes 557088 | tf_op jit(solution)/shard_map/all_to_all | solution.py:278
  210.6 0.9 combine.1
  (11 shorter events, 0.2 us)
Async XLA Ops:
  7.2 12.8 %slice-start = ((bf16[256,256]{1,0:T(8,128)(2,1)}), bf16[96,256]{1,0:T(8,128)(2,1)S(1)}, s32[]{:S(2)}) async-start(bf16[256,256]{1,0:T(8,128)(2,1)} %param.2), calls=%async_computation.15 | async-start | bytes 98304 | tf_op jit(solution)/shard_map/slice | solution.py:229
  7.2 62.5 %all-gather.9.cloned.1.call-start = ((), (), s32[]{:S(2)}) async-start(), calls=%async_computation.14 | async-start | bytes 2949120 | tf_op jit(solution)/shard_map/all_gather | solution.py:224
  45.1 5.0 %copy-start.3 = (bf16[256,256]{1,0:T(8,128)(2,1)S(1)}, bf16[256,256]{1,0:T(8,128)(2,1)}, u32[]{:S(2)}) copy-start(bf16[256,256]{1,0:T(8,128)(2,1)} %param.2) | copy-start | bytes 393220
  46.4 17.4 %all-to-all-start.2 = ((bf16[4,8,96,256]{3,2,1,0:T(8,128)(2,1)}), bf16[4,8,96,256]{3,2,1,0:T(8,128)(2,1)S(1)}, u32[]{:S(2)}, u32[]{:S(2)}) async-start(bf16[4,8,96,256]{3,2,1,0:T(8,128)(2,1)} %broadcast_in_dim.8), calls=%async_computation.2 | async-start | bytes 3145728 | tf_op jit(solution)/shard_map/all_to_all | solution.py:234
  50.0 79.6 %all-gather.5.cloned.1.call-start = ((), (), s32[]{:S(2)}) async-start(), calls=%async_computation.12 | async-start | bytes 2359296 | tf_op jit(solution)/shard_map/all_gather | solution.py:261
  63.8 2.2 %copy-start.2 = (bf16[256,8192]{1,0:T(8,128)(2,1)S(1)}, bf16[256,8192]{1,0:T(8,128)(2,1)}, u32[]{:S(2)}) copy-start(bf16[256,8192]{1,0:T(8,128)(2,1)} %data_ref.3) | copy-start | bytes 12582916
  77.1 14.3 %all-to-all-start.3 = ((f32[32,4,128]{2,1,0:T(4,128)}), f32[32,4,128]{2,1,0:T(4,128)S(1)}, u32[]{:S(2)}, u32[]{:S(2)}) async-start(f32[32,4,128]{2,1,0:T(4,128)} %get-tuple-element.14), calls=%async_computation.3 | async-start | bytes 131072 | tf_op jit(solution)/shard_map/all_to_all | solution.py:265
  82.5 108.5 %all-gather.7.cloned.1.call-start = ((), (), s32[]{:S(2)}) async-start(), calls=%async_computation.13 | async-start | bytes 4456448 | tf_op jit(solution)/shard_map/all_gather | solution.py:268
  129.5 1.6 copy-start
  131.1 15.2 %copy-start.1 = (f32[256,2048]{1,0:T(8,128)S(1)}, f32[256,2048]{1,0:T(8,128)}, u32[]{:S(2)}) copy-start(f32[256,2048]{1,0:T(8,128)} %all-gather.5.cloned.1.call-done.block_ref.wide_ref) | copy-start | bytes 6291460
  196.9 13.7 %all-to-all-start.11 = ((bf16[4,272,256]{2,1,0:T(8,128)(2,1)}), bf16[4,272,256]{2,1,0:T(8,128)(2,1)S(1)}, u32[]{:S(2)}, u32[]{:S(2)}) async-start(bf16[4,272,256]{2,1,0:T(8,128)(2,1)} %get-tuple-element.18), calls=%async_computation.11 | async-start | bytes 1114112 | tf_op jit(solution)/shard_map/all_to_all | solution.py:278
Sparse Core Ops, SparseCore 0:
  18.9 50.6 all-gather.8
  77.2 45.9 all-gather.4
  125.4 50.8 all-gather.6

commit v5 on v4

--- a/solution.py
+++ b/solution.py
@@ -54,37 +54,88 @@
     return top + jnp.log(jnp.sum(jnp.exp(got - top[None]), axis=0))
 
 
-def products(read, data_ref, nx, ny, width):
+def prepare_kernel(high, noise_ref, data_ref, by_x_ref, by_y_ref, sq_ref, held, sem):
+    nx = by_x_ref.shape[0]
+    ny, sent, width = by_y_ref.shape
+    rows = noise_ref.shape[0]
+    low = rows - high
+    share = (sent - low) // nx
+    at = (lax.axis_index(ROW[0]) * lax.axis_size(ROW[1]) + lax.axis_index(ROW[1])) * share
+    copy = pltpu.make_async_copy(data_ref.at[pl.ds(pl.multiple_of(at, share), share), :], held, sem)
+    copy.start()
+    for x in range(nx):
+        by_x_ref[x] = noise_ref[:high]
+    for y in range(ny):
+        by_y_ref[y, :low] = noise_ref[high:]
+    squares = jnp.square(noise_ref[...].astype(F32))
+    squares = as_rows(jnp.sum(squares, axis=1, keepdims=True))[:1]
+    for k in range(rows // LANES):
+        sq_ref[k : k + 1, :] = squares[:, lanes(k)]
+    copy.wait()
+    for y in range(ny):
+        for x in range(nx):
+            block = held[:, (x * ny + y) * width : (x * ny + y + 1) * width]
+            by_y_ref[y, low + x * share : low + (x + 1) * share] = block
+
+
+def data_copies(data_ref, held, sems):
+    ny, nx, _, width = held.shape
+    return [
+        [
+            pltpu.make_async_copy(
+                data_ref.at[:, (x * ny + y) * width : (x * ny + y + 1) * width], held.at[y, x], sems.at[y, x]
+            )
+            for x in range(nx)
+        ]
+        for y in range(ny)
+    ]
+
+
+def products(read, held):
+    ny, nx, _, _ = held.shape
     total = None
     for y in range(ny):
-        left = jnp.concatenate([read(y, x) for x in range(nx)], axis=1)
-        right = jnp.concatenate(
-            [data_ref[:, (x * ny + y) * width : (x * ny + y + 1) * width] for x in range(nx)], axis=1
-        )
+        left = [read(y, x) for x in range(nx)]
+        left = jnp.concatenate(left, axis=1)
+        right = jnp.concatenate([held[y, x] for x in range(nx)], axis=1)
         one = lax.dot_general(left, right, (((1,), (1,)), ((), ())), preferred_element_type=F32)
         total = one if total is None else total + one
     return total
 
 
-def second_kernel(scale, second_ref, data_ref, out_ref):
-    nx, ny, _, width = second_ref.shape
-    out_ref[...] = products(lambda y, x: second_ref[x, y], data_ref, nx, ny, width) * scale
-
-
-def first_kernel(scale, first_ref, data_ref, low_ref, pot_ref, sq_ref, out_ref, copy_ref, send_ref, held, sems):
-    ny, nx, high, width = first_ref.shape
-    copies = [pltpu.make_async_copy(first_ref.at[y], held.at[y], sems.at[y]) for y in range(ny)]
-    for copy in copies:
-        copy.start()
+def second_kernel(scale, second_ref, data_ref, out_ref, held, sems):
+    copies = data_copies(data_ref, held, sems)
+    for group in copies:
+        for copy in group:
+            copy.start()
+
+    def read(y, x):
+        copies[y][x].wait()
+        return second_ref[x, y]
+
+    out_ref[...] = products(read, held) * scale
+
+
+def first_kernel(
+    scale, first_ref, data_ref, low_ref, pot_ref, sq_ref, out_ref, copy_ref, send_ref, rows_held, held, sems, row_sems
+):
+    ny, _, high, _ = first_ref.shape
+    copies = data_copies(data_ref, held, sems)
+    row_copies = [pltpu.make_async_copy(first_ref.at[y], rows_held.at[y], row_sems.at[y]) for y in range(ny)]
+    for y in range(ny):
+        row_copies[y].start()
+        for copy in copies[y]:
+            copy.start()
 
     def read(y, x):
         if x == 0:
-            copies[y].wait()
-        return held[y, x]
-
-    out_ref[:high] = products(read, data_ref, nx, ny, width) * scale
+            row_copies[y].wait()
+        copies[y][x].wait()
+        return rows_held[y, x]
+
+    out_ref[:high] = products(read, held) * scale
     out_ref[high:] = low_ref[...]
-    out = pltpu.make_async_copy(out_ref, copy_ref, sems.at[ny])
+    out = pltpu.make_async_copy(out_ref, copy_ref, row_sems.at[ny])
     out.start()
     local = local_rows(out_ref, pot_ref[...])
     chunks = local.shape[1] // LANES
@@ -147,7 +198,7 @@
 def final_kernel(log_cols, got_ref, wide_ref, data_ref, out_ref, pot_ref, weights, held, sems):
     ny, nx, cols, width = data_ref.shape
     rows = wide_ref.shape[0]
-    copies = [pltpu.make_async_copy(data_ref.at[y], held.at[y], sems.at[y]) for y in range(ny)]
+    copies = [pltpu.make_async_copy(data_ref.at[:, x], held.at[x], sems.at[x]) for x in range(nx)]
     for copy in copies:
         copy.start()
     pot = -(log_cols + joined(got_ref[...]))
@@ -167,10 +218,9 @@
     place = lax.broadcasted_iota(jnp.int32, local.shape, 0)
     extra = jnp.where(place == 0, first, jnp.where(place == 1, second, third))
     extra = jnp.where(place < 3, extra, 0.0).astype(BF16)
-    for copy in copies:
-        copy.wait()
     for x in range(nx):
-        right = jnp.concatenate([held[y, x] for y in range(ny)], axis=0)
+        copies[x].wait()
+        right = jnp.concatenate([held[x, y] for y in range(ny)], axis=0)
         term = jnp.dot(weights[...], right, preferred_element_type=F32)
         out_ref[x, :rows, :] = (term * inverse).astype(BF16)
         out_ref[x, rows:, :] = extra
@@ -190,10 +240,10 @@
         data,
         scratch_shapes=[
             pltpu.VMEM(wide.shape, BF16),
-            pltpu.VMEM(data.shape, BF16),
-            pltpu.SemaphoreType.DMA((ny,)),
+            pltpu.VMEM((nx, ny, cols, width), BF16),
+            pltpu.SemaphoreType.DMA((nx,)),
         ],
-        vmem=52,
+        vmem=50,
     )
 
 
@@ -219,41 +269,60 @@
     log_rows, log_cols = _log(rows * nrow), _log(cols * ncol)
     chunks = rows // LANES
 
-    sent = jnp.broadcast_to(noise[None, :FIRST_ROWS], (nx, FIRST_ROWS, width))
-    part = lax.all_to_all(sent, "x", 0, 0)
-    first = lax.all_gather(part, "y")
     low = rows - FIRST_ROWS
     share = cols // nrow
-    piece = lax.dynamic_slice_in_dim(data, lax.axis_index(ROW) * share, share, 0)
-    piece = piece.reshape(share, nx, ny, width).transpose(2, 1, 0, 3).reshape(ny, nx * share, width)
-    sent = jnp.broadcast_to(noise[None, FIRST_ROWS:], (ny, low, width))
-    sent = jnp.concatenate([sent, piece], axis=1)
-    part, sent = lax.optimization_barrier((part, sent))
-    got = lax.all_to_all(sent, "y", 0, 0)
+    by_x, by_y, noise_sq = call(
+        functools.partial(prepare_kernel, FIRST_ROWS),
+        "prepare",
+        (
+            shape((nx, FIRST_ROWS, width), BF16),
+            shape((ny, low + nx * share, width), BF16),
+            shape((chunks, LANES)),
+        ),
+        [VMEM, HBM],
+        (VMEM, VMEM, VMEM),
+        noise,
+        data,
+        scratch_shapes=[pltpu.VMEM((share, features), BF16), pltpu.SemaphoreType.DMA],
+        vmem=52,
+    )
+    part = lax.all_to_all(by_x, "x", 0, 0)
+    first = lax.all_gather(part, "y")
+    part, by_y = lax.optimization_barrier((part, by_y))
+    got = lax.all_to_all(by_y, "y", 0, 0)
     second = jnp.broadcast_to(got[None, :, :low], (nx, ny, low, width))
     second = lax.all_to_all(second, "x", 0, 0)
     piece = got[:, low:].reshape(ny, nx, share, width)
 
-    noise_sq = jnp.sum(jnp.square(noise.astype(F32)), axis=1)
     data_sq = jnp.sum(jnp.square(data.astype(F32)), axis=1)
     col_pot = (data_sq * (-1.0 / (features * EPSILON))).reshape(-1, LANES)
     scale = 2.0 / (features * EPSILON)
     lower = call(
-        functools.partial(second_kernel, scale), "second_rows", shape((low, cols)), [VMEM, VMEM], VMEM, second, data
+        functools.partial(second_kernel, scale),
+        "second_rows",
+        shape((low, cols)),
+        [VMEM, HBM],
+        VMEM,
+        second,
+        data,
+        scratch_shapes=[pltpu.VMEM((ny, nx, cols, width), BF16), pltpu.SemaphoreType.DMA((ny, nx))],
+        vmem=50,
     )
     scaled, copied, sent = call(
         functools.partial(first_kernel, scale),
         "first_rows",
         (shape((rows, cols)), shape((rows, cols)), shape((ncol, 2 * chunks, LANES))),
-        [HBM, VMEM, VMEM, VMEM, VMEM],
+        [HBM, HBM, VMEM, VMEM, VMEM],
         (VMEM, HBM, VMEM),
         first,
         data,
         lower,
         col_pot,
-        noise_sq.reshape(-1, LANES),
+        noise_sq,
         scratch_shapes=[
             pltpu.VMEM((ny, nx, FIRST_ROWS, width), BF16),
+            pltpu.VMEM((ny, nx, cols, width), BF16),
+            pltpu.SemaphoreType.DMA((ny, nx)),
             pltpu.SemaphoreType.DMA((ny + 1,)),
         ],
         vmem=52,

time: 219 us -> 219 us (level)
  Pallas kernels: 19.5 us -> 22.3 us
    pallas_call x11 -> x12, Pallas kernels: 19.5 us -> 22.3 us  [call(): pl.pallas_call(kernel, out_shape=out_shape, in_specs=in_specs, out_specs=...]
  transfers between devices with their start and end apart: 6 -> 6, of which waited for: 4 -> 4; matrix products, arithmetic and copies ran while one was open for 3% -> 3% of each run, Pallas kernels for 2% -> 4%
where the time goes in v5:
time: 219 us
  blocking collectives  130 us (59%)
  waiting for transfers between devices  30.8 us (14%)
  Pallas kernels  22.3 us (10%)
  between operations  13.9 us (6%)
  starting transfers between devices  12.1 us (6%)
  local copies, waits for them, and re-layouts  6.17 us (3%)
  other arithmetic  3.71 us (2%)
    all_to_all x4, blocking collectives, shards(): got = lax.all_to_all(sent, ROW, 0, 0)  68.1 us
    all_to_all x3, blocking collectives, shards(): got = lax.all_to_all(sent, 'x' if step > WIDE_FROM else COL, 0, 0)  26.5 us
    all_to_all x1, blocking collectives, shards(): got = lax.all_to_all(by_y, 'y', 0, 0)  24.3 us
    pallas_call x12, Pallas kernels, call(): pl.pallas_call(kernel, out_shape=out_shape, in_specs=in_specs, out_specs=...  22.3 us
    all_to_all x1, waiting for transfers between devices, shards(): second = lax.all_to_all(second, 'x', 0, 0)  10.9 us
    all_to_all x1, blocking collectives, shards(): part = lax.all_to_all(by_x, 'x', 0, 0)  10.6 us
    all_to_all x1, waiting for transfers between devices, shards(): got = lax.all_to_all(terms, 'x', 0, 0)  9.62 us
    all_to_all x1, waiting for transfers between devices, shards(): got = lax.all_to_all(sent, 'x' if step > WIDE_FROM else COL, 0, 0)  8.08 us
  transfers between devices with their start and end apart: 6, of which 4 were waited for; matrix products, arithmetic and copies ran while one was open for 3% of the time, Pallas kernels for 4%

profile of v5, /device:TPU:1, one launch (start us, length us, event | category | flops | bytes accessed | tf_op | source)
XLA Modules:
  0.0 218.5 jit_solution(11653354542341335101)
XLA Ops:
  7.2 0.0 all-gather.9.cloned.1.call-start
  7.2 0.0 copy-start.3
  7.2 0.9 copy-done.3
  8.1 1.0 prepare.1
  9.1 10.6 %all_to_all.60 = bf16[4,160,256]{2,1,0:T(8,128)(2,1)} all-to-all(bf16[4,160,256]{2,1,0:T(8,128)(2,1)S(1)} %get-tuple-element.16), channel_id=1, replica_groups=mesh['z'=8,'core'=2,'x'=4,'y'=8] {'x'}, dimensions={0} | all-to-all | bytes 655360 | tf_op jit(solution)/shard_map/all_to_all | solution.py:289
  19.8 0.0 all-gather.9.cloned.1.call-update
  19.8 24.3 %all_to_all.61 = bf16[8,160,256]{2,1,0:T(8,128)(2,1)S(1)} all-to-all(bf16[8,160,256]{2,1,0:T(8,128)(2,1)S(1)} %get-tuple-element.18), channel_id=1, replica_groups=mesh['z'=8,'core'=2,'x'=4,'y'=8] {'y'}, dimensions={0} | all-to-all | bytes 1310720 | tf_op jit(solution)/shard_map/all_to_all | solution.py:292
  44.1 1.3 broadcast_in_dim.2
  45.4 3.6 %all-to-all-start.2 = ((bf16[4,8,96,256]{3,2,1,0:T(8,128)(2,1)}), bf16[4,8,96,256]{3,2,1,0:T(8,128)(2,1)S(1)}, u32[]{:S(2)}, u32[]{:S(2)}) async-start(bf16[4,8,96,256]{3,2,1,0:T(8,128)(2,1)} %broadcast_in_dim.2), calls=%async_computation.2 | async-start | bytes 3145728 | tf_op jit(solution)/shard_map/all_to_all | solution.py:294
  49.0 0.0 all-gather.5.cloned.1.call-start
  49.0 3.1 %multiply_reduce_fusion = f32[256]{0:T(256)S(1)} fusion(bf16[256,8192]{1,0:T(8,128)(2,1)} %data_ref.5), kind=kLoop, calls=%fused_computation | loop fusion | flops 6291200 | bytes 4195328 | tf_op jit(solution)/shard_map/reduce_sum | solution.py:297
  52.2 10.9 %all-to-all-done.2.second_ref = bf16[4,8,96,256]{3,2,1,0:T(8,128)(2,1)S(1)} async-done(((bf16[4,8,96,256]{3,2,1,0:T(8,128)(2,1)}), bf16[4,8,96,256]{3,2,1,0:T(8,128)(2,1)S(1)}, u32[]{:S(2)}, u32[]{:S(2)}) %all-to-all-start.2) | async-done | bytes 1572896 | tf_op jit(solution)/shard_map/all_to_all | solution.py:294
  63.1 4.3 %second_rows.1.low_ref = f32[96,256]{1,0:T(8,128)S(1)} custom-call(bf16[4,8,96,256]{3,2,1,0:T(8,128)(2,1)S(1)} %all-to-all-done.2.second_ref, bf16[256,8192]{1,0:T(8,128)(2,1)} %data_ref.5), custom_call_target="tpu_custom_call" | custom-call | tf_op jit(solution)/shard_map/second_rows/pallas_call | solution.py:25
  67.4 2.2 %all-gather.9.cloned.1.call-done = bf16[32,160,256]{2,1,0:T(8,128)(2,1)} async-done(((bf16[4,160,256]{2,1,0:T(8,128)(2,1)}), bf16[32,160,256]{2,1,0:T(8,128)(2,1)}) %all-gather.9.cloned.1.call-update) | async-done | bytes 2621456 | tf_op jit(solution)/shard_map/all_gather | solution.py:290
  69.6 6.8 %first_rows.1 = (f32[256,256]{1,0:T(8,128)S(1)}, f32[256,256]{1,0:T(8,128)}, f32[32,4,128]{2,1,0:T(4,128)}) custom-call(bf16[8,4,160,256]{3,2,1,0:T(8,128)(2,1)} %bitcast.7, bf16[256,8192]{1,0:T(8,128)(2,1)} %data_ref.5, f32[96,256]{1,0:T(8,128)S(1)} %second_rows.1.low_ref, f32[2,128]{1,0:T(2,128)S(1)} %multiply_bitcast_fusion.pot_ref, ...), custom_call_target="tpu_custom_call" | custom-call | tf_op jit(solution)/shard_map/first_rows/pallas_call | solution.py:25
  76.3 0.0 all-gather.5.cloned.1.call-update
  76.4 5.0 %all-to-all-start.3 = ((f32[32,4,128]{2,1,0:T(4,128)}), f32[32,4,128]{2,1,0:T(4,128)S(1)}, u32[]{:S(2)}, u32[]{:S(2)}) async-start(f32[32,4,128]{2,1,0:T(4,128)} %get-tuple-element.20), calls=%async_computation.3 | async-start | bytes 131072 | tf_op jit(solution)/shard_map/all_to_all | solution.py:334
  81.3 0.0 all-gather.7.cloned.1.call-start
  81.4 0.7 slice.9
  82.1 8.1 %all-to-all-done.3.got_ref.began_ref = f32[32,4,128]{2,1,0:T(4,128)S(1)} async-done(((f32[32,4,128]{2,1,0:T(4,128)}), f32[32,4,128]{2,1,0:T(4,128)S(1)}, u32[]{:S(2)}, u32[]{:S(2)}) %all-to-all-start.3) | async-done | bytes 65568 | tf_op jit(solution)/shard_map/all_to_all | solution.py:334
  90.2 0.0 all-gather.7.cloned.1.call-update
  90.2 0.2 half_cols.4
  90.5 25.8 %all_to_all.62.got_ref = f32[16,2,128]{2,1,0:T(2,128)S(1)} all-to-all(f32[16,2,128]{2,1,0:T(2,128)S(1)} %half_cols.4), channel_id=1, replica_groups=mesh['z'=8,'core'=2,'x'=4,'y'=8] {'z','core'}, dimensions={0} | all-to-all | bytes 32768 | tf_op jit(solution)/shard_map/all_to_all | solution.py:339
  116.3 0.3 half_rows.3
  116.6 11.7 %all_to_all.63.got_ref = f32[32,2,128]{2,1,0:T(2,128)S(1)} all-to-all(f32[32,2,128]{2,1,0:T(2,128)S(1)} %half_rows.3), channel_id=1, replica_groups=mesh['z'=8,'core'=2,'x'=4,'y'=8] {'x','y'}, dimensions={0} | all-to-all | bytes 65536 | tf_op jit(solution)/shard_map/all_to_all | solution.py:334
  128.4 0.0 all-gather.5.cloned.1.call-done.block_ref.wide_ref
  128.4 0.0 copy-start
  128.4 1.6 copy-done
  130.0 0.7 half_cols.5
  130.7 14.8 %all_to_all.64.got_ref = f32[16,16,128]{2,1,0:T(8,128)S(1)} all-to-all(f32[16,16,128]{2,1,0:T(8,128)S(1)} %half_cols.5), channel_id=1, replica_groups=mesh['z'=8,'core'=2,'x'=4,'y'=8] {'z','core'}, dimensions={0} | all-to-all | bytes 262144 | tf_op jit(solution)/shard_map/all_to_all | solution.py:339
  145.5 0.0 copy-start.1
  145.5 1.6 copy-done.1
  147.1 0.0 copy-start.2
  147.1 0.6 half_rows.4
  147.6 8.3 %all_to_all.65.got_ref = f32[4,2,128]{2,1,0:T(2,128)S(1)} all-to-all(f32[4,2,128]{2,1,0:T(2,128)S(1)} %half_rows.4), channel_id=1, replica_groups=mesh['z'=8,'core'=2,'x'=4,'y'=8] {'x'}, dimensions={0} | all-to-all | bytes 8192 | tf_op jit(solution)/shard_map/all_to_all | solution.py:334
  156.0 0.7 half_cols.6
  156.7 14.3 %all_to_all.66.got_ref = f32[16,16,128]{2,1,0:T(8,128)S(1)} all-to-all(f32[16,16,128]{2,1,0:T(8,128)S(1)} %half_cols.6), channel_id=1, replica_groups=mesh['z'=8,'core'=2,'x'=4,'y'=8] {'z','core'}, dimensions={0} | all-to-all | bytes 262144 | tf_op jit(solution)/shard_map/all_to_all | solution.py:339
  171.0 0.6 half_rows.5
  171.6 6.5 %all_to_all.67.got_ref = f32[4,2,128]{2,1,0:T(2,128)S(1)} all-to-all(f32[4,2,128]{2,1,0:T(2,128)S(1)} %half_rows.5), channel_id=1, replica_groups=mesh['z'=8,'core'=2,'x'=4,'y'=8] {'x'}, dimensions={0} | all-to-all | bytes 8192 | tf_op jit(solution)/shard_map/all_to_all | solution.py:334
  178.1 0.7 half_cols.7
  178.8 13.2 %all_to_all.68.got_ref = f32[16,16,128]{2,1,0:T(8,128)S(1)} all-to-all(f32[16,16,128]{2,1,0:T(8,128)S(1)} %half_cols.7), channel_id=1, replica_groups=mesh['z'=8,'core'=2,'x'=4,'y'=8] {'z','core'}, dimensions={0} | all-to-all | bytes 262144 | tf_op jit(solution)/shard_map/all_to_all | solution.py:339
  191.9 0.0 all-gather.7.cloned.1.call-done.data_ref
  191.9 0.0 copy-done.2
  191.9 5.4 %final_terms.1 = (bf16[4,272,256]{2,1,0:T(8,128)(2,1)}, f32[16,128]{1,0:T(8,128)S(1)}) custom-call(f32[16,16,128]{2,1,0:T(8,128)S(1)} %all_to_all.68.got_ref, f32[256,2048]{1,0:T(8,128)S(1)} %copy-done.2, bf16[8,4,256,256]{3,2,1,0:T(8,128)(2,1)} %all-gather.7.cloned.1.call-done.data_ref), custom_call_target="tpu_custom_call" | custom-call | tf_op jit(solution)/shard_map/final_terms/pallas_call | solution.py:25
  197.4 3.5 %all-to-all-start.11 = ((bf16[4,272,256]{2,1,0:T(8,128)(2,1)}), bf16[4,272,256]{2,1,0:T(8,128)(2,1)S(1)}, u32[]{:S(2)}, u32[]{:S(2)}) async-start(bf16[4,272,256]{2,1,0:T(8,128)(2,1)} %get-tuple-element.24), calls=%async_computation.11 | async-start | bytes 1114112 | tf_op jit(solution)/shard_map/all_to_all | solution.py:347
  200.9 0.6 bitcast_add_fusion
  201.4 9.6 %all-to-all-done.11.got_ref = bf16[4,272,256]{2,1,0:T(8,128)(2,1)S(1)} async-done(((bf16[4,272,256]{2,1,0:T(8,128)(2,1)}), bf16[4,272,256]{2,1,0:T(8,128)(2,1)S(1)}, u32[]{:S(2)}, u32[]{:S(2)}) %all-to-all-start.11) | async-done | bytes 557088 | tf_op jit(solution)/shard_map/all_to_all | solution.py:347
  211.0 0.9 combine.1
  (2 shorter events, 0.0 us)
Async XLA Ops:
  7.2 62.4 %all-gather.9.cloned.1.call-start = ((), (), s32[]{:S(2)}) async-start(), calls=%async_computation.14 | async-start | bytes 2949120 | tf_op jit(solution)/shard_map/all_gather | solution.py:290
  7.2 0.9 copy-start.3
  45.4 17.7 %all-to-all-start.2 = ((bf16[4,8,96,256]{3,2,1,0:T(8,128)(2,1)}), bf16[4,8,96,256]{3,2,1,0:T(8,128)(2,1)S(1)}, u32[]{:S(2)}, u32[]{:S(2)}) async-start(bf16[4,8,96,256]{3,2,1,0:T(8,128)(2,1)} %broadcast_in_dim.2), calls=%async_computation.2 | async-start | bytes 3145728 | tf_op jit(solution)/shard_map/all_to_all | solution.py:294
  49.0 79.4 %all-gather.5.cloned.1.call-start = ((), (), s32[]{:S(2)}) async-start(), calls=%async_computation.12 | async-start | bytes 2359296 | tf_op jit(solution)/shard_map/all_gather | solution.py:330
  76.4 13.8 %all-to-all-start.3 = ((f32[32,4,128]{2,1,0:T(4,128)}), f32[32,4,128]{2,1,0:T(4,128)S(1)}, u32[]{:S(2)}, u32[]{:S(2)}) async-start(f32[32,4,128]{2,1,0:T(4,128)} %get-tuple-element.20), calls=%async_computation.3 | async-start | bytes 131072 | tf_op jit(solution)/shard_map/all_to_all | solution.py:334
  81.3 110.6 %all-gather.7.cloned.1.call-start = ((), (), s32[]{:S(2)}) async-start(), calls=%async_computation.13 | async-start | bytes 4456448 | tf_op jit(solution)/shard_map/all_gather | solution.py:337
  128.4 1.6 copy-start
  145.5 1.6 copy-start.1
  147.1 44.9 %copy-start.2 = (f32[256,2048]{1,0:T(8,128)S(1)}, f32[256,2048]{1,0:T(8,128)}, u32[]{:S(2)}) copy-start(f32[256,2048]{1,0:T(8,128)} %all-gather.5.cloned.1.call-done.block_ref.wide_ref) | copy-start | bytes 6291460
  197.4 13.7 %all-to-all-start.11 = ((bf16[4,272,256]{2,1,0:T(8,128)(2,1)}), bf16[4,272,256]{2,1,0:T(8,128)(2,1)S(1)}, u32[]{:S(2)}, u32[]{:S(2)}) async-start(bf16[4,272,256]{2,1,0:T(8,128)(2,1)} %get-tuple-element.24), calls=%async_computation.11 | async-start | bytes 1114112 | tf_op jit(solution)/shard_map/all_to_all | solution.py:347
Sparse Core Ops, SparseCore 0:
  19.9 49.6 all-gather.8
  76.5 45.8 all-gather.4
  124.5 50.7 all-gather.6

commit v6 on v5

--- a/solution.py
+++ b/solution.py
@@ -78,64 +78,28 @@
             by_y_ref[y, low + x * share : low + (x + 1) * share] = block
 
 
-def data_copies(data_ref, held, sems):
-    ny, nx, _, width = held.shape
-    return [
-        [
-            pltpu.make_async_copy(
-                data_ref.at[:, (x * ny + y) * width : (x * ny + y + 1) * width], held.at[y, x], sems.at[y, x]
-            )
-            for x in range(nx)
-        ]
-        for y in range(ny)
-    ]
-
-
-def products(read, held):
-    ny, nx, _, _ = held.shape
+def products(read, data_ref, nx, ny, width):
     total = None
     for y in range(ny):
-        left = [read(y, x) for x in range(nx)]
-        left = jnp.concatenate(left, axis=1)
-        right = jnp.concatenate([held[y, x] for x in range(nx)], axis=1)
-        one = lax.dot_general(left, right, (((1,), (1,)), ((), ())), preferred_element_type=F32)
-        total = one if total is None else total + one
+        for x in range(nx):
+            at = (x * ny + y) * width
+            one = lax.dot_general(
+                read(y, x), data_ref[:, at : at + width], (((1,), (1,)), ((), ())), preferred_element_type=F32
+            )
+            total = one if total is None else total + one
     return total
 
 
-def second_kernel(scale, second_ref, data_ref, out_ref, held, sems):
-    copies = data_copies(data_ref, held, sems)
-    for group in copies:
-        for copy in group:
-            copy.start()
-
-    def read(y, x):
-        copies[y][x].wait()
-        return second_ref[x, y]
-
-    out_ref[...] = products(read, held) * scale
-
-
-def first_kernel(
-    scale, first_ref, data_ref, low_ref, pot_ref, sq_ref, out_ref, copy_ref, send_ref, rows_held, held, sems, row_sems
-):
-    ny, _, high, _ = first_ref.shape
-    copies = data_copies(data_ref, held, sems)
-    row_copies = [pltpu.make_async_copy(first_ref.at[y], rows_held.at[y], row_sems.at[y]) for y in range(ny)]
-    for y in range(ny):
-        row_copies[y].start()
-        for copy in copies[y]:
-            copy.start()
-
-    def read(y, x):
-        if x == 0:
-            row_copies[y].wait()
-        copies[y][x].wait()
-        return rows_held[y, x]
-
-    out_ref[:high] = products(read, held) * scale
+def second_kernel(scale, second_ref, data_ref, out_ref):
+    nx, ny, _, width = second_ref.shape
+    out_ref[...] = products(lambda y, x: second_ref[x, y], data_ref, nx, ny, width) * scale
+
+
+def first_kernel(scale, first_ref, data_ref, low_ref, pot_ref, sq_ref, out_ref, copy_ref, send_ref, sem):
+    ny, nx, high, width = first_ref.shape
+    out_ref[:high] = products(lambda y, x: first_ref[y, x], data_ref, nx, ny, width) * scale
     out_ref[high:] = low_ref[...]
-    out = pltpu.make_async_copy(out_ref, copy_ref, row_sems.at[ny])
+    out = pltpu.make_async_copy(out_ref, copy_ref, sem)
     out.start()
     local = local_rows(out_ref, pot_ref[...])
     chunks = local.shape[1] // LANES
@@ -174,31 +138,36 @@
     return call(functools.partial(rows_kernel, log_cols), "half_rows", out, [VMEM, VMEM], VMEM, got, block)
 
 
-def cols_kernel(log_rows, got_ref, block_ref, out_ref):
+def cols_kernel(log_rows, got_ref, block_ref, out_ref, *kept_ref):
     chunks = block_ref.shape[0] // LANES
     pot = -(log_rows + joined(got_ref[:, :chunks, :]))
     pot = jnp.concatenate([as_column(pot[k : k + 1]) for k in range(chunks)], axis=0)
     members = out_ref.shape[0]
     for k in range(out_ref.shape[1]):
-        scores = block_ref[:, lanes(k)] + pot
+        block = block_ref[:, lanes(k)]
+        for kept in kept_ref:
+            kept[:, lanes(k)] = block
+        scores = block + pot
         top = jnp.max(scores, axis=0, keepdims=True)
         local = top + jnp.log(jnp.sum(jnp.exp(scores - top), axis=0, keepdims=True))
         out_ref[:, k, :] = jnp.broadcast_to(local, (members, LANES))
 
 
-def half_cols(got, block, members, log_rows):
-    out = shape((members, block.shape[1] // LANES, LANES))
-    return call(functools.partial(cols_kernel, log_rows), "half_cols", out, [VMEM, VMEM], VMEM, got, block)
+def half_cols(got, block, members, log_rows, keep=False):
+    out = [shape((members, block.shape[1] // LANES, LANES))] + [shape(block.shape)] * keep
+    return call(
+        functools.partial(cols_kernel, log_rows), "half_cols", out, [VMEM, VMEM], [VMEM] * len(out), got, block
+    )
 
 
 def rounded(values):
     return values.astype(BF16).astype(F32)
 
 
-def final_kernel(log_cols, got_ref, wide_ref, data_ref, out_ref, pot_ref, weights, held, sems):
+def final_kernel(log_cols, got_ref, wide_ref, data_ref, out_ref, pot_ref, weights, held, terms, sems):
     ny, nx, cols, width = data_ref.shape
     rows = wide_ref.shape[0]
-    copies = [pltpu.make_async_copy(data_ref.at[:, x], held.at[x], sems.at[x]) for x in range(nx)]
+    copies = [pltpu.make_async_copy(data_ref.at[y], held.at[y], sems.at[y]) for y in range(ny)]
     for copy in copies:
         copy.start()
     pot = -(log_cols + joined(got_ref[...]))
@@ -218,10 +187,17 @@
     place = lax.broadcasted_iota(jnp.int32, local.shape, 0)
     extra = jnp.where(place == 0, first, jnp.where(place == 1, second, third))
     extra = jnp.where(place < 3, extra, 0.0).astype(BF16)
+    half = ny // 2
+    for copy in copies[:half]:
+        copy.wait()
     for x in range(nx):
-        copies[x].wait()
-        right = jnp.concatenate([held[x, y] for y in range(ny)], axis=0)
-        term = jnp.dot(weights[...], right, preferred_element_type=F32)
+        right = jnp.concatenate([held[y, x] for y in range(half)], axis=0)
+        terms[x] = jnp.dot(weights[:, : half * cols], right, preferred_element_type=F32)
+    for copy in copies[half:]:
+        copy.wait()
+    for x in range(nx):
+        right = jnp.concatenate([held[y, x] for y in range(half, ny)], axis=0)
+        term = terms[x] + jnp.dot(weights[:, half * cols :], right, preferred_element_type=F32)
         out_ref[x, :rows, :] = (term * inverse).astype(BF16)
         out_ref[x, rows:, :] = extra
 
@@ -240,8 +216,9 @@
         data,
         scratch_shapes=[
             pltpu.VMEM(wide.shape, BF16),
-            pltpu.VMEM((nx, ny, cols, width), BF16),
-            pltpu.SemaphoreType.DMA((nx,)),
+            pltpu.VMEM(data.shape, BF16),
+            pltpu.VMEM((nx, rows, width), F32),
+            pltpu.SemaphoreType.DMA((ny,)),
         ],
         vmem=50,
     )
@@ -294,38 +271,24 @@
     second = lax.all_to_all(second, "x", 0, 0)
     piece = got[:, low:].reshape(ny, nx, share, width)
 
+    scale = 2.0 / (features * EPSILON)
     data_sq = jnp.sum(jnp.square(data.astype(F32)), axis=1)
     col_pot = (data_sq * (-1.0 / (features * EPSILON))).reshape(-1, LANES)
-    scale = 2.0 / (features * EPSILON)
     lower = call(
-        functools.partial(second_kernel, scale),
-        "second_rows",
-        shape((low, cols)),
-        [VMEM, HBM],
-        VMEM,
-        second,
-        data,
-        scratch_shapes=[pltpu.VMEM((ny, nx, cols, width), BF16), pltpu.SemaphoreType.DMA((ny, nx))],
-        vmem=50,
+        functools.partial(second_kernel, scale), "second_rows", shape((low, cols)), [VMEM, VMEM], VMEM, second, data
     )
     scaled, copied, sent = call(
         functools.partial(first_kernel, scale),
         "first_rows",
         (shape((rows, cols)), shape((rows, cols)), shape((ncol, 2 * chunks, LANES))),
-        [HBM, HBM, VMEM, VMEM, VMEM],
+        [VMEM] * 5,
         (VMEM, HBM, VMEM),
         first,
         data,
         lower,
         col_pot,
         noise_sq,
-        scratch_shapes=[
-            pltpu.VMEM((ny, nx, FIRST_ROWS, width), BF16),
-            pltpu.VMEM((ny, nx, cols, width), BF16),
-            pltpu.SemaphoreType.DMA((ny, nx)),
-            pltpu.SemaphoreType.DMA((ny + 1,)),
-        ],
-        vmem=52,
+        scratch_shapes=[pltpu.SemaphoreType.DMA],
     )
     wide = lax.all_gather(copied, "y", axis=1, tiled=True)
 
@@ -335,7 +298,10 @@
         if step == 0:
             began, piece = lax.optimization_barrier((got, piece))
             mine = lax.all_gather(piece, ROW, axis=2, tiled=True)
-        sent = half_cols(got, wide if step >= WIDE_FROM else scaled, nrow, log_rows)
+        if step == WIDE_FROM:
+            sent, wide = half_cols(got, wide, nrow, log_rows, keep=True)
+        else:
+            (sent,) = half_cols(got, wide if step > WIDE_FROM else scaled, nrow, log_rows)
         got = lax.all_to_all(sent, ROW, 0, 0)
         if step < WIDE_FROM:
             sent = half_rows(got, scaled, ncol, log_cols)

time: 219 us -> 215 us (0.982)
  Pallas kernels: 22.3 us -> 14 us
  local copies, waits for them, and re-layouts: 6.17 us -> 10.7 us
    pallas_call x12, Pallas kernels: 22.3 us -> 14 us  [call(): pl.pallas_call(kernel, out_shape=out_shape, in_specs=in_specs, out_specs=...]
    unnamed x8 -> x10, local copies, waits for them, and re-layouts: 4.08 us -> 8.66 us
  transfers between devices with their start and end apart: 6 -> 6, of which waited for: 4 -> 4; matrix products, arithmetic and copies ran while one was open for 3% -> 3% of each run, Pallas kernels for 4% -> 3%
where the time goes in v6:
time: 215 us; the launch traced here: 214 us
  blocking collectives  128 us (60%)
  waiting for transfers between devices  31.5 us (15%)
  Pallas kernels  14 us (7%)
  between operations  13.9 us (6%)
  starting transfers between devices  12.1 us (6%)
  local copies, waits for them, and re-layouts  10.7 us (5%)
  other arithmetic  3.71 us (2%)
    all_to_all x4, blocking collectives, shards(): got = lax.all_to_all(sent, ROW, 0, 0)  66.8 us
    all_to_all x3, blocking collectives, shards(): got = lax.all_to_all(sent, 'x' if step > WIDE_FROM else COL, 0, 0)  26.4 us
    all_to_all x1, blocking collectives, shards(): got = lax.all_to_all(by_y, 'y', 0, 0)  24.3 us
    pallas_call x12, Pallas kernels, call(): pl.pallas_call(kernel, out_shape=out_shape, in_specs=in_specs, out_specs=...  14 us
    all_to_all x1, waiting for transfers between devices, shards(): second = lax.all_to_all(second, 'x', 0, 0)  10.9 us
    all_to_all x1, blocking collectives, shards(): part = lax.all_to_all(by_x, 'x', 0, 0)  10.6 us
    all_to_all x1, waiting for transfers between devices, shards(): got = lax.all_to_all(terms, 'x', 0, 0)  9.61 us
    unnamed x10, local copies, waits for them, and re-layouts  8.66 us
  transfers between devices with their start and end apart: 6, of which 4 were waited for; matrix products, arithmetic and copies ran while one was open for 3% of the time, Pallas kernels for 3%

profile of v6, /device:TPU:1, one launch (start us, length us, event | category | flops | bytes accessed | tf_op | source)
XLA Modules:
  0.0 214.1 jit_solution(2328757715230402088)
XLA Ops:
  7.2 0.0 all-gather.9.cloned.1.call-start
  7.2 0.0 copy-start.4
  7.2 0.9 copy-done.4
  8.1 1.0 prepare.1
  9.1 10.6 %all_to_all.60 = bf16[4,160,256]{2,1,0:T(8,128)(2,1)} all-to-all(bf16[4,160,256]{2,1,0:T(8,128)(2,1)S(1)} %get-tuple-element.18), channel_id=1, replica_groups=mesh['z'=8,'core'=2,'x'=4,'y'=8] {'x'}, dimensions={0} | all-to-all | bytes 655360 | tf_op jit(solution)/shard_map/all_to_all | solution.py:266
  19.8 0.0 all-gather.9.cloned.1.call-update
  19.8 24.3 %all_to_all.61 = bf16[8,160,256]{2,1,0:T(8,128)(2,1)S(1)} all-to-all(bf16[8,160,256]{2,1,0:T(8,128)(2,1)S(1)} %get-tuple-element.20), channel_id=1, replica_groups=mesh['z'=8,'core'=2,'x'=4,'y'=8] {'y'}, dimensions={0} | all-to-all | bytes 1310720 | tf_op jit(solution)/shard_map/all_to_all | solution.py:269
  44.1 1.3 broadcast_in_dim.2
  45.4 3.6 %all-to-all-start.2 = ((bf16[4,8,96,256]{3,2,1,0:T(8,128)(2,1)}), bf16[4,8,96,256]{3,2,1,0:T(8,128)(2,1)S(1)}, u32[]{:S(2)}, u32[]{:S(2)}) async-start(bf16[4,8,96,256]{3,2,1,0:T(8,128)(2,1)} %broadcast_in_dim.2), calls=%async_computation.2 | async-start | bytes 3145728 | tf_op jit(solution)/shard_map/all_to_all | solution.py:271
  49.0 0.0 all-gather.5.cloned.1.call-start
  49.0 3.1 %multiply_reduce_fusion = f32[256]{0:T(256)S(1)} fusion(bf16[256,8192]{1,0:T(8,128)(2,1)} %data_ref.5), kind=kLoop, calls=%fused_computation | loop fusion | flops 6291200 | bytes 4195328 | tf_op jit(solution)/shard_map/reduce_sum | solution.py:275
  52.2 10.9 %all-to-all-done.2.second_ref = bf16[4,8,96,256]{3,2,1,0:T(8,128)(2,1)S(1)} async-done(((bf16[4,8,96,256]{3,2,1,0:T(8,128)(2,1)}), bf16[4,8,96,256]{3,2,1,0:T(8,128)(2,1)S(1)}, u32[]{:S(2)}, u32[]{:S(2)}) %all-to-all-start.2) | async-done | bytes 1572896 | tf_op jit(solution)/shard_map/all_to_all | solution.py:271
  63.1 0.0 copy-start
  63.1 2.2 %copy-done = bf16[256,8192]{1,0:T(8,128)(2,1)S(1)} copy-done((bf16[256,8192]{1,0:T(8,128)(2,1)S(1)}, bf16[256,8192]{1,0:T(8,128)(2,1)}, u32[]{:S(2)}) %copy-start) | copy-done | bytes 4194328
  65.3 1.4 second_rows.1.low_ref
  66.7 2.8 %all-gather.9.cloned.1.call-done = bf16[32,160,256]{2,1,0:T(8,128)(2,1)} async-done(((bf16[4,160,256]{2,1,0:T(8,128)(2,1)}), bf16[32,160,256]{2,1,0:T(8,128)(2,1)}) %all-gather.9.cloned.1.call-update) | async-done | bytes 2621456 | tf_op jit(solution)/shard_map/all_gather | solution.py:267
  69.6 0.0 copy-start.1
  69.6 2.2 %copy-done.1 = bf16[256,8192]{1,0:T(8,128)(2,1)S(1)} copy-done((bf16[256,8192]{1,0:T(8,128)(2,1)S(1)}, bf16[256,8192]{1,0:T(8,128)(2,1)}, u32[]{:S(2)}) %copy-start.1) | copy-done | bytes 4194328
  71.8 0.0 copy-start.2
  71.8 1.7 copy-done.2
  73.5 2.9 %first_rows.1 = (f32[256,256]{1,0:T(8,128)S(1)}, f32[256,256]{1,0:T(8,128)}, f32[32,4,128]{2,1,0:T(4,128)}) custom-call(bf16[8,4,160,256]{3,2,1,0:T(8,128)(2,1)S(1)} %bitcast.7, bf16[256,8192]{1,0:T(8,128)(2,1)S(1)} %copy-done.1, f32[96,256]{1,0:T(8,128)S(1)} %second_rows.1.low_ref, f32[2,128]{1,0:T(2,128)S(1)} %multiply_bitcast_fusion.pot_ref, ...), custom_call_target="tpu_custom_call" | custom-call | tf_op jit(solution)/shard_map/first_rows/pallas_call | solution.py:25
  76.4 0.0 all-gather.5.cloned.1.call-update
  76.4 5.0 %all-to-all-start.3 = ((f32[32,4,128]{2,1,0:T(4,128)}), f32[32,4,128]{2,1,0:T(4,128)S(1)}, u32[]{:S(2)}, u32[]{:S(2)}) async-start(f32[32,4,128]{2,1,0:T(4,128)} %get-tuple-element.22), calls=%async_computation.3 | async-start | bytes 131072 | tf_op jit(solution)/shard_map/all_to_all | solution.py:297
  81.4 0.0 all-gather.7.cloned.1.call-start
  81.4 0.7 slice.9
  82.2 8.1 %all-to-all-done.3.got_ref.began_ref = f32[32,4,128]{2,1,0:T(4,128)S(1)} async-done(((f32[32,4,128]{2,1,0:T(4,128)}), f32[32,4,128]{2,1,0:T(4,128)S(1)}, u32[]{:S(2)}, u32[]{:S(2)}) %all-to-all-start.3) | async-done | bytes 65568 | tf_op jit(solution)/shard_map/all_to_all | solution.py:297
  90.3 0.0 all-gather.7.cloned.1.call-update
  90.3 0.2 half_cols.4
  90.5 25.2 %all_to_all.62.got_ref = f32[16,2,128]{2,1,0:T(2,128)S(1)} all-to-all(f32[16,2,128]{2,1,0:T(2,128)S(1)} %half_cols.4), channel_id=1, replica_groups=mesh['z'=8,'core'=2,'x'=4,'y'=8] {'z','core'}, dimensions={0} | all-to-all | bytes 32768 | tf_op jit(solution)/shard_map/all_to_all | solution.py:305
  115.7 0.3 half_rows.3
  116.0 11.8 %all_to_all.63.got_ref = f32[32,2,128]{2,1,0:T(2,128)S(1)} all-to-all(f32[32,2,128]{2,1,0:T(2,128)S(1)} %half_rows.3), channel_id=1, replica_groups=mesh['z'=8,'core'=2,'x'=4,'y'=8] {'x','y'}, dimensions={0} | all-to-all | bytes 65536 | tf_op jit(solution)/shard_map/all_to_all | solution.py:297
  127.8 0.0 all-gather.5.cloned.1.call-done.block_ref
  127.8 1.6 copy-done.3
  129.3 0.8 half_cols.5
  130.2 14.8 %all_to_all.64.got_ref = f32[16,16,128]{2,1,0:T(8,128)S(1)} all-to-all(f32[16,16,128]{2,1,0:T(8,128)S(1)} %get-tuple-element.25), channel_id=1, replica_groups=mesh['z'=8,'core'=2,'x'=4,'y'=8] {'z','core'}, dimensions={0} | all-to-all | bytes 262144 | tf_op jit(solution)/shard_map/all_to_all | solution.py:305
  144.9 0.6 half_rows.4
  145.5 8.2 %all_to_all.65.got_ref = f32[4,2,128]{2,1,0:T(2,128)S(1)} all-to-all(f32[4,2,128]{2,1,0:T(2,128)S(1)} %half_rows.4), channel_id=1, replica_groups=mesh['z'=8,'core'=2,'x'=4,'y'=8] {'x'}, dimensions={0} | all-to-all | bytes 8192 | tf_op jit(solution)/shard_map/all_to_all | solution.py:297
  153.7 0.7 half_cols.6
  154.4 14.0 %all_to_all.66.got_ref = f32[16,16,128]{2,1,0:T(8,128)S(1)} all-to-all(f32[16,16,128]{2,1,0:T(8,128)S(1)} %half_cols.6), channel_id=1, replica_groups=mesh['z'=8,'core'=2,'x'=4,'y'=8] {'z','core'}, dimensions={0} | all-to-all | bytes 262144 | tf_op jit(solution)/shard_map/all_to_all | solution.py:305
  168.3 0.6 half_rows.5
  168.9 6.5 %all_to_all.67.got_ref = f32[4,2,128]{2,1,0:T(2,128)S(1)} all-to-all(f32[4,2,128]{2,1,0:T(2,128)S(1)} %half_rows.5), channel_id=1, replica_groups=mesh['z'=8,'core'=2,'x'=4,'y'=8] {'x'}, dimensions={0} | all-to-all | bytes 8192 | tf_op jit(solution)/shard_map/all_to_all | solution.py:297
  175.4 0.7 half_cols.7
  176.1 13.0 %all_to_all.68.got_ref = f32[16,16,128]{2,1,0:T(8,128)S(1)} all-to-all(f32[16,16,128]{2,1,0:T(8,128)S(1)} %half_cols.7), channel_id=1, replica_groups=mesh['z'=8,'core'=2,'x'=4,'y'=8] {'z','core'}, dimensions={0} | all-to-all | bytes 262144 | tf_op jit(solution)/shard_map/all_to_all | solution.py:305
  189.1 3.8 %final_terms.1 = (bf16[4,272,256]{2,1,0:T(8,128)(2,1)}, f32[16,128]{1,0:T(8,128)S(1)}) custom-call(f32[16,16,128]{2,1,0:T(8,128)S(1)} %all_to_all.68.got_ref, f32[256,2048]{1,0:T(8,128)S(1)} %get-tuple-element.26.block_ref.wide_ref, bf16[8,4,256,256]{3,2,1,0:T(8,128)(2,1)} %all-gather.7.cloned.1.call-done.data_ref), custom_call_target="tpu_custom_call" | custom-call | tf_op jit(solution)/shard_map/final_terms/pallas_call | solution.py:25
  192.9 3.5 %all-to-all-start.11 = ((bf16[4,272,256]{2,1,0:T(8,128)(2,1)}), bf16[4,272,256]{2,1,0:T(8,128)(2,1)S(1)}, u32[]{:S(2)}, u32[]{:S(2)}) async-start(bf16[4,272,256]{2,1,0:T(8,128)(2,1)} %get-tuple-element.28), calls=%async_computation.11 | async-start | bytes 1114112 | tf_op jit(solution)/shard_map/all_to_all | solution.py:313
  196.4 0.6 bitcast_add_fusion
  197.0 9.6 %all-to-all-done.11.got_ref = bf16[4,272,256]{2,1,0:T(8,128)(2,1)S(1)} async-done(((bf16[4,272,256]{2,1,0:T(8,128)(2,1)}), bf16[4,272,256]{2,1,0:T(8,128)(2,1)S(1)}, u32[]{:S(2)}, u32[]{:S(2)}) %all-to-all-start.11) | async-done | bytes 557088 | tf_op jit(solution)/shard_map/all_to_all | solution.py:313
  206.6 0.9 combine.1
  (4 shorter events, 0.0 us)
Async XLA Ops:
  7.2 62.4 %all-gather.9.cloned.1.call-start = ((), (), s32[]{:S(2)}) async-start(), calls=%async_computation.14 | async-start | bytes 2949120 | tf_op jit(solution)/shard_map/all_gather | solution.py:267
  7.2 0.9 copy-start.4
  45.4 17.7 %all-to-all-start.2 = ((bf16[4,8,96,256]{3,2,1,0:T(8,128)(2,1)}), bf16[4,8,96,256]{3,2,1,0:T(8,128)(2,1)S(1)}, u32[]{:S(2)}, u32[]{:S(2)}) async-start(bf16[4,8,96,256]{3,2,1,0:T(8,128)(2,1)} %broadcast_in_dim.2), calls=%async_computation.2 | async-start | bytes 3145728 | tf_op jit(solution)/shard_map/all_to_all | solution.py:271
  49.0 78.8 %all-gather.5.cloned.1.call-start = ((), (), s32[]{:S(2)}) async-start(), calls=%async_computation.12 | async-start | bytes 2359296 | tf_op jit(solution)/shard_map/all_gather | solution.py:293
  63.1 2.2 %copy-start = (bf16[256,8192]{1,0:T(8,128)(2,1)S(1)}, bf16[256,8192]{1,0:T(8,128)(2,1)}, u32[]{:S(2)}) copy-start(bf16[256,8192]{1,0:T(8,128)(2,1)} %data_ref.5) | copy-start | bytes 12582916
  69.6 2.2 %copy-start.1 = (bf16[256,8192]{1,0:T(8,128)(2,1)S(1)}, bf16[256,8192]{1,0:T(8,128)(2,1)}, u32[]{:S(2)}) copy-start(bf16[256,8192]{1,0:T(8,128)(2,1)} %data_ref.5) | copy-start | bytes 12582916
  71.8 1.7 copy-start.2
  76.4 13.8 %all-to-all-start.3 = ((f32[32,4,128]{2,1,0:T(4,128)}), f32[32,4,128]{2,1,0:T(4,128)S(1)}, u32[]{:S(2)}, u32[]{:S(2)}) async-start(f32[32,4,128]{2,1,0:T(4,128)} %get-tuple-element.22), calls=%async_computation.3 | async-start | bytes 131072 | tf_op jit(solution)/shard_map/all_to_all | solution.py:297
  81.4 107.7 %all-gather.7.cloned.1.call-start = ((), (), s32[]{:S(2)}) async-start(), calls=%async_computation.13 | async-start | bytes 4456448 | tf_op jit(solution)/shard_map/all_gather | solution.py:300
  127.8 1.6 copy-start.3
  192.9 13.7 %all-to-all-start.11 = ((bf16[4,272,256]{2,1,0:T(8,128)(2,1)}), bf16[4,272,256]{2,1,0:T(8,128)(2,1)S(1)}, u32[]{:S(2)}, u32[]{:S(2)}) async-start(bf16[4,272,256]{2,1,0:T(8,128)(2,1)} %get-tuple-element.28), calls=%async_computation.11 | async-start | bytes 1114112 | tf_op jit(solution)/shard_map/all_to_all | solution.py:313
Sparse Core Ops, SparseCore 0:
  19.9 49.6 all-gather.8
  76.6 45.1 all-gather.4
  123.9 50.8 all-gather.6

commit v7 on v6

--- a/solution.py
+++ b/solution.py
@@ -21,7 +21,7 @@
 F32, BF16 = jnp.float32, jnp.bfloat16
 
 
-def call(kernel, name, out_shape, in_specs, out_specs, *args, scratch_shapes=(), vmem=40):
+def call(kernel, name, out_shape, in_specs, out_specs, *args, scratch_shapes=(), vmem=40, cost=None):
     return pl.pallas_call(
         kernel,
         out_shape=out_shape,
@@ -29,6 +29,7 @@
         out_specs=out_specs,
         scratch_shapes=scratch_shapes,
         compiler_params=pltpu.CompilerParams(vmem_limit_bytes=vmem * MIB),
+        cost_estimate=cost,
         name=name,
     )(*args)
 
@@ -78,6 +79,30 @@
             by_y_ref[y, low + x * share : low + (x + 1) * share] = block
 
 
+def fan_kernel(got_ref, second_ref, piece_ref):
+    nx, ny, low, _ = second_ref.shape
+    share = piece_ref.shape[2]
+    for y in range(ny):
+        block = got_ref[y, :low]
+        for x in range(nx):
+            second_ref[x, y] = block
+            piece_ref[y, x] = got_ref[y, low + x * share : low + (x + 1) * share]
+
+
+def load_kernel(scale, after_ref, data_ref, out_ref, pot_ref, sems):
+    parts = pot_ref.shape[0]
+    copies = [pltpu.make_async_copy(data_ref.at[lanes(k)], out_ref.at[lanes(k)], sems.at[k]) for k in range(parts)]
+    for copy in copies:
+        copy.start()
+    for k in range(parts):
+        copies[k].wait()
+        total = None
+        for f in range(out_ref.shape[1] // LANES):
+            block = out_ref[lanes(k), lanes(f)].astype(F32)
+            total = block * block if total is None else total + block * block
+        pot_ref[k : k + 1, :] = as_rows(jnp.sum(total, axis=1, keepdims=True))[:1] * scale
+
+
 def products(read, data_ref, nx, ny, width):
     total = None
     for y in range(ny):
@@ -138,25 +163,58 @@
     return call(functools.partial(rows_kernel, log_cols), "half_rows", out, [VMEM, VMEM], VMEM, got, block)
 
 
-def cols_kernel(log_rows, got_ref, block_ref, out_ref, *kept_ref):
-    chunks = block_ref.shape[0] // LANES
+def column_pot(got_ref, chunks, log_rows):
     pot = -(log_rows + joined(got_ref[:, :chunks, :]))
-    pot = jnp.concatenate([as_column(pot[k : k + 1]) for k in range(chunks)], axis=0)
-    members = out_ref.shape[0]
-    for k in range(out_ref.shape[1]):
-        block = block_ref[:, lanes(k)]
-        for kept in kept_ref:
-            kept[:, lanes(k)] = block
-        scores = block + pot
+    return jnp.concatenate([as_column(pot[k : k + 1]) for k in range(chunks)], axis=0)
+
+
+def send_cols(block_ref, pot, out_ref, places):
+    for k in places:
+        scores = block_ref[:, lanes(k)] + pot
         top = jnp.max(scores, axis=0, keepdims=True)
         local = top + jnp.log(jnp.sum(jnp.exp(scores - top), axis=0, keepdims=True))
-        out_ref[:, k, :] = jnp.broadcast_to(local, (members, LANES))
-
-
-def half_cols(got, block, members, log_rows, keep=False):
-    out = [shape((members, block.shape[1] // LANES, LANES))] + [shape(block.shape)] * keep
+        out_ref[:, k, :] = jnp.broadcast_to(local, (out_ref.shape[0], LANES))
+
+
+def cols_kernel(log_rows, got_ref, block_ref, out_ref):
+    pot = column_pot(got_ref, block_ref.shape[0] // LANES, log_rows)
+    send_cols(block_ref, pot, out_ref, range(out_ref.shape[1]))
+
+
+def half_cols(got, block, members, log_rows):
+    out = shape((members, block.shape[1] // LANES, LANES))
+    return call(functools.partial(cols_kernel, log_rows), "half_cols", out, [VMEM, VMEM], VMEM, got, block)
+
+
+def first_wide_kernel(log_rows, got_ref, block_ref, out_ref, held_ref, sems):
+    parts = sems.shape[0]
+    places = out_ref.shape[1] // parts
+    width = places * LANES
+    copies = [
+        pltpu.make_async_copy(
+            block_ref.at[:, k * width : (k + 1) * width], held_ref.at[:, k * width : (k + 1) * width], sems.at[k]
+        )
+        for k in range(parts)
+    ]
+    for copy in copies:
+        copy.start()
+    pot = column_pot(got_ref, block_ref.shape[0] // LANES, log_rows)
+    for k in range(parts):
+        copies[k].wait()
+        send_cols(held_ref, pot, out_ref, range(k * places, (k + 1) * places))
+
+
+def first_wide(got, block, members, log_rows):
     return call(
-        functools.partial(cols_kernel, log_rows), "half_cols", out, [VMEM, VMEM], [VMEM] * len(out), got, block
+        functools.partial(first_wide_kernel, log_rows),
+        "first_wide",
+        (shape((members, block.shape[1] // LANES, LANES)), shape(block.shape)),
+        [VMEM, HBM],
+        (VMEM, VMEM),
+        got,
+        block,
+        scratch_shapes=[pltpu.SemaphoreType.DMA((4,))],
+        vmem=51,
     )
 
 
@@ -267,15 +325,32 @@
     first = lax.all_gather(part, "y")
     part, by_y = lax.optimization_barrier((part, by_y))
     got = lax.all_to_all(by_y, "y", 0, 0)
-    second = jnp.broadcast_to(got[None, :, :low], (nx, ny, low, width))
+    second, piece = call(
+        fan_kernel,
+        "fan",
+        (shape((nx, ny, low, width), BF16), shape((ny, nx, share, width), BF16)),
+        [VMEM],
+        (VMEM, VMEM),
+        got,
+    )
     second = lax.all_to_all(second, "x", 0, 0)
-    piece = got[:, low:].reshape(ny, nx, share, width)
 
     scale = 2.0 / (features * EPSILON)
-    data_sq = jnp.sum(jnp.square(data.astype(F32)), axis=1)
-    col_pot = (data_sq * (-1.0 / (features * EPSILON))).reshape(-1, LANES)
+    held, col_pot = call(
+        functools.partial(load_kernel, -1.0 / (features * EPSILON)),
+        "load",
+        (shape(data.shape, BF16), shape((cols // LANES, LANES))),
+        [HBM, HBM],
+        (VMEM, VMEM),
+        got,
+        data,
+        scratch_shapes=[pltpu.SemaphoreType.DMA((cols // LANES,))],
+        vmem=48,
+        cost=pl.CostEstimate(flops=4 * data.size, bytes_accessed=4 * data.size, transcendentals=0),
+    )
+    data_sq = col_pot * -EPSILON
     lower = call(
-        functools.partial(second_kernel, scale), "second_rows", shape((low, cols)), [VMEM, VMEM], VMEM, second, data
+        functools.partial(second_kernel, scale), "second_rows", shape((low, cols)), [VMEM, VMEM], VMEM, second, held
     )
     scaled, copied, sent = call(
         functools.partial(first_kernel, scale),
@@ -284,7 +359,7 @@
         [VMEM] * 5,
         (VMEM, HBM, VMEM),
         first,
-        data,
+        held,
         lower,
         col_pot,
         noise_sq,
@@ -299,9 +374,9 @@
             began, piece = lax.optimization_barrier((got, piece))
             mine = lax.all_gather(piece, ROW, axis=2, tiled=True)
         if step == WIDE_FROM:
-            sent, wide = half_cols(got, wide, nrow, log_rows, keep=True)
+            sent, wide = first_wide(got, wide, nrow, log_rows)
         else:
-            (sent,) = half_cols(got, wide if step > WIDE_FROM else scaled, nrow, log_rows)
+            sent = half_cols(got, wide if step > WIDE_FROM else scaled, nrow, log_rows)
         got = lax.all_to_all(sent, ROW, 0, 0)
         if step < WIDE_FROM:
             sent = half_rows(got, scaled, ncol, log_cols)
@@ -309,7 +384,7 @@
             sent = half_rows(got, wide, nx, log_cols)
     terms, col_pot = final_terms(got, wide, mine, log_cols)
     own = lax.dynamic_slice_in_dim(col_pot, lax.axis_index("y") * (cols // LANES), cols // LANES, 0)
-    data_potential = data_sq / features + EPSILON * own.reshape(cols)
+    data_potential = (data_sq + EPSILON * own).reshape(cols)
     got = lax.all_to_all(terms, "x", 0, 0)
     targets, noise_potential = call(
         functools.partial(combine_kernel, log_rows, features),

time: 215 us -> 215 us (level)
  blocking collectives: 128 us -> 143 us
  waiting for transfers between devices: 31.5 us -> 21 us
  starting transfers between devices: 12.1 us -> 7.17 us
  Pallas kernels: 14 us -> 18.1 us
  other arithmetic: 3.71 us -> 0.57 us
    all_to_all x3 -> x4, blocking collectives: 26.4 us -> 39.8 us  [shards(): got = lax.all_to_all(sent, 'x' if step > WIDE_FROM else COL, 0, 0)]
    all_to_all x1 -> x0, waiting for transfers between devices: 8.09 us -> none  [shards(): got = lax.all_to_all(sent, 'x' if step > WIDE_FROM else COL, 0, 0)]
    all_to_all x1 -> x0, starting transfers between devices: 4.95 us -> none  [shards(): got = lax.all_to_all(sent, 'x' if step > WIDE_FROM else COL, 0, 0)]
    pallas_call x12 -> x14, Pallas kernels: 14 us -> 18.1 us  [call(): pl.pallas_call(kernel, out_shape=out_shape, in_specs=in_specs, out_specs=...]
    reduce_sum x1 -> x0, other arithmetic: 3.13 us -> none  [shards(): data_sq = jnp.sum(jnp.square(data.astype(F32)), axis=1)]
    unnamed x10 -> x12, local copies, waits for them, and re-layouts: 8.66 us -> 10.2 us
  transfers between devices with their start and end apart: 6 -> 5, of which waited for: 4 -> 3; matrix products, arithmetic and copies ran while one was open for 3% -> 0% of each run, Pallas kernels for 3% -> 5%
where the time goes in v7:
time: 215 us; the launch traced here: 214 us
  blocking collectives  143 us (67%)
  waiting for transfers between devices  21 us (10%)
  Pallas kernels  18.1 us (8%)
  between operations  13.9 us (6%)
  local copies, waits for them, and re-layouts  10.2 us (5%)
  starting transfers between devices  7.17 us (3%)
    all_to_all x4, blocking collectives, shards(): got = lax.all_to_all(sent, ROW, 0, 0)  68.1 us
    all_to_all x4, blocking collectives, shards(): got = lax.all_to_all(sent, 'x' if step > WIDE_FROM else COL, 0, 0)  39.8 us
    all_to_all x1, blocking collectives, shards(): got = lax.all_to_all(by_y, 'y', 0, 0)  24.3 us
    pallas_call x14, Pallas kernels, call(): pl.pallas_call(kernel, out_shape=out_shape, in_specs=in_specs, out_specs=...  18.1 us
    all_to_all x1, blocking collectives, shards(): part = lax.all_to_all(by_x, 'x', 0, 0)  10.6 us
    unnamed x12, local copies, waits for them, and re-layouts  10.2 us
    all_to_all x1, waiting for transfers between devices, shards(): got = lax.all_to_all(terms, 'x', 0, 0)  9.61 us
    all_to_all x1, waiting for transfers between devices, shards(): second = lax.all_to_all(second, 'x', 0, 0)  9.24 us
  transfers between devices with their start and end apart: 5, of which 3 were waited for; matrix products, arithmetic and copies ran while one was open for 0% of the time, Pallas kernels for 5%

profile of v7, /device:TPU:1, one launch (start us, length us, event | category | flops | bytes accessed | tf_op | source)
XLA Modules:
  0.0 213.8 jit_solution(6231381152060373741)
XLA Ops:
  7.2 0.0 all-gather.9.cloned.1.call-start
  7.2 0.0 copy-start.5
  7.2 0.9 copy-done.5
  8.1 1.0 prepare.1
  9.1 10.6 %all_to_all.60 = bf16[4,160,256]{2,1,0:T(8,128)(2,1)} all-to-all(bf16[4,160,256]{2,1,0:T(8,128)(2,1)S(1)} %get-tuple-element.22), channel_id=1, replica_groups=mesh['z'=8,'core'=2,'x'=4,'y'=8] {'x'}, dimensions={0} | all-to-all | bytes 655360 | tf_op jit(solution)/shard_map/all_to_all | solution.py:324
  19.8 0.0 all-gather.9.cloned.1.call-update
  19.8 24.3 %all_to_all.61.after_ref.got_ref = bf16[8,160,256]{2,1,0:T(8,128)(2,1)S(1)} all-to-all(bf16[8,160,256]{2,1,0:T(8,128)(2,1)S(1)} %get-tuple-element.24), channel_id=1, replica_groups=mesh['z'=8,'core'=2,'x'=4,'y'=8] {'y'}, dimensions={0} | all-to-all | bytes 1310720 | tf_op jit(solution)/shard_map/all_to_all | solution.py:327
  44.1 0.8 fan.1
  44.9 0.0 copy-start.4
  44.9 1.2 copy-done.4
  46.1 3.6 %all-to-all-start.2 = ((bf16[4,8,96,256]{3,2,1,0:T(8,128)(2,1)}), bf16[4,8,96,256]{3,2,1,0:T(8,128)(2,1)S(1)}, u32[]{:S(2)}, u32[]{:S(2)}) async-start(bf16[4,8,96,256]{3,2,1,0:T(8,128)(2,1)} %copy-done.4), calls=%async_computation.2 | async-start | bytes 3145728 | tf_op jit(solution)/shard_map/all_to_all | solution.py:336
  49.7 0.0 all-gather.5.cloned.1.call-start
  49.7 2.9 %load.1 = (bf16[256,8192]{1,0:T(8,128)(2,1)S(1)}, f32[2,128]{1,0:T(2,128)S(1)}) custom-call(bf16[8,160,256]{2,1,0:T(8,128)(2,1)S(1)} %all_to_all.61.after_ref.got_ref, bf16[256,8192]{1,0:T(8,128)(2,1)} %data_ref.3), custom_call_target="tpu_custom_call" | custom-call | flops 8388608 | bytes 8388608 | tf_op jit(solution)/shard_map/load/pallas_call | solution.py:25
  52.6 0.0 copy-start
  52.6 1.9 copy-done
  54.5 9.2 %all-to-all-done.2.second_ref = bf16[4,8,96,256]{3,2,1,0:T(8,128)(2,1)S(1)} async-done(((bf16[4,8,96,256]{3,2,1,0:T(8,128)(2,1)}), bf16[4,8,96,256]{3,2,1,0:T(8,128)(2,1)S(1)}, u32[]{:S(2)}, u32[]{:S(2)}) %all-to-all-start.2) | async-done | bytes 1572896 | tf_op jit(solution)/shard_map/all_to_all | solution.py:336
  63.8 0.0 copy-start.1
  63.8 2.2 %copy-done.1 = bf16[256,8192]{1,0:T(8,128)(2,1)S(1)} copy-done((bf16[256,8192]{1,0:T(8,128)(2,1)S(1)}, bf16[256,8192]{1,0:T(8,128)(2,1)}, u32[]{:S(2)}) %copy-start.1) | copy-done | bytes 4194328
  66.0 1.4 second_rows.1.low_ref
  67.4 2.1 all-gather.9.cloned.1.call-done
  69.6 0.0 copy-start.2
  69.6 2.2 %copy-done.2 = bf16[256,8192]{1,0:T(8,128)(2,1)S(1)} copy-done((bf16[256,8192]{1,0:T(8,128)(2,1)S(1)}, bf16[256,8192]{1,0:T(8,128)(2,1)}, u32[]{:S(2)}) %copy-start.2) | copy-done | bytes 4194328
  71.8 0.0 copy-start.3
  71.8 1.7 copy-done.3
  73.5 2.3 %first_rows.1 = (f32[256,256]{1,0:T(8,128)S(1)}, f32[256,256]{1,0:T(8,128)}, f32[32,4,128]{2,1,0:T(4,128)S(1)}) custom-call(bf16[8,4,160,256]{3,2,1,0:T(8,128)(2,1)S(1)} %bitcast.4, bf16[256,8192]{1,0:T(8,128)(2,1)S(1)} %copy-done.2, f32[96,256]{1,0:T(8,128)S(1)} %second_rows.1.low_ref, f32[2,128]{1,0:T(2,128)S(1)} %get-tuple-element.27.pot_ref, ...), custom_call_target="tpu_custom_call" | custom-call | tf_op jit(solution)/shard_map/first_rows/pallas_call | solution.py:25
  75.8 0.0 all-gather.5.cloned.1.call-update
  75.8 0.0 all-gather.7.cloned.1.call-start
  75.8 13.7 %all_to_all.62.got_ref.began_ref = f32[32,4,128]{2,1,0:T(4,128)S(1)} all-to-all(f32[32,4,128]{2,1,0:T(4,128)S(1)} %get-tuple-element.29), channel_id=1, replica_groups=mesh['z'=8,'core'=2,'x'=4,'y'=8] {'x','y'}, dimensions={0} | all-to-all | bytes 131072 | tf_op jit(solution)/shard_map/all_to_all | solution.py:372
  89.5 0.0 all-gather.7.cloned.1.call-update
  89.5 0.2 half_cols.3
  89.8 25.6 %all_to_all.63.got_ref = f32[16,2,128]{2,1,0:T(2,128)S(1)} all-to-all(f32[16,2,128]{2,1,0:T(2,128)S(1)} %half_cols.3), channel_id=1, replica_groups=mesh['z'=8,'core'=2,'x'=4,'y'=8] {'z','core'}, dimensions={0} | all-to-all | bytes 32768 | tf_op jit(solution)/shard_map/all_to_all | solution.py:380
  115.4 0.3 half_rows.3
  115.7 11.7 %all_to_all.64.got_ref = f32[32,2,128]{2,1,0:T(2,128)S(1)} all-to-all(f32[32,2,128]{2,1,0:T(2,128)S(1)} %half_rows.3), channel_id=1, replica_groups=mesh['z'=8,'core'=2,'x'=4,'y'=8] {'x','y'}, dimensions={0} | all-to-all | bytes 65536 | tf_op jit(solution)/shard_map/all_to_all | solution.py:372
  127.4 1.8 first_wide.1
  129.2 15.1 %all_to_all.65.got_ref = f32[16,16,128]{2,1,0:T(8,128)S(1)} all-to-all(f32[16,16,128]{2,1,0:T(8,128)S(1)} %get-tuple-element.32), channel_id=1, replica_groups=mesh['z'=8,'core'=2,'x'=4,'y'=8] {'z','core'}, dimensions={0} | all-to-all | bytes 262144 | tf_op jit(solution)/shard_map/all_to_all | solution.py:380
  144.3 0.6 half_rows.4
  144.9 8.0 %all_to_all.66.got_ref = f32[4,2,128]{2,1,0:T(2,128)S(1)} all-to-all(f32[4,2,128]{2,1,0:T(2,128)S(1)} %half_rows.4), channel_id=1, replica_groups=mesh['z'=8,'core'=2,'x'=4,'y'=8] {'x'}, dimensions={0} | all-to-all | bytes 8192 | tf_op jit(solution)/shard_map/all_to_all | solution.py:372
  152.8 0.7 half_cols.4
  153.5 14.3 %all_to_all.67.got_ref = f32[16,16,128]{2,1,0:T(8,128)S(1)} all-to-all(f32[16,16,128]{2,1,0:T(8,128)S(1)} %half_cols.4), channel_id=1, replica_groups=mesh['z'=8,'core'=2,'x'=4,'y'=8] {'z','core'}, dimensions={0} | all-to-all | bytes 262144 | tf_op jit(solution)/shard_map/all_to_all | solution.py:380
  167.9 0.6 half_rows.5
  168.5 6.5 %all_to_all.68.got_ref = f32[4,2,128]{2,1,0:T(2,128)S(1)} all-to-all(f32[4,2,128]{2,1,0:T(2,128)S(1)} %half_rows.5), channel_id=1, replica_groups=mesh['z'=8,'core'=2,'x'=4,'y'=8] {'x'}, dimensions={0} | all-to-all | bytes 8192 | tf_op jit(solution)/shard_map/all_to_all | solution.py:372
  175.0 0.7 half_cols.5
  175.7 13.2 %all_to_all.69.got_ref = f32[16,16,128]{2,1,0:T(8,128)S(1)} all-to-all(f32[16,16,128]{2,1,0:T(8,128)S(1)} %half_cols.5), channel_id=1, replica_groups=mesh['z'=8,'core'=2,'x'=4,'y'=8] {'z','core'}, dimensions={0} | all-to-all | bytes 262144 | tf_op jit(solution)/shard_map/all_to_all | solution.py:380
  188.8 3.8 %final_terms.1 = (bf16[4,272,256]{2,1,0:T(8,128)(2,1)}, f32[16,128]{1,0:T(8,128)S(1)}) custom-call(f32[16,16,128]{2,1,0:T(8,128)S(1)} %all_to_all.69.got_ref, f32[256,2048]{1,0:T(8,128)S(1)} %get-tuple-element.33.block_ref.wide_ref, bf16[8,4,256,256]{3,2,1,0:T(8,128)(2,1)} %all-gather.7.cloned.1.call-done.data_ref), custom_call_target="tpu_custom_call" | custom-call | tf_op jit(solution)/shard_map/final_terms/pallas_call | solution.py:25
  192.7 3.5 %all-to-all-start.11 = ((bf16[4,272,256]{2,1,0:T(8,128)(2,1)}), bf16[4,272,256]{2,1,0:T(8,128)(2,1)S(1)}, u32[]{:S(2)}, u32[]{:S(2)}) async-start(bf16[4,272,256]{2,1,0:T(8,128)(2,1)} %get-tuple-element.36), calls=%async_computation.11 | async-start | bytes 1114112 | tf_op jit(solution)/shard_map/all_to_all | solution.py:388
  196.2 0.6 add_bitcast_fusion
  196.7 9.6 %all-to-all-done.11.got_ref = bf16[4,272,256]{2,1,0:T(8,128)(2,1)S(1)} async-done(((bf16[4,272,256]{2,1,0:T(8,128)(2,1)}), bf16[4,272,256]{2,1,0:T(8,128)(2,1)S(1)}, u32[]{:S(2)}, u32[]{:S(2)}) %all-to-all-start.11) | async-done | bytes 557088 | tf_op jit(solution)/shard_map/all_to_all | solution.py:388
  206.4 0.9 combine.1
  (2 shorter events, 0.0 us)
Async XLA Ops:
  7.2 62.4 %all-gather.9.cloned.1.call-start = ((), (), s32[]{:S(2)}) async-start(), calls=%async_computation.14 | async-start | bytes 2949120 | tf_op jit(solution)/shard_map/all_gather | solution.py:325
  7.2 0.9 copy-start.5
  44.9 1.2 copy-start.4
  46.1 17.7 %all-to-all-start.2 = ((bf16[4,8,96,256]{3,2,1,0:T(8,128)(2,1)}), bf16[4,8,96,256]{3,2,1,0:T(8,128)(2,1)S(1)}, u32[]{:S(2)}, u32[]{:S(2)}) async-start(bf16[4,8,96,256]{3,2,1,0:T(8,128)(2,1)} %copy-done.4), calls=%async_computation.2 | async-start | bytes 3145728 | tf_op jit(solution)/shard_map/all_to_all | solution.py:336
  49.7 77.7 %all-gather.5.cloned.1.call-start = ((), (), s32[]{:S(2)}) async-start(), calls=%async_computation.12 | async-start | bytes 2359296 | tf_op jit(solution)/shard_map/all_gather | solution.py:368
  52.6 1.9 copy-start
  63.8 2.2 %copy-start.1 = (bf16[256,8192]{1,0:T(8,128)(2,1)S(1)}, bf16[256,8192]{1,0:T(8,128)(2,1)}, u32[]{:S(2)}) copy-start(bf16[256,8192]{1,0:T(8,128)(2,1)} %copy-done) | copy-start | bytes 12582916
  69.6 2.2 %copy-start.2 = (bf16[256,8192]{1,0:T(8,128)(2,1)S(1)}, bf16[256,8192]{1,0:T(8,128)(2,1)}, u32[]{:S(2)}) copy-start(bf16[256,8192]{1,0:T(8,128)(2,1)} %copy-done) | copy-start | bytes 12582916
  71.8 1.7 copy-start.3
  75.8 113.1 %all-gather.7.cloned.1.call-start = ((), (), s32[]{:S(2)}) async-start(), calls=%async_computation.13 | async-start | bytes 4456448 | tf_op jit(solution)/shard_map/all_gather | solution.py:375
  192.7 13.7 %all-to-all-start.11 = ((bf16[4,272,256]{2,1,0:T(8,128)(2,1)}), bf16[4,272,256]{2,1,0:T(8,128)(2,1)S(1)}, u32[]{:S(2)}, u32[]{:S(2)}) async-start(bf16[4,272,256]{2,1,0:T(8,128)(2,1)} %get-tuple-element.36), calls=%async_computation.11 | async-start | bytes 1114112 | tf_op jit(solution)/shard_map/all_to_all | solution.py:388
Sparse Core Ops, SparseCore 0:
  19.9 49.6 all-gather.8
  75.9 46.0 all-gather.4
  124.1 50.6 all-gather.6

commit v8 on v7

--- a/solution.py
+++ b/solution.py
@@ -21,7 +21,7 @@
 F32, BF16 = jnp.float32, jnp.bfloat16
 
 
-def call(kernel, name, out_shape, in_specs, out_specs, *args, scratch_shapes=(), vmem=40, cost=None):
+def call(kernel, name, out_shape, in_specs, out_specs, *args, scratch_shapes=(), vmem=40):
     return pl.pallas_call(
         kernel,
         out_shape=out_shape,
@@ -29,7 +29,6 @@
         out_specs=out_specs,
         scratch_shapes=scratch_shapes,
         compiler_params=pltpu.CompilerParams(vmem_limit_bytes=vmem * MIB),
-        cost_estimate=cost,
         name=name,
     )(*args)
 
@@ -79,52 +78,36 @@
             by_y_ref[y, low + x * share : low + (x + 1) * share] = block
 
 
-def fan_kernel(got_ref, second_ref, piece_ref):
-    nx, ny, low, _ = second_ref.shape
-    share = piece_ref.shape[2]
-    for y in range(ny):
-        block = got_ref[y, :low]
-        for x in range(nx):
-            second_ref[x, y] = block
-            piece_ref[y, x] = got_ref[y, low + x * share : low + (x + 1) * share]
-
-
-def load_kernel(scale, after_ref, data_ref, out_ref, pot_ref, sems):
-    parts = pot_ref.shape[0]
-    copies = [pltpu.make_async_copy(data_ref.at[lanes(k)], out_ref.at[lanes(k)], sems.at[k]) for k in range(parts)]
-    for copy in copies:
-        copy.start()
-    for k in range(parts):
-        copies[k].wait()
-        total = None
-        for f in range(out_ref.shape[1] // LANES):
-            block = out_ref[lanes(k), lanes(f)].astype(F32)
-            total = block * block if total is None else total + block * block
-        pot_ref[k : k + 1, :] = as_rows(jnp.sum(total, axis=1, keepdims=True))[:1] * scale
-
-
-def products(read, data_ref, nx, ny, width):
+def inner_kernel(
+    scale, first_ref, second_ref, data_ref, pot_ref, sq_ref, out_ref, copy_ref, send_ref, rows_held, held, row_sems, sems
+):
+    ny, nx, _, width = first_ref.shape
+    wide = ny * width
+    copies = [
+        (
+            pltpu.make_async_copy(
+                data_ref.at[:, x * wide : (x + 1) * wide], held.at[:, x * wide : (x + 1) * wide], sems.at[x]
+            ),
+            pltpu.make_async_copy(first_ref.at[:, x], rows_held.at[:, x], row_sems.at[x]),
+        )
+        for x in range(nx)
+    ]
+    for pair in copies:
+        for copy in pair:
+            copy.start()
     total = None
-    for y in range(ny):
-        for x in range(nx):
-            at = (x * ny + y) * width
+    for x in range(nx):
+        for copy in copies[x]:
+            copy.wait()
+        for y in range(ny):
+            left = jnp.concatenate([rows_held[y, x], second_ref[x, y]], axis=0)
+            at = x * wide + y * width
             one = lax.dot_general(
-                read(y, x), data_ref[:, at : at + width], (((1,), (1,)), ((), ())), preferred_element_type=F32
+                left, held[:, at : at + width], (((1,), (1,)), ((), ())), preferred_element_type=F32
             )
             total = one if total is None else total + one
-    return total
-
-
-def second_kernel(scale, second_ref, data_ref, out_ref):
-    nx, ny, _, width = second_ref.shape
-    out_ref[...] = products(lambda y, x: second_ref[x, y], data_ref, nx, ny, width) * scale
-
-
-def first_kernel(scale, first_ref, data_ref, low_ref, pot_ref, sq_ref, out_ref, copy_ref, send_ref, sem):
-    ny, nx, high, width = first_ref.shape
-    out_ref[:high] = products(lambda y, x: first_ref[y, x], data_ref, nx, ny, width) * scale
-    out_ref[high:] = low_ref[...]
-    out = pltpu.make_async_copy(out_ref, copy_ref, sem)
+    out_ref[...] = total * scale
+    out = pltpu.make_async_copy(out_ref, copy_ref, sems.at[nx])
     out.start()
     local = local_rows(out_ref, pot_ref[...])
     chunks = local.shape[1] // LANES
@@ -325,45 +308,31 @@
     first = lax.all_gather(part, "y")
     part, by_y = lax.optimization_barrier((part, by_y))
     got = lax.all_to_all(by_y, "y", 0, 0)
-    second, piece = call(
-        fan_kernel,
-        "fan",
-        (shape((nx, ny, low, width), BF16), shape((ny, nx, share, width), BF16)),
-        [VMEM],
-        (VMEM, VMEM),
-        got,
-    )
+    second = jnp.broadcast_to(got[None, :, :low], (nx, ny, low, width))
     second = lax.all_to_all(second, "x", 0, 0)
-
+    piece = got[:, low:].reshape(ny, nx, share, width)
+
+    data_sq = jnp.sum(jnp.square(data.astype(F32)), axis=1)
+    col_pot = (data_sq * (-1.0 / (features * EPSILON))).reshape(-1, LANES)
     scale = 2.0 / (features * EPSILON)
-    held, col_pot = call(
-        functools.partial(load_kernel, -1.0 / (features * EPSILON)),
-        "load",
-        (shape(data.shape, BF16), shape((cols // LANES, LANES))),
-        [HBM, HBM],
-        (VMEM, VMEM),
-        got,
-        data,
-        scratch_shapes=[pltpu.SemaphoreType.DMA((cols // LANES,))],
-        vmem=48,
-        cost=pl.CostEstimate(flops=4 * data.size, bytes_accessed=4 * data.size, transcendentals=0),
-    )
-    data_sq = col_pot * -EPSILON
-    lower = call(
-        functools.partial(second_kernel, scale), "second_rows", shape((low, cols)), [VMEM, VMEM], VMEM, second, held
-    )
     scaled, copied, sent = call(
-        functools.partial(first_kernel, scale),
-        "first_rows",
+        functools.partial(inner_kernel, scale),
+        "inner",
         (shape((rows, cols)), shape((rows, cols)), shape((ncol, 2 * chunks, LANES))),
-        [VMEM] * 5,
+        [HBM, VMEM, HBM, VMEM, VMEM],
         (VMEM, HBM, VMEM),
         first,
-        held,
-        lower,
+        second,
+        data,
         col_pot,
         noise_sq,
-        scratch_shapes=[pltpu.SemaphoreType.DMA],
+        scratch_shapes=[
+            pltpu.VMEM(first.shape, BF16),
+            pltpu.VMEM(data.shape, BF16),
+            pltpu.SemaphoreType.DMA((nx,)),
+            pltpu.SemaphoreType.DMA((nx + 1,)),
+        ],
+        vmem=51,
     )
     wide = lax.all_gather(copied, "y", axis=1, tiled=True)
 
@@ -384,7 +353,7 @@
             sent = half_rows(got, wide, nx, log_cols)
     terms, col_pot = final_terms(got, wide, mine, log_cols)
     own = lax.dynamic_slice_in_dim(col_pot, lax.axis_index("y") * (cols // LANES), cols // LANES, 0)
-    data_potential = (data_sq + EPSILON * own).reshape(cols)
+    data_potential = data_sq / features + EPSILON * own.reshape(cols)
     got = lax.all_to_all(terms, "x", 0, 0)
     targets, noise_potential = call(
         functools.partial(combine_kernel, log_rows, features),

time: 215 us -> 210 us (0.977)
  blocking collectives: 143 us -> 126 us
  waiting for transfers between devices: 21 us -> 35.1 us
  local copies, waits for them, and re-layouts: 10.2 us -> 3 us
  starting transfers between devices: 7.17 us -> 12.1 us
  other arithmetic: 0.57 us -> 3.71 us
    all_to_all x4 -> x3, blocking collectives: 39.8 us -> 26.3 us  [shards(): got = lax.all_to_all(sent, 'x' if step > WIDE_FROM else COL, 0, 0)]
    unnamed x12 -> x2, local copies, waits for them, and re-layouts: 10.2 us -> 0.9 us
    all_to_all x0 -> x1, waiting for transfers between devices: none -> 8.08 us  [shards(): got = lax.all_to_all(sent, 'x' if step > WIDE_FROM else COL, 0, 0)]
    all_to_all x0 -> x1, starting transfers between devices: none -> 4.95 us  [shards(): got = lax.all_to_all(sent, 'x' if step > WIDE_FROM else COL, 0, 0)]
    all_gather x1, waiting for transfers between devices: 2.12 us -> 6.48 us  [shards(): first = lax.all_gather(part, 'y')]
    all_to_all x4, blocking collectives: 68.1 us -> 64.3 us  [shards(): got = lax.all_to_all(sent, ROW, 0, 0)]
    reduce_sum x0 -> x1, other arithmetic: none -> 3.13 us  [shards(): data_sq = jnp.sum(jnp.square(data.astype(F32)), axis=1)]
    pallas_call x14 -> x11, Pallas kernels: 18.1 us -> 16.2 us  [call(): pl.pallas_call(kernel, out_shape=out_shape, in_specs=in_specs, out_specs=...]
  transfers between devices with their start and end apart: 5 -> 6, of which waited for: 3 -> 4; matrix products, arithmetic and copies ran while one was open for 0% -> 3% of each run, Pallas kernels for 5% -> 2%
where the time goes in v8:
time: 210 us
  blocking collectives  126 us (60%)
  waiting for transfers between devices  35.1 us (17%)
  Pallas kernels  16.2 us (8%)
  between operations  13.8 us (7%)
  starting transfers between devices  12.1 us (6%)
  other arithmetic  3.71 us (2%)
  local copies, waits for them, and re-layouts  3 us (1%)
    all_to_all x4, blocking collectives, shards(): got = lax.all_to_all(sent, ROW, 0, 0)  64.3 us
    all_to_all x3, blocking collectives, shards(): got = lax.all_to_all(sent, 'x' if step > WIDE_FROM else COL, 0, 0)  26.3 us
    all_to_all x1, blocking collectives, shards(): got = lax.all_to_all(by_y, 'y', 0, 0)  24.3 us
    pallas_call x11, Pallas kernels, call(): pl.pallas_call(kernel, out_shape=out_shape, in_specs=in_specs, out_specs=...  16.2 us
    all_to_all x1, waiting for transfers between devices, shards(): second = lax.all_to_all(second, 'x', 0, 0)  10.9 us
    all_to_all x1, blocking collectives, shards(): part = lax.all_to_all(by_x, 'x', 0, 0)  10.6 us
    all_to_all x1, waiting for transfers between devices, shards(): got = lax.all_to_all(terms, 'x', 0, 0)  9.61 us
    all_to_all x1, waiting for transfers between devices, shards(): got = lax.all_to_all(sent, 'x' if step > WIDE_FROM else COL, 0, 0)  8.08 us
  transfers between devices with their start and end apart: 6, of which 4 were waited for; matrix products, arithmetic and copies ran while one was open for 3% of the time, Pallas kernels for 2%

profile of v8, /device:TPU:1, one launch (start us, length us, event | category | flops | bytes accessed | tf_op | source)
XLA Modules:
  0.0 209.6 jit_solution(11012621366526304498)
XLA Ops:
  7.2 0.0 all-gather.9.cloned.1.call-start
  7.2 0.0 copy-start
  7.2 0.9 copy-done
  8.1 1.0 prepare.1
  9.1 10.6 %all_to_all.60 = bf16[4,160,256]{2,1,0:T(8,128)(2,1)} all-to-all(bf16[4,160,256]{2,1,0:T(8,128)(2,1)S(1)} %get-tuple-element.18), channel_id=1, replica_groups=mesh['z'=8,'core'=2,'x'=4,'y'=8] {'x'}, dimensions={0} | all-to-all | bytes 655360 | tf_op jit(solution)/shard_map/all_to_all | solution.py:307
  19.8 0.0 all-gather.9.cloned.1.call-update
  19.8 24.3 %all_to_all.61 = bf16[8,160,256]{2,1,0:T(8,128)(2,1)S(1)} all-to-all(bf16[8,160,256]{2,1,0:T(8,128)(2,1)S(1)} %get-tuple-element.20), channel_id=1, replica_groups=mesh['z'=8,'core'=2,'x'=4,'y'=8] {'y'}, dimensions={0} | all-to-all | bytes 1310720 | tf_op jit(solution)/shard_map/all_to_all | solution.py:310
  44.1 1.3 broadcast_in_dim.2
  45.4 3.6 %all-to-all-start.2 = ((bf16[4,8,96,256]{3,2,1,0:T(8,128)(2,1)}), bf16[4,8,96,256]{3,2,1,0:T(8,128)(2,1)S(1)}, u32[]{:S(2)}, u32[]{:S(2)}) async-start(bf16[4,8,96,256]{3,2,1,0:T(8,128)(2,1)} %broadcast_in_dim.2), calls=%async_computation.2 | async-start | bytes 3145728 | tf_op jit(solution)/shard_map/all_to_all | solution.py:312
  49.0 0.0 all-gather.5.cloned.1.call-start
  49.0 3.1 %multiply_reduce_fusion = f32[256]{0:T(256)S(1)} fusion(bf16[256,8192]{1,0:T(8,128)(2,1)} %data_ref.3), kind=kLoop, calls=%fused_computation | loop fusion | flops 6291200 | bytes 4195328 | tf_op jit(solution)/shard_map/reduce_sum | solution.py:315
  52.2 10.9 %all-to-all-done.2.second_ref = bf16[4,8,96,256]{3,2,1,0:T(8,128)(2,1)S(1)} async-done(((bf16[4,8,96,256]{3,2,1,0:T(8,128)(2,1)}), bf16[4,8,96,256]{3,2,1,0:T(8,128)(2,1)S(1)}, u32[]{:S(2)}, u32[]{:S(2)}) %all-to-all-start.2) | async-done | bytes 1572896 | tf_op jit(solution)/shard_map/all_to_all | solution.py:312
  63.1 6.5 %all-gather.9.cloned.1.call-done = bf16[32,160,256]{2,1,0:T(8,128)(2,1)} async-done(((bf16[4,160,256]{2,1,0:T(8,128)(2,1)}), bf16[32,160,256]{2,1,0:T(8,128)(2,1)}) %all-gather.9.cloned.1.call-update) | async-done | bytes 2621456 | tf_op jit(solution)/shard_map/all_gather | solution.py:308
  69.6 5.5 %inner.1 = (f32[256,256]{1,0:T(8,128)S(1)}, f32[256,256]{1,0:T(8,128)}, f32[32,4,128]{2,1,0:T(4,128)}) custom-call(bf16[8,4,160,256]{3,2,1,0:T(8,128)(2,1)} %bitcast.7, bf16[4,8,96,256]{3,2,1,0:T(8,128)(2,1)S(1)} %all-to-all-done.2.second_ref, bf16[256,8192]{1,0:T(8,128)(2,1)} %data_ref.3, f32[2,128]{1,0:T(2,128)S(1)} %multiply_bitcast_fusion.pot_ref, ...), custom_call_target="tpu_custom_call" | custom-call | tf_op jit(solution)/shard_map/inner/pallas_call | solution.py:25
  75.1 0.0 all-gather.5.cloned.1.call-update
  75.1 5.0 %all-to-all-start.3 = ((f32[32,4,128]{2,1,0:T(4,128)}), f32[32,4,128]{2,1,0:T(4,128)S(1)}, u32[]{:S(2)}, u32[]{:S(2)}) async-start(f32[32,4,128]{2,1,0:T(4,128)} %get-tuple-element.22), calls=%async_computation.3 | async-start | bytes 131072 | tf_op jit(solution)/shard_map/all_to_all | solution.py:341
  80.0 0.0 all-gather.7.cloned.1.call-start
  80.1 0.7 slice.9
  80.8 8.1 %all-to-all-done.3.got_ref.began_ref = f32[32,4,128]{2,1,0:T(4,128)S(1)} async-done(((f32[32,4,128]{2,1,0:T(4,128)}), f32[32,4,128]{2,1,0:T(4,128)S(1)}, u32[]{:S(2)}, u32[]{:S(2)}) %all-to-all-start.3) | async-done | bytes 65568 | tf_op jit(solution)/shard_map/all_to_all | solution.py:341
  88.9 0.0 all-gather.7.cloned.1.call-update
  88.9 0.2 half_cols.3
  89.2 22.1 %all_to_all.62.got_ref = f32[16,2,128]{2,1,0:T(2,128)S(1)} all-to-all(f32[16,2,128]{2,1,0:T(2,128)S(1)} %half_cols.3), channel_id=1, replica_groups=mesh['z'=8,'core'=2,'x'=4,'y'=8] {'z','core'}, dimensions={0} | all-to-all | bytes 32768 | tf_op jit(solution)/shard_map/all_to_all | solution.py:349
  111.3 0.3 half_rows.3
  111.6 11.7 %all_to_all.63.got_ref = f32[32,2,128]{2,1,0:T(2,128)S(1)} all-to-all(f32[32,2,128]{2,1,0:T(2,128)S(1)} %half_rows.3), channel_id=1, replica_groups=mesh['z'=8,'core'=2,'x'=4,'y'=8] {'x','y'}, dimensions={0} | all-to-all | bytes 65536 | tf_op jit(solution)/shard_map/all_to_all | solution.py:341
  123.3 0.0 all-gather.5.cloned.1.call-done.block_ref
  123.3 1.8 first_wide.1
  125.1 15.0 %all_to_all.64.got_ref = f32[16,16,128]{2,1,0:T(8,128)S(1)} all-to-all(f32[16,16,128]{2,1,0:T(8,128)S(1)} %get-tuple-element.25), channel_id=1, replica_groups=mesh['z'=8,'core'=2,'x'=4,'y'=8] {'z','core'}, dimensions={0} | all-to-all | bytes 262144 | tf_op jit(solution)/shard_map/all_to_all | solution.py:349
  140.1 0.6 half_rows.4
  140.7 8.1 %all_to_all.65.got_ref = f32[4,2,128]{2,1,0:T(2,128)S(1)} all-to-all(f32[4,2,128]{2,1,0:T(2,128)S(1)} %half_rows.4), channel_id=1, replica_groups=mesh['z'=8,'core'=2,'x'=4,'y'=8] {'x'}, dimensions={0} | all-to-all | bytes 8192 | tf_op jit(solution)/shard_map/all_to_all | solution.py:341
  148.9 0.7 half_cols.4
  149.6 14.1 %all_to_all.66.got_ref = f32[16,16,128]{2,1,0:T(8,128)S(1)} all-to-all(f32[16,16,128]{2,1,0:T(8,128)S(1)} %half_cols.4), channel_id=1, replica_groups=mesh['z'=8,'core'=2,'x'=4,'y'=8] {'z','core'}, dimensions={0} | all-to-all | bytes 262144 | tf_op jit(solution)/shard_map/all_to_all | solution.py:349
  163.6 0.6 half_rows.5
  164.2 6.5 %all_to_all.67.got_ref = f32[4,2,128]{2,1,0:T(2,128)S(1)} all-to-all(f32[4,2,128]{2,1,0:T(2,128)S(1)} %half_rows.5), channel_id=1, replica_groups=mesh['z'=8,'core'=2,'x'=4,'y'=8] {'x'}, dimensions={0} | all-to-all | bytes 8192 | tf_op jit(solution)/shard_map/all_to_all | solution.py:341
  170.7 0.7 half_cols.5
  171.4 13.2 %all_to_all.68.got_ref = f32[16,16,128]{2,1,0:T(8,128)S(1)} all-to-all(f32[16,16,128]{2,1,0:T(8,128)S(1)} %half_cols.5), channel_id=1, replica_groups=mesh['z'=8,'core'=2,'x'=4,'y'=8] {'z','core'}, dimensions={0} | all-to-all | bytes 262144 | tf_op jit(solution)/shard_map/all_to_all | solution.py:349
  184.6 0.0 all-gather.7.cloned.1.call-done.data_ref
  184.6 3.8 %final_terms.1 = (bf16[4,272,256]{2,1,0:T(8,128)(2,1)}, f32[16,128]{1,0:T(8,128)S(1)}) custom-call(f32[16,16,128]{2,1,0:T(8,128)S(1)} %all_to_all.68.got_ref, f32[256,2048]{1,0:T(8,128)S(1)} %get-tuple-element.26.block_ref.wide_ref, bf16[8,4,256,256]{3,2,1,0:T(8,128)(2,1)} %all-gather.7.cloned.1.call-done.data_ref), custom_call_target="tpu_custom_call" | custom-call | tf_op jit(solution)/shard_map/final_terms/pallas_call | solution.py:25
  188.4 3.5 %all-to-all-start.11 = ((bf16[4,272,256]{2,1,0:T(8,128)(2,1)}), bf16[4,272,256]{2,1,0:T(8,128)(2,1)S(1)}, u32[]{:S(2)}, u32[]{:S(2)}) async-start(bf16[4,272,256]{2,1,0:T(8,128)(2,1)} %get-tuple-element.28), calls=%async_computation.11 | async-start | bytes 1114112 | tf_op jit(solution)/shard_map/all_to_all | solution.py:357
  191.9 0.6 bitcast_add_fusion
  192.5 9.6 %all-to-all-done.11.got_ref = bf16[4,272,256]{2,1,0:T(8,128)(2,1)S(1)} async-done(((bf16[4,272,256]{2,1,0:T(8,128)(2,1)}), bf16[4,272,256]{2,1,0:T(8,128)(2,1)S(1)}, u32[]{:S(2)}, u32[]{:S(2)}) %all-to-all-start.11) | async-done | bytes 557088 | tf_op jit(solution)/shard_map/all_to_all | solution.py:357
  202.1 0.9 combine.1
  (2 shorter events, 0.0 us)
Async XLA Ops:
  7.2 62.4 %all-gather.9.cloned.1.call-start = ((), (), s32[]{:S(2)}) async-start(), calls=%async_computation.14 | async-start | bytes 2949120 | tf_op jit(solution)/shard_map/all_gather | solution.py:308
  7.2 0.9 copy-start
  45.4 17.7 %all-to-all-start.2 = ((bf16[4,8,96,256]{3,2,1,0:T(8,128)(2,1)}), bf16[4,8,96,256]{3,2,1,0:T(8,128)(2,1)S(1)}, u32[]{:S(2)}, u32[]{:S(2)}) async-start(bf16[4,8,96,256]{3,2,1,0:T(8,128)(2,1)} %broadcast_in_dim.2), calls=%async_computation.2 | async-start | bytes 3145728 | tf_op jit(solution)/shard_map/all_to_all | solution.py:312
  49.0 74.3 %all-gather.5.cloned.1.call-start = ((), (), s32[]{:S(2)}) async-start(), calls=%async_computation.12 | async-start | bytes 2359296 | tf_op jit(solution)/shard_map/all_gather | solution.py:337
  75.1 13.8 %all-to-all-start.3 = ((f32[32,4,128]{2,1,0:T(4,128)}), f32[32,4,128]{2,1,0:T(4,128)S(1)}, u32[]{:S(2)}, u32[]{:S(2)}) async-start(f32[32,4,128]{2,1,0:T(4,128)} %get-tuple-element.22), calls=%async_computation.3 | async-start | bytes 131072 | tf_op jit(solution)/shard_map/all_to_all | solution.py:341
  80.0 104.5 %all-gather.7.cloned.1.call-start = ((), (), s32[]{:S(2)}) async-start(), calls=%async_computation.13 | async-start | bytes 4456448 | tf_op jit(solution)/shard_map/all_gather | solution.py:344
  188.4 13.7 %all-to-all-start.11 = ((bf16[4,272,256]{2,1,0:T(8,128)(2,1)}), bf16[4,272,256]{2,1,0:T(8,128)(2,1)S(1)}, u32[]{:S(2)}, u32[]{:S(2)}) async-start(bf16[4,272,256]{2,1,0:T(8,128)(2,1)} %get-tuple-element.28), calls=%async_computation.11 | async-start | bytes 1114112 | tf_op jit(solution)/shard_map/all_to_all | solution.py:357
Sparse Core Ops, SparseCore 0:
  19.9 49.6 all-gather.8
  75.2 42.7 all-gather.4
  120.1 50.5 all-gather.6

commit v9 on v8

--- a/solution.py
+++ b/solution.py
@@ -54,17 +54,15 @@
     return top + jnp.log(jnp.sum(jnp.exp(got - top[None]), axis=0))
 
 
-def prepare_kernel(high, noise_ref, data_ref, by_x_ref, by_y_ref, sq_ref, held, sem):
-    nx = by_x_ref.shape[0]
+def prepare_kernel(high, noise_ref, data_ref, by_y_ref, sq_ref, held, sem):
     ny, sent, width = by_y_ref.shape
     rows = noise_ref.shape[0]
     low = rows - high
+    nx = data_ref.shape[1] // (ny * width)
     share = (sent - low) // nx
     at = (lax.axis_index(ROW[0]) * lax.axis_size(ROW[1]) + lax.axis_index(ROW[1])) * share
     copy = pltpu.make_async_copy(data_ref.at[pl.ds(pl.multiple_of(at, share), share), :], held, sem)
     copy.start()
-    for x in range(nx):
-        by_x_ref[x] = noise_ref[:high]
     for y in range(ny):
         by_y_ref[y, :low] = noise_ref[high:]
     squares = jnp.square(noise_ref[...].astype(F32))
@@ -79,9 +77,25 @@
 
 
 def inner_kernel(
-    scale, first_ref, second_ref, data_ref, pot_ref, sq_ref, out_ref, copy_ref, send_ref, rows_held, held, row_sems, sems
+    scale,
+    first_ref,
+    second_ref,
+    data_ref,
+    pot_ref,
+    sq_ref,
+    got_ref,
+    out_ref,
+    copy_ref,
+    send_ref,
+    piece_ref,
+    rows_held,
+    held,
+    row_sems,
+    sems,
 ):
     ny, nx, _, width = first_ref.shape
+    apart = pltpu.make_async_copy(got_ref.at[:, second_ref.shape[2] :], piece_ref, row_sems.at[nx])
+    apart.start()
     wide = ny * width
     copies = [
         (
@@ -116,6 +130,7 @@
         send_ref[:, k, :] = jnp.broadcast_to(local[:, lanes(k)], (members, LANES))
         send_ref[:, chunks + k, :] = jnp.broadcast_to(sq_ref[k : k + 1], (members, LANES))
     out.wait()
+    apart.wait()
 
 
 def row_top(block_ref, pot):
@@ -289,50 +304,51 @@
 
     low = rows - FIRST_ROWS
     share = cols // nrow
-    by_x, by_y, noise_sq = call(
+    part = lax.all_to_all(jnp.broadcast_to(noise[None, :FIRST_ROWS], (nx, FIRST_ROWS, width)), "x", 0, 0)
+    first = lax.all_gather(part, "y")
+    part, noise = lax.optimization_barrier((part, noise))
+    by_y, noise_sq = call(
         functools.partial(prepare_kernel, FIRST_ROWS),
         "prepare",
-        (
-            shape((nx, FIRST_ROWS, width), BF16),
-            shape((ny, low + nx * share, width), BF16),
-            shape((chunks, LANES)),
-        ),
+        (shape((ny, low + nx * share, width), BF16), shape((chunks, LANES))),
         [VMEM, HBM],
-        (VMEM, VMEM, VMEM),
+        (VMEM, VMEM),
         noise,
         data,
         scratch_shapes=[pltpu.VMEM((share, features), BF16), pltpu.SemaphoreType.DMA],
         vmem=52,
     )
-    part = lax.all_to_all(by_x, "x", 0, 0)
-    first = lax.all_gather(part, "y")
-    part, by_y = lax.optimization_barrier((part, by_y))
     got = lax.all_to_all(by_y, "y", 0, 0)
     second = jnp.broadcast_to(got[None, :, :low], (nx, ny, low, width))
     second = lax.all_to_all(second, "x", 0, 0)
-    piece = got[:, low:].reshape(ny, nx, share, width)
 
     data_sq = jnp.sum(jnp.square(data.astype(F32)), axis=1)
     col_pot = (data_sq * (-1.0 / (features * EPSILON))).reshape(-1, LANES)
     scale = 2.0 / (features * EPSILON)
-    scaled, copied, sent = call(
+    scaled, copied, sent, piece = call(
         functools.partial(inner_kernel, scale),
         "inner",
-        (shape((rows, cols)), shape((rows, cols)), shape((ncol, 2 * chunks, LANES))),
-        [HBM, VMEM, HBM, VMEM, VMEM],
-        (VMEM, HBM, VMEM),
+        (
+            shape((rows, cols)),
+            shape((rows, cols)),
+            shape((ncol, 2 * chunks, LANES)),
+            shape((ny, nx * share, width), BF16),
+        ),
+        [HBM, VMEM, HBM, VMEM, VMEM, HBM],
+        (VMEM, HBM, VMEM, HBM),
         first,
         second,
         data,
         col_pot,
         noise_sq,
+        got,
         scratch_shapes=[
             pltpu.VMEM(first.shape, BF16),
             pltpu.VMEM(data.shape, BF16),
-            pltpu.SemaphoreType.DMA((nx,)),
+            pltpu.SemaphoreType.DMA((nx + 1,)),
             pltpu.SemaphoreType.DMA((nx + 1,)),
         ],
-        vmem=51,
+        vmem=50,
     )
     wide = lax.all_gather(copied, "y", axis=1, tiled=True)
 
@@ -341,7 +357,7 @@
         got = lax.all_to_all(sent, "x" if step > WIDE_FROM else COL, 0, 0)
         if step == 0:
             began, piece = lax.optimization_barrier((got, piece))
-            mine = lax.all_gather(piece, ROW, axis=2, tiled=True)
+            mine = lax.all_gather(piece.reshape(ny, nx, share, width), ROW, axis=2, tiled=True)
         if step == WIDE_FROM:
             sent, wide = first_wide(got, wide, nrow, log_rows)
         else:

time: 210 us -> 211 us (level)
  blocking collectives: 126 us -> 140 us
  waiting for transfers between devices: 35.1 us -> 26.1 us
  starting transfers between devices: 12.1 us -> 7.17 us
    all_to_all x3 -> x4, blocking collectives: 26.3 us -> 40 us  [shards(): got = lax.all_to_all(sent, 'x' if step > WIDE_FROM else COL, 0, 0)]
    all_to_all x1 -> x0, waiting for transfers between devices: 8.08 us -> none  [shards(): got = lax.all_to_all(sent, 'x' if step > WIDE_FROM else COL, 0, 0)]
    all_to_all x1 -> x0, starting transfers between devices: 4.95 us -> none  [shards(): got = lax.all_to_all(sent, 'x' if step > WIDE_FROM else COL, 0, 0)]
  transfers between devices with their start and end apart: 6 -> 5, of which waited for: 4 -> 3; matrix products, arithmetic and copies ran while one was open for 3% -> 2% of each run, Pallas kernels for 2% -> 3%
where the time goes in v9:
time: 211 us; the launch traced here: 210 us
  blocking collectives  140 us (66%)
  waiting for transfers between devices  26.1 us (12%)
  Pallas kernels  15.7 us (7%)
  between operations  13.8 us (7%)
  starting transfers between devices  7.17 us (3%)
  other arithmetic  3.71 us (2%)
  local copies, waits for them, and re-layouts  3.2 us (2%)
    all_to_all x4, blocking collectives, shards(): got = lax.all_to_all(sent, ROW, 0, 0)  64.6 us
    all_to_all x4, blocking collectives, shards(): got = lax.all_to_all(sent, 'x' if step > WIDE_FROM else COL, 0, 0)  40 us
    all_to_all x1, blocking collectives, shards(): got = lax.all_to_all(by_y, 'y', 0, 0)  25.2 us
    pallas_call x11, Pallas kernels, call(): pl.pallas_call(kernel, out_shape=out_shape, in_specs=in_specs, out_specs=...  15.7 us
    all_to_all x1, waiting for transfers between devices, shards(): second = lax.all_to_all(second, 'x', 0, 0)  10.9 us
    all_to_all x1, blocking collectives, shards(): lax.all_to_all(jnp.broadcast_to(noise[None, :FIRST_ROWS], (nx, FIRST_ROWS...  10.6 us
    all_to_all x1, waiting for transfers between devices, shards(): got = lax.all_to_all(terms, 'x', 0, 0)  9.61 us
    all_gather x1, waiting for transfers between devices, shards(): first = lax.all_gather(part, 'y')  5.57 us
  transfers between devices with their start and end apart: 5, of which 3 were waited for; matrix products, arithmetic and copies ran while one was open for 2% of the time, Pallas kernels for 3%

profile of v9, /device:TPU:1, one launch (start us, length us, event | category | flops | bytes accessed | tf_op | source)
XLA Modules:
  0.0 210.2 jit_solution(14833439584802002536)
XLA Ops:
  7.2 0.0 all-gather.9.cloned.1.call-start
  7.2 0.9 slice.6
  8.1 10.6 %all_to_all.60 = bf16[4,160,256]{2,1,0:T(8,128)(2,1)} all-to-all(bf16[4,160,256]{2,1,0:T(8,128)(2,1)S(1)} %broadcast_in_dim.4), channel_id=1, replica_groups=mesh['z'=8,'core'=2,'x'=4,'y'=8] {'x'}, dimensions={0} | all-to-all | bytes 655360 | tf_op jit(solution)/shard_map/all_to_all | solution.py:307
  18.8 0.0 all-gather.9.cloned.1.call-update
  18.8 0.0 copy-start
  18.8 0.9 copy-done
  19.7 1.0 prepare.1
  20.7 25.2 %all_to_all.61.got_ref = bf16[8,160,256]{2,1,0:T(8,128)(2,1)S(1)} all-to-all(bf16[8,160,256]{2,1,0:T(8,128)(2,1)S(1)} %get-tuple-element.19), channel_id=1, replica_groups=mesh['z'=8,'core'=2,'x'=4,'y'=8] {'y'}, dimensions={0} | all-to-all | bytes 1310720 | tf_op jit(solution)/shard_map/all_to_all | solution.py:321
  46.0 1.4 broadcast_in_dim.5
  47.3 3.6 %all-to-all-start.2 = ((bf16[4,8,96,256]{3,2,1,0:T(8,128)(2,1)}), bf16[4,8,96,256]{3,2,1,0:T(8,128)(2,1)S(1)}, u32[]{:S(2)}, u32[]{:S(2)}) async-start(bf16[4,8,96,256]{3,2,1,0:T(8,128)(2,1)} %broadcast_in_dim.5), calls=%async_computation.2 | async-start | bytes 3145728 | tf_op jit(solution)/shard_map/all_to_all | solution.py:323
  50.9 0.0 all-gather.5.cloned.1.call-start
  50.9 3.1 %multiply_reduce_fusion = f32[256]{0:T(256)S(1)} fusion(bf16[256,8192]{1,0:T(8,128)(2,1)} %data_ref.3), kind=kLoop, calls=%fused_computation | loop fusion | flops 6291200 | bytes 4195328 | tf_op jit(solution)/shard_map/reduce_sum | solution.py:325
  54.1 10.9 %all-to-all-done.2.second_ref = bf16[4,8,96,256]{3,2,1,0:T(8,128)(2,1)S(1)} async-done(((bf16[4,8,96,256]{3,2,1,0:T(8,128)(2,1)}), bf16[4,8,96,256]{3,2,1,0:T(8,128)(2,1)S(1)}, u32[]{:S(2)}, u32[]{:S(2)}) %all-to-all-start.2) | async-done | bytes 1572896 | tf_op jit(solution)/shard_map/all_to_all | solution.py:323
  64.9 5.6 %all-gather.9.cloned.1.call-done = bf16[32,160,256]{2,1,0:T(8,128)(2,1)} async-done(((bf16[4,160,256]{2,1,0:T(8,128)(2,1)}), bf16[32,160,256]{2,1,0:T(8,128)(2,1)}) %all-gather.9.cloned.1.call-update) | async-done | bytes 2621456 | tf_op jit(solution)/shard_map/all_gather | solution.py:308
  70.5 5.0 %inner.1 = (f32[256,256]{1,0:T(8,128)S(1)}, f32[256,256]{1,0:T(8,128)}, f32[32,4,128]{2,1,0:T(4,128)S(1)}, bf16[8,64,256]{2,1,0:T(8,128)(2,1)}) custom-call(bf16[8,4,160,256]{3,2,1,0:T(8,128)(2,1)} %bitcast.7, bf16[4,8,96,256]{3,2,1,0:T(8,128)(2,1)S(1)} %all-to-all-done.2.second_ref, bf16[256,8192]{1,0:T(8,128)(2,1)} %data_ref.3, ...), custom_call_target="tpu_custom_call" | custom-call | tf_op jit(solution)/shard_map/inner/pallas_call | solution.py:25
  75.5 0.0 all-gather.5.cloned.1.call-update
  75.5 0.0 all-gather.7.cloned.1.call-start
  75.6 13.8 %all_to_all.62.got_ref.began_ref = f32[32,4,128]{2,1,0:T(4,128)S(1)} all-to-all(f32[32,4,128]{2,1,0:T(4,128)S(1)} %get-tuple-element.21), channel_id=1, replica_groups=mesh['z'=8,'core'=2,'x'=4,'y'=8] {'x','y'}, dimensions={0} | all-to-all | bytes 131072 | tf_op jit(solution)/shard_map/all_to_all | solution.py:357
  89.4 0.0 all-gather.7.cloned.1.call-update
  89.4 0.2 half_cols.3
  89.7 22.1 %all_to_all.63.got_ref = f32[16,2,128]{2,1,0:T(2,128)S(1)} all-to-all(f32[16,2,128]{2,1,0:T(2,128)S(1)} %half_cols.3), channel_id=1, replica_groups=mesh['z'=8,'core'=2,'x'=4,'y'=8] {'z','core'}, dimensions={0} | all-to-all | bytes 32768 | tf_op jit(solution)/shard_map/all_to_all | solution.py:365
  111.7 0.3 half_rows.3
  112.0 11.7 %all_to_all.64.got_ref = f32[32,2,128]{2,1,0:T(2,128)S(1)} all-to-all(f32[32,2,128]{2,1,0:T(2,128)S(1)} %half_rows.3), channel_id=1, replica_groups=mesh['z'=8,'core'=2,'x'=4,'y'=8] {'x','y'}, dimensions={0} | all-to-all | bytes 65536 | tf_op jit(solution)/shard_map/all_to_all | solution.py:357
  123.8 0.0 all-gather.5.cloned.1.call-done.block_ref
  123.8 1.8 first_wide.1
  125.6 15.1 %all_to_all.65.got_ref = f32[16,16,128]{2,1,0:T(8,128)S(1)} all-to-all(f32[16,16,128]{2,1,0:T(8,128)S(1)} %get-tuple-element.24), channel_id=1, replica_groups=mesh['z'=8,'core'=2,'x'=4,'y'=8] {'z','core'}, dimensions={0} | all-to-all | bytes 262144 | tf_op jit(solution)/shard_map/all_to_all | solution.py:365
  140.7 0.6 half_rows.4
  141.2 8.0 %all_to_all.66.got_ref = f32[4,2,128]{2,1,0:T(2,128)S(1)} all-to-all(f32[4,2,128]{2,1,0:T(2,128)S(1)} %half_rows.4), channel_id=1, replica_groups=mesh['z'=8,'core'=2,'x'=4,'y'=8] {'x'}, dimensions={0} | all-to-all | bytes 8192 | tf_op jit(solution)/shard_map/all_to_all | solution.py:357
  149.2 0.7 half_cols.4
  149.9 14.3 %all_to_all.67.got_ref = f32[16,16,128]{2,1,0:T(8,128)S(1)} all-to-all(f32[16,16,128]{2,1,0:T(8,128)S(1)} %half_cols.4), channel_id=1, replica_groups=mesh['z'=8,'core'=2,'x'=4,'y'=8] {'z','core'}, dimensions={0} | all-to-all | bytes 262144 | tf_op jit(solution)/shard_map/all_to_all | solution.py:365
  164.3 0.6 half_rows.5
  164.8 6.5 %all_to_all.68.got_ref = f32[4,2,128]{2,1,0:T(2,128)S(1)} all-to-all(f32[4,2,128]{2,1,0:T(2,128)S(1)} %half_rows.5), channel_id=1, replica_groups=mesh['z'=8,'core'=2,'x'=4,'y'=8] {'x'}, dimensions={0} | all-to-all | bytes 8192 | tf_op jit(solution)/shard_map/all_to_all | solution.py:357
  171.3 0.7 half_cols.5
  172.0 13.2 %all_to_all.69.got_ref = f32[16,16,128]{2,1,0:T(8,128)S(1)} all-to-all(f32[16,16,128]{2,1,0:T(8,128)S(1)} %half_cols.5), channel_id=1, replica_groups=mesh['z'=8,'core'=2,'x'=4,'y'=8] {'z','core'}, dimensions={0} | all-to-all | bytes 262144 | tf_op jit(solution)/shard_map/all_to_all | solution.py:365
  185.2 0.0 all-gather.7.cloned.1.call-done.data_ref
  185.2 3.8 %final_terms.1 = (bf16[4,272,256]{2,1,0:T(8,128)(2,1)}, f32[16,128]{1,0:T(8,128)S(1)}) custom-call(f32[16,16,128]{2,1,0:T(8,128)S(1)} %all_to_all.69.got_ref, f32[256,2048]{1,0:T(8,128)S(1)} %get-tuple-element.25.block_ref.wide_ref, bf16[8,4,256,256]{3,2,1,0:T(8,128)(2,1)} %all-gather.7.cloned.1.call-done.data_ref), custom_call_target="tpu_custom_call" | custom-call | tf_op jit(solution)/shard_map/final_terms/pallas_call | solution.py:25
  189.0 3.5 %all-to-all-start.11 = ((bf16[4,272,256]{2,1,0:T(8,128)(2,1)}), bf16[4,272,256]{2,1,0:T(8,128)(2,1)S(1)}, u32[]{:S(2)}, u32[]{:S(2)}) async-start(bf16[4,272,256]{2,1,0:T(8,128)(2,1)} %get-tuple-element.28), calls=%async_computation.11 | async-start | bytes 1114112 | tf_op jit(solution)/shard_map/all_to_all | solution.py:373
  192.5 0.6 bitcast_add_fusion
  193.1 9.6 %all-to-all-done.11.got_ref = bf16[4,272,256]{2,1,0:T(8,128)(2,1)S(1)} async-done(((bf16[4,272,256]{2,1,0:T(8,128)(2,1)}), bf16[4,272,256]{2,1,0:T(8,128)(2,1)S(1)}, u32[]{:S(2)}, u32[]{:S(2)}) %all-to-all-start.11) | async-done | bytes 557088 | tf_op jit(solution)/shard_map/all_to_all | solution.py:373
  202.7 0.9 combine.1
  (3 shorter events, 0.1 us)
Async XLA Ops:
  7.2 63.3 %all-gather.9.cloned.1.call-start = ((), (), s32[]{:S(2)}) async-start(), calls=%async_computation.14 | async-start | bytes 2949120 | tf_op jit(solution)/shard_map/all_gather | solution.py:308
  18.8 0.9 copy-start
  47.3 17.6 %all-to-all-start.2 = ((bf16[4,8,96,256]{3,2,1,0:T(8,128)(2,1)}), bf16[4,8,96,256]{3,2,1,0:T(8,128)(2,1)S(1)}, u32[]{:S(2)}, u32[]{:S(2)}) async-start(bf16[4,8,96,256]{3,2,1,0:T(8,128)(2,1)} %broadcast_in_dim.5), calls=%async_computation.2 | async-start | bytes 3145728 | tf_op jit(solution)/shard_map/all_to_all | solution.py:323
  50.9 72.9 %all-gather.5.cloned.1.call-start = ((), (), s32[]{:S(2)}) async-start(), calls=%async_computation.12 | async-start | bytes 2359296 | tf_op jit(solution)/shard_map/all_gather | solution.py:353
  75.5 109.7 %all-gather.7.cloned.1.call-start = ((), (), s32[]{:S(2)}) async-start(), calls=%async_computation.13 | async-start | bytes 4456448 | tf_op jit(solution)/shard_map/all_gather | solution.py:360
  189.0 13.7 %all-to-all-start.11 = ((bf16[4,272,256]{2,1,0:T(8,128)(2,1)}), bf16[4,272,256]{2,1,0:T(8,128)(2,1)S(1)}, u32[]{:S(2)}, u32[]{:S(2)}) async-start(bf16[4,272,256]{2,1,0:T(8,128)(2,1)} %get-tuple-element.28), calls=%async_computation.11 | async-start | bytes 1114112 | tf_op jit(solution)/shard_map/all_to_all | solution.py:373
Sparse Core Ops, SparseCore 0:
  18.9 51.5 all-gather.8
  75.6 42.7 all-gather.4
  120.5 50.6 all-gather.6

commit v10 on v9

--- a/solution.py
+++ b/solution.py
@@ -76,6 +76,20 @@
             by_y_ref[y, low + x * share : low + (x + 1) * share] = block
 
 
+def load_kernel(scale, after_ref, data_ref, out_ref, pot_ref, sems):
+    parts = pot_ref.shape[0]
+    copies = [pltpu.make_async_copy(data_ref.at[lanes(k)], out_ref.at[lanes(k)], sems.at[k]) for k in range(parts)]
+    for copy in copies:
+        copy.start()
+    for k in range(parts):
+        copies[k].wait()
+        total = None
+        for f in range(out_ref.shape[1] // LANES):
+            block = out_ref[lanes(k), lanes(f)].astype(F32)
+            total = block * block if total is None else total + block * block
+        pot_ref[k : k + 1, :] = as_rows(jnp.sum(total, axis=1, keepdims=True))[:1] * scale
+
+
 def inner_kernel(
     scale,
     first_ref,
@@ -88,40 +102,23 @@
     copy_ref,
     send_ref,
     piece_ref,
-    rows_held,
-    held,
-    row_sems,
     sems,
 ):
     ny, nx, _, width = first_ref.shape
-    apart = pltpu.make_async_copy(got_ref.at[:, second_ref.shape[2] :], piece_ref, row_sems.at[nx])
+    apart = pltpu.make_async_copy(got_ref.at[:, second_ref.shape[2] :], piece_ref, sems.at[0])
     apart.start()
     wide = ny * width
-    copies = [
-        (
-            pltpu.make_async_copy(
-                data_ref.at[:, x * wide : (x + 1) * wide], held.at[:, x * wide : (x + 1) * wide], sems.at[x]
-            ),
-            pltpu.make_async_copy(first_ref.at[:, x], rows_held.at[:, x], row_sems.at[x]),
-        )
-        for x in range(nx)
-    ]
-    for pair in copies:
-        for copy in pair:
-            copy.start()
     total = None
     for x in range(nx):
-        for copy in copies[x]:
-            copy.wait()
         for y in range(ny):
-            left = jnp.concatenate([rows_held[y, x], second_ref[x, y]], axis=0)
+            left = jnp.concatenate([first_ref[y, x], second_ref[x, y]], axis=0)
             at = x * wide + y * width
             one = lax.dot_general(
-                left, held[:, at : at + width], (((1,), (1,)), ((), ())), preferred_element_type=F32
+                left, data_ref[:, at : at + width], (((1,), (1,)), ((), ())), preferred_element_type=F32
             )
             total = one if total is None else total + one
     out_ref[...] = total * scale
-    out = pltpu.make_async_copy(out_ref, copy_ref, sems.at[nx])
+    out = pltpu.make_async_copy(out_ref, copy_ref, sems.at[1])
     out.start()
     local = local_rows(out_ref, pot_ref[...])
     chunks = local.shape[1] // LANES
@@ -280,12 +277,18 @@
     )
 
 
-def combine_kernel(log_rows, features, got_ref, began_ref, out_ref, pot_ref):
+def combine_kernel(log_rows, features, got_ref, began_ref, begin_ref, col_ref, out_ref, pot_ref, col_pot_ref):
     nx, rows = got_ref.shape[0], out_ref.shape[0]
     chunks = rows // LANES
     locals_ = [jnp.sum(got_ref[x, rows:, :].astype(F32), axis=0, keepdims=True) for x in range(nx)]
     top = functools.reduce(jnp.maximum, locals_)
     whole = top + jnp.log(functools.reduce(jnp.add, [jnp.exp(v - top) for v in locals_]))
+    parts = col_pot_ref.shape[0]
+    mine = lax.axis_index("y")
+    own = jnp.zeros(col_pot_ref.shape, F32)
+    for y in range(col_ref.shape[0] // parts):
+        own = jnp.where(mine == y, col_ref[y * parts : (y + 1) * parts, :], own)
+    col_pot_ref[...] = EPSILON * (own - begin_ref[...])
     noise_sq = jnp.sum(began_ref[:, chunks:, :], axis=0)
     for k in range(chunks):
         pot_ref[k : k + 1, :] = noise_sq[k : k + 1] * (1.0 / features) - EPSILON * (log_rows + whole[:, lanes(k)])
@@ -322,8 +325,18 @@
     second = jnp.broadcast_to(got[None, :, :low], (nx, ny, low, width))
     second = lax.all_to_all(second, "x", 0, 0)
 
-    data_sq = jnp.sum(jnp.square(data.astype(F32)), axis=1)
-    col_pot = (data_sq * (-1.0 / (features * EPSILON))).reshape(-1, LANES)
+    held, col_pot = call(
+        functools.partial(load_kernel, -1.0 / (features * EPSILON)),
+        "load",
+        (shape(data.shape, BF16), shape((cols // LANES, LANES))),
+        [HBM, HBM],
+        (VMEM, VMEM),
+        got,
+        data,
+        scratch_shapes=[pltpu.SemaphoreType.DMA((cols // LANES,))],
+        vmem=46,
+    )
+    begin_pot = col_pot
     scale = 2.0 / (features * EPSILON)
     scaled, copied, sent, piece = call(
         functools.partial(inner_kernel, scale),
@@ -334,21 +347,15 @@
             shape((ncol, 2 * chunks, LANES)),
             shape((ny, nx * share, width), BF16),
         ),
-        [HBM, VMEM, HBM, VMEM, VMEM, HBM],
+        [VMEM, VMEM, VMEM, VMEM, VMEM, HBM],
         (VMEM, HBM, VMEM, HBM),
         first,
         second,
-        data,
-        col_pot,
+        held,
+        begin_pot,
         noise_sq,
         got,
-        scratch_shapes=[
-            pltpu.VMEM(first.shape, BF16),
-            pltpu.VMEM(data.shape, BF16),
-            pltpu.SemaphoreType.DMA((nx + 1,)),
-            pltpu.SemaphoreType.DMA((nx + 1,)),
-        ],
-        vmem=50,
+        scratch_shapes=[pltpu.SemaphoreType.DMA((2,))],
     )
     wide = lax.all_gather(copied, "y", axis=1, tiled=True)
 
@@ -368,19 +375,19 @@
         elif step < ITERS - 1:
             sent = half_rows(got, wide, nx, log_cols)
     terms, col_pot = final_terms(got, wide, mine, log_cols)
-    own = lax.dynamic_slice_in_dim(col_pot, lax.axis_index("y") * (cols // LANES), cols // LANES, 0)
-    data_potential = data_sq / features + EPSILON * own.reshape(cols)
     got = lax.all_to_all(terms, "x", 0, 0)
-    targets, noise_potential = call(
+    targets, noise_potential, data_potential = call(
         functools.partial(combine_kernel, log_rows, features),
         "combine",
-        (shape((rows, width), BF16), shape((chunks, LANES))),
-        [VMEM, VMEM],
-        (VMEM, VMEM),
+        (shape((rows, width), BF16), shape((chunks, LANES)), shape(begin_pot.shape)),
+        [VMEM] * 4,
+        (VMEM, VMEM, VMEM),
         got,
         began,
-    )
-    return (noise_potential.reshape(rows), data_potential, targets)
+        begin_pot,
+        col_pot,
+    )
+    return (noise_potential.reshape(rows), data_potential.reshape(cols), targets)
 
 
 def _log(count):

time: 211 us -> 211 us (level)
  blocking collectives: 140 us -> 153 us
  waiting for transfers between devices: 26.1 us -> 14.8 us
  local copies, waits for them, and re-layouts: 3.2 us -> 9.09 us
  other arithmetic: 3.71 us -> 0 us
  starting transfers between devices: 7.17 us -> 3.69 us
    all_to_all x0 -> x1, blocking collectives: none -> 12.6 us  [shards(): got = lax.all_to_all(terms, 'x', 0, 0)]
    all_to_all x1 -> x0, waiting for transfers between devices: 9.61 us -> none  [shards(): got = lax.all_to_all(terms, 'x', 0, 0)]
    unnamed x2 -> x8, local copies, waits for them, and re-layouts: 0.9 us -> 6.77 us
    all_to_all x1 -> x0, starting transfers between devices: 3.48 us -> none  [shards(): got = lax.all_to_all(terms, 'x', 0, 0)]
    reduce_sum x1 -> x0, other arithmetic: 3.13 us -> none  [shards(): data_sq = jnp.sum(jnp.square(data.astype(F32)), axis=1)]
    pallas_call x11 -> x12, Pallas kernels: 15.7 us -> 15.5 us  [call(): pl.pallas_call(kernel, out_shape=out_shape, in_specs=in_specs, out_specs=...]
  transfers between devices with their start and end apart: 5 -> 4, of which waited for: 3 -> 2; matrix products, arithmetic and copies ran while one was open for 2% -> 1% of each run, Pallas kernels for 3% -> 4%
where the time goes in v10:
time: 211 us; the launch traced here: 210 us
  blocking collectives  153 us (73%)
  Pallas kernels  15.5 us (7%)
  waiting for transfers between devices  14.8 us (7%)
  between operations  13.8 us (7%)
  local copies, waits for them, and re-layouts  9.09 us (4%)
  starting transfers between devices  3.69 us (2%)
    all_to_all x4, blocking collectives, shards(): got = lax.all_to_all(sent, ROW, 0, 0)  64.5 us
    all_to_all x4, blocking collectives, shards(): got = lax.all_to_all(sent, 'x' if step > WIDE_FROM else COL, 0, 0)  40 us
    all_to_all x1, blocking collectives, shards(): got = lax.all_to_all(by_y, 'y', 0, 0)  25.2 us
    pallas_call x12, Pallas kernels, call(): pl.pallas_call(kernel, out_shape=out_shape, in_specs=in_specs, out_specs=...  15.5 us
    all_to_all x1, blocking collectives, shards(): got = lax.all_to_all(terms, 'x', 0, 0)  12.6 us
    all_to_all x1, blocking collectives, shards(): lax.all_to_all(jnp.broadcast_to(noise[None, :FIRST_ROWS], (nx, FIRST_ROWS...  10.6 us
    all_to_all x1, waiting for transfers between devices, shards(): second = lax.all_to_all(second, 'x', 0, 0)  9.23 us
    unnamed x8, local copies, waits for them, and re-layouts  6.77 us
  transfers between devices with their start and end apart: 4, of which 2 were waited for; matrix products, arithmetic and copies ran while one was open for 1% of the time, Pallas kernels for 4%

profile of v10, /device:TPU:1, one launch (start us, length us, event | category | flops | bytes accessed | tf_op | source)
XLA Modules:
  0.0 209.9 jit_solution(5745887923586093641)
XLA Ops:
  7.2 0.0 all-gather.9.cloned.1.call-start
  7.2 0.9 slice.6
  8.1 10.6 %all_to_all.60 = bf16[4,160,256]{2,1,0:T(8,128)(2,1)} all-to-all(bf16[4,160,256]{2,1,0:T(8,128)(2,1)S(1)} %broadcast_in_dim.4), channel_id=1, replica_groups=mesh['z'=8,'core'=2,'x'=4,'y'=8] {'x'}, dimensions={0} | all-to-all | bytes 655360 | tf_op jit(solution)/shard_map/all_to_all | solution.py:310
  18.8 0.0 all-gather.9.cloned.1.call-update
  18.8 0.0 copy-start.3
  18.8 0.9 copy-done.3
  19.7 1.0 prepare.1
  20.7 25.2 %all_to_all.61.after_ref.got_ref = bf16[8,160,256]{2,1,0:T(8,128)(2,1)S(1)} all-to-all(bf16[8,160,256]{2,1,0:T(8,128)(2,1)S(1)} %get-tuple-element.22), channel_id=1, replica_groups=mesh['z'=8,'core'=2,'x'=4,'y'=8] {'y'}, dimensions={0} | all-to-all | bytes 1310720 | tf_op jit(solution)/shard_map/all_to_all | solution.py:324
  46.0 1.4 broadcast_in_dim.5
  47.3 3.6 %all-to-all-start.2 = ((bf16[4,8,96,256]{3,2,1,0:T(8,128)(2,1)}), bf16[4,8,96,256]{3,2,1,0:T(8,128)(2,1)S(1)}, u32[]{:S(2)}, u32[]{:S(2)}) async-start(bf16[4,8,96,256]{3,2,1,0:T(8,128)(2,1)} %broadcast_in_dim.5), calls=%async_computation.2 | async-start | bytes 3145728 | tf_op jit(solution)/shard_map/all_to_all | solution.py:326
  50.9 0.0 all-gather.5.cloned.1.call-start
  51.0 2.8 %load.1 = (bf16[256,8192]{1,0:T(8,128)(2,1)S(1)}, f32[2,128]{1,0:T(2,128)S(1)}) custom-call(bf16[8,160,256]{2,1,0:T(8,128)(2,1)S(1)} %all_to_all.61.after_ref.got_ref, bf16[256,8192]{1,0:T(8,128)(2,1)} %data_ref.3), custom_call_target="tpu_custom_call" | custom-call | tf_op jit(solution)/shard_map/load/pallas_call | solution.py:25
  53.8 0.0 copy-start
  53.8 1.9 copy-done
  55.7 9.2 %all-to-all-done.2.second_ref = bf16[4,8,96,256]{3,2,1,0:T(8,128)(2,1)S(1)} async-done(((bf16[4,8,96,256]{3,2,1,0:T(8,128)(2,1)}), bf16[4,8,96,256]{3,2,1,0:T(8,128)(2,1)S(1)}, u32[]{:S(2)}, u32[]{:S(2)}) %all-to-all-start.2) | async-done | bytes 1572896 | tf_op jit(solution)/shard_map/all_to_all | solution.py:326
  65.0 5.5 %all-gather.9.cloned.1.call-done = bf16[32,160,256]{2,1,0:T(8,128)(2,1)} async-done(((bf16[4,160,256]{2,1,0:T(8,128)(2,1)}), bf16[32,160,256]{2,1,0:T(8,128)(2,1)}) %all-gather.9.cloned.1.call-update) | async-done | bytes 2621456 | tf_op jit(solution)/shard_map/all_gather | solution.py:311
  70.5 0.0 copy-start.1
  70.5 2.2 %copy-done.1 = bf16[256,8192]{1,0:T(8,128)(2,1)S(1)} copy-done((bf16[256,8192]{1,0:T(8,128)(2,1)S(1)}, bf16[256,8192]{1,0:T(8,128)(2,1)}, u32[]{:S(2)}) %copy-start.1) | copy-done | bytes 4194328
  72.7 0.0 copy-start.2
  72.7 1.7 copy-done.2
  74.4 2.2 %inner.1 = (f32[256,256]{1,0:T(8,128)S(1)}, f32[256,256]{1,0:T(8,128)}, f32[32,4,128]{2,1,0:T(4,128)S(1)}, bf16[8,64,256]{2,1,0:T(8,128)(2,1)}) custom-call(bf16[8,4,160,256]{3,2,1,0:T(8,128)(2,1)S(1)} %bitcast.4, bf16[4,8,96,256]{3,2,1,0:T(8,128)(2,1)S(1)} %all-to-all-done.2.second_ref, bf16[256,8192]{1,0:T(8,128)(2,1)S(1)} %copy-done.1, ...), custom_call_target="tpu_custom_call" | custom-call | tf_op jit(solution)/shard_map/inner/pallas_call | solution.py:25
  76.7 0.0 all-gather.5.cloned.1.call-update
  76.7 0.0 all-gather.7.cloned.1.call-start
  76.7 13.8 %all_to_all.62.got_ref.began_ref = f32[32,4,128]{2,1,0:T(4,128)S(1)} all-to-all(f32[32,4,128]{2,1,0:T(4,128)S(1)} %get-tuple-element.26), channel_id=1, replica_groups=mesh['z'=8,'core'=2,'x'=4,'y'=8] {'x','y'}, dimensions={0} | all-to-all | bytes 131072 | tf_op jit(solution)/shard_map/all_to_all | solution.py:364
  90.5 0.0 all-gather.7.cloned.1.call-update
  90.5 0.2 half_cols.3
  90.8 22.1 %all_to_all.63.got_ref = f32[16,2,128]{2,1,0:T(2,128)S(1)} all-to-all(f32[16,2,128]{2,1,0:T(2,128)S(1)} %half_cols.3), channel_id=1, replica_groups=mesh['z'=8,'core'=2,'x'=4,'y'=8] {'z','core'}, dimensions={0} | all-to-all | bytes 32768 | tf_op jit(solution)/shard_map/all_to_all | solution.py:372
  112.9 0.3 half_rows.3
  113.2 11.7 %all_to_all.64.got_ref = f32[32,2,128]{2,1,0:T(2,128)S(1)} all-to-all(f32[32,2,128]{2,1,0:T(2,128)S(1)} %half_rows.3), channel_id=1, replica_groups=mesh['z'=8,'core'=2,'x'=4,'y'=8] {'x','y'}, dimensions={0} | all-to-all | bytes 65536 | tf_op jit(solution)/shard_map/all_to_all | solution.py:364
  124.9 0.0 all-gather.5.cloned.1.call-done.block_ref
  125.0 1.8 first_wide.1
  126.8 15.1 %all_to_all.65.got_ref = f32[16,16,128]{2,1,0:T(8,128)S(1)} all-to-all(f32[16,16,128]{2,1,0:T(8,128)S(1)} %get-tuple-element.29), channel_id=1, replica_groups=mesh['z'=8,'core'=2,'x'=4,'y'=8] {'z','core'}, dimensions={0} | all-to-all | bytes 262144 | tf_op jit(solution)/shard_map/all_to_all | solution.py:372
  141.9 0.6 half_rows.4
  142.4 8.0 %all_to_all.66.got_ref = f32[4,2,128]{2,1,0:T(2,128)S(1)} all-to-all(f32[4,2,128]{2,1,0:T(2,128)S(1)} %half_rows.4), channel_id=1, replica_groups=mesh['z'=8,'core'=2,'x'=4,'y'=8] {'x'}, dimensions={0} | all-to-all | bytes 8192 | tf_op jit(solution)/shard_map/all_to_all | solution.py:364
  150.4 0.7 half_cols.4
  151.2 14.2 %all_to_all.67.got_ref = f32[16,16,128]{2,1,0:T(8,128)S(1)} all-to-all(f32[16,16,128]{2,1,0:T(8,128)S(1)} %half_cols.4), channel_id=1, replica_groups=mesh['z'=8,'core'=2,'x'=4,'y'=8] {'z','core'}, dimensions={0} | all-to-all | bytes 262144 | tf_op jit(solution)/shard_map/all_to_all | solution.py:372
  165.3 0.6 half_rows.5
  165.9 6.5 %all_to_all.68.got_ref = f32[4,2,128]{2,1,0:T(2,128)S(1)} all-to-all(f32[4,2,128]{2,1,0:T(2,128)S(1)} %half_rows.5), channel_id=1, replica_groups=mesh['z'=8,'core'=2,'x'=4,'y'=8] {'x'}, dimensions={0} | all-to-all | bytes 8192 | tf_op jit(solution)/shard_map/all_to_all | solution.py:364
  172.4 0.7 half_cols.5
  173.2 13.2 %all_to_all.69.got_ref = f32[16,16,128]{2,1,0:T(8,128)S(1)} all-to-all(f32[16,16,128]{2,1,0:T(8,128)S(1)} %half_cols.5), channel_id=1, replica_groups=mesh['z'=8,'core'=2,'x'=4,'y'=8] {'z','core'}, dimensions={0} | all-to-all | bytes 262144 | tf_op jit(solution)/shard_map/all_to_all | solution.py:372
  186.3 0.0 all-gather.7.cloned.1.call-done.data_ref
  186.3 3.5 %final_terms.1 = (bf16[4,272,256]{2,1,0:T(8,128)(2,1)S(1)}, f32[16,128]{1,0:T(8,128)S(1)}) custom-call(f32[16,16,128]{2,1,0:T(8,128)S(1)} %all_to_all.69.got_ref, f32[256,2048]{1,0:T(8,128)S(1)} %get-tuple-element.30.block_ref.wide_ref, bf16[8,4,256,256]{3,2,1,0:T(8,128)(2,1)} %all-gather.7.cloned.1.call-done.data_ref), custom_call_target="tpu_custom_call" | custom-call | tf_op jit(solution)/shard_map/final_terms/pallas_call | solution.py:25
  189.8 12.6 %all_to_all.70.got_ref = bf16[4,272,256]{2,1,0:T(8,128)(2,1)S(1)} all-to-all(bf16[4,272,256]{2,1,0:T(8,128)(2,1)S(1)} %get-tuple-element.33), channel_id=1, replica_groups=mesh['z'=8,'core'=2,'x'=4,'y'=8] {'x'}, dimensions={0} | all-to-all | bytes 1114112 | tf_op jit(solution)/shard_map/all_to_all | solution.py:378
  202.4 0.9 combine.1
  (2 shorter events, 0.0 us)
Async XLA Ops:
  7.2 63.3 %all-gather.9.cloned.1.call-start = ((), (), s32[]{:S(2)}) async-start(), calls=%async_computation.14 | async-start | bytes 2949120 | tf_op jit(solution)/shard_map/all_gather | solution.py:311
  18.8 0.9 copy-start.3
  47.3 17.6 %all-to-all-start.2 = ((bf16[4,8,96,256]{3,2,1,0:T(8,128)(2,1)}), bf16[4,8,96,256]{3,2,1,0:T(8,128)(2,1)S(1)}, u32[]{:S(2)}, u32[]{:S(2)}) async-start(bf16[4,8,96,256]{3,2,1,0:T(8,128)(2,1)} %broadcast_in_dim.5), calls=%async_computation.2 | async-start | bytes 3145728 | tf_op jit(solution)/shard_map/all_to_all | solution.py:326
  50.9 74.0 %all-gather.5.cloned.1.call-start = ((), (), s32[]{:S(2)}) async-start(), calls=%async_computation.12 | async-start | bytes 2359296 | tf_op jit(solution)/shard_map/all_gather | solution.py:360
  53.8 1.9 copy-start
  70.5 2.2 %copy-start.1 = (bf16[256,8192]{1,0:T(8,128)(2,1)S(1)}, bf16[256,8192]{1,0:T(8,128)(2,1)}, u32[]{:S(2)}) copy-start(bf16[256,8192]{1,0:T(8,128)(2,1)} %copy-done) | copy-start | bytes 12582916
  72.7 1.7 copy-start.2
  76.7 109.6 %all-gather.7.cloned.1.call-start = ((), (), s32[]{:S(2)}) async-start(), calls=%async_computation.13 | async-start | bytes 4456448 | tf_op jit(solution)/shard_map/all_gather | solution.py:367
Sparse Core Ops, SparseCore 0:
  18.9 51.5 all-gather.8
  76.8 42.7 all-gather.4
  121.7 50.5 all-gather.6

commit v11 on v9

--- a/solution.py
+++ b/solution.py
@@ -54,15 +54,17 @@
     return top + jnp.log(jnp.sum(jnp.exp(got - top[None]), axis=0))
 
 
-def prepare_kernel(high, noise_ref, data_ref, by_y_ref, sq_ref, held, sem):
+def prepare_kernel(high, noise_ref, data_ref, by_x_ref, by_y_ref, sq_ref, held, sem):
+    nx = by_x_ref.shape[0]
     ny, sent, width = by_y_ref.shape
     rows = noise_ref.shape[0]
     low = rows - high
-    nx = data_ref.shape[1] // (ny * width)
     share = (sent - low) // nx
     at = (lax.axis_index(ROW[0]) * lax.axis_size(ROW[1]) + lax.axis_index(ROW[1])) * share
     copy = pltpu.make_async_copy(data_ref.at[pl.ds(pl.multiple_of(at, share), share), :], held, sem)
     copy.start()
+    for x in range(nx):
+        by_x_ref[x] = noise_ref[:high]
     for y in range(ny):
         by_y_ref[y, :low] = noise_ref[high:]
     squares = jnp.square(noise_ref[...].astype(F32))
@@ -280,12 +282,18 @@
     )
 
 
-def combine_kernel(log_rows, features, got_ref, began_ref, out_ref, pot_ref):
+def combine_kernel(log_rows, features, got_ref, began_ref, begin_ref, col_ref, out_ref, pot_ref, col_pot_ref):
     nx, rows = got_ref.shape[0], out_ref.shape[0]
     chunks = rows // LANES
     locals_ = [jnp.sum(got_ref[x, rows:, :].astype(F32), axis=0, keepdims=True) for x in range(nx)]
     top = functools.reduce(jnp.maximum, locals_)
     whole = top + jnp.log(functools.reduce(jnp.add, [jnp.exp(v - top) for v in locals_]))
+    parts = col_pot_ref.shape[0]
+    mine = lax.axis_index("y")
+    own = jnp.zeros(col_pot_ref.shape, F32)
+    for y in range(col_ref.shape[0] // parts):
+        own = jnp.where(mine == y, col_ref[y * parts : (y + 1) * parts, :], own)
+    col_pot_ref[...] = EPSILON * (own - begin_ref[...])
     noise_sq = jnp.sum(began_ref[:, chunks:, :], axis=0)
     for k in range(chunks):
         pot_ref[k : k + 1, :] = noise_sq[k : k + 1] * (1.0 / features) - EPSILON * (log_rows + whole[:, lanes(k)])
@@ -304,26 +312,30 @@
 
     low = rows - FIRST_ROWS
     share = cols // nrow
-    part = lax.all_to_all(jnp.broadcast_to(noise[None, :FIRST_ROWS], (nx, FIRST_ROWS, width)), "x", 0, 0)
-    first = lax.all_gather(part, "y")
-    part, noise = lax.optimization_barrier((part, noise))
-    by_y, noise_sq = call(
+    by_x, by_y, noise_sq = call(
         functools.partial(prepare_kernel, FIRST_ROWS),
         "prepare",
-        (shape((ny, low + nx * share, width), BF16), shape((chunks, LANES))),
+        (
+            shape((nx, FIRST_ROWS, width), BF16),
+            shape((ny, low + nx * share, width), BF16),
+            shape((chunks, LANES)),
+        ),
         [VMEM, HBM],
-        (VMEM, VMEM),
+        (VMEM, VMEM, VMEM),
         noise,
         data,
         scratch_shapes=[pltpu.VMEM((share, features), BF16), pltpu.SemaphoreType.DMA],
         vmem=52,
     )
+    part = lax.all_to_all(by_x, "x", 0, 0)
+    first = lax.all_gather(part, "y")
+    part, by_y = lax.optimization_barrier((part, by_y))
     got = lax.all_to_all(by_y, "y", 0, 0)
     second = jnp.broadcast_to(got[None, :, :low], (nx, ny, low, width))
     second = lax.all_to_all(second, "x", 0, 0)
 
     data_sq = jnp.sum(jnp.square(data.astype(F32)), axis=1)
-    col_pot = (data_sq * (-1.0 / (features * EPSILON))).reshape(-1, LANES)
+    begin_pot = (data_sq * (-1.0 / (features * EPSILON))).reshape(-1, LANES)
     scale = 2.0 / (features * EPSILON)
     scaled, copied, sent, piece = call(
         functools.partial(inner_kernel, scale),
@@ -339,7 +351,7 @@
         first,
         second,
         data,
-        col_pot,
+        begin_pot,
         noise_sq,
         got,
         scratch_shapes=[
@@ -368,19 +380,19 @@
         elif step < ITERS - 1:
             sent = half_rows(got, wide, nx, log_cols)
     terms, col_pot = final_terms(got, wide, mine, log_cols)
-    own = lax.dynamic_slice_in_dim(col_pot, lax.axis_index("y") * (cols // LANES), cols // LANES, 0)
-    data_potential = data_sq / features + EPSILON * own.reshape(cols)
     got = lax.all_to_all(terms, "x", 0, 0)
-    targets, noise_potential = call(
+    targets, noise_potential, data_potential = call(
         functools.partial(combine_kernel, log_rows, features),
         "combine",
-        (shape((rows, width), BF16), shape((chunks, LANES))),
-        [VMEM, VMEM],
-        (VMEM, VMEM),
+        (shape((rows, width), BF16), shape((chunks, LANES)), shape(begin_pot.shape)),
+        [VMEM] * 4,
+        (VMEM, VMEM, VMEM),
         got,
         began,
-    )
-    return (noise_potential.reshape(rows), data_potential, targets)
+        begin_pot,
+        col_pot,
+    )
+    return (noise_potential.reshape(rows), data_potential.reshape(cols), targets)
 
 
 def _log(count):

time: 211 us -> 208 us (0.986)
  blocking collectives: 140 us -> 152 us
  waiting for transfers between devices: 26.1 us -> 17.4 us
  starting transfers between devices: 7.17 us -> 3.68 us
    all_to_all x1 -> x2, blocking collectives: 10.6 us -> 23.2 us  [the longest x1 12.5 us: shards(): got = lax.all_to_all(terms, 'x', 0, 0)]
    all_to_all x1 -> x0, waiting for transfers between devices: 9.61 us -> none  [shards(): got = lax.all_to_all(terms, 'x', 0, 0)]
    all_to_all x1 -> x0, starting transfers between devices: 3.48 us -> none  [shards(): got = lax.all_to_all(terms, 'x', 0, 0)]
  transfers between devices with their start and end apart: 5 -> 4, of which waited for: 3 -> 2; matrix products, arithmetic and copies ran while one was open for 2% -> 2% of each run, Pallas kernels for 3% -> 2%
where the time goes in v11:
time: 208 us; the launch traced here: 207 us
  blocking collectives  152 us (73%)
  waiting for transfers between devices  17.4 us (8%)
  Pallas kernels  15.4 us (7%)
  between operations  13.8 us (7%)
  starting transfers between devices  3.68 us (2%)
  other arithmetic  3.14 us (2%)
  local copies, waits for them, and re-layouts  2.27 us (1%)
    all_to_all x4, blocking collectives, shards(): got = lax.all_to_all(sent, ROW, 0, 0)  64.5 us
    all_to_all x4, blocking collectives, shards(): got = lax.all_to_all(sent, 'x' if step > WIDE_FROM else COL, 0, 0)  39.7 us
    all_to_all x1, blocking collectives, shards(): got = lax.all_to_all(by_y, 'y', 0, 0)  24.3 us
    pallas_call x11, Pallas kernels, call(): pl.pallas_call(kernel, out_shape=out_shape, in_specs=in_specs, out_specs=...  15.4 us
    all_to_all x1, blocking collectives, shards(): got = lax.all_to_all(terms, 'x', 0, 0)  12.5 us
    all_to_all x1, waiting for transfers between devices, shards(): second = lax.all_to_all(second, 'x', 0, 0)  10.9 us
    all_to_all x1, blocking collectives, shards(): part = lax.all_to_all(by_x, 'x', 0, 0)  10.6 us
    all_gather x1, waiting for transfers between devices, shards(): first = lax.all_gather(part, 'y')  6.48 us
  transfers between devices with their start and end apart: 4, of which 2 were waited for; matrix products, arithmetic and copies ran while one was open for 2% of the time, Pallas kernels for 2%

profile of v11, /device:TPU:1, one launch (start us, length us, event | category | flops | bytes accessed | tf_op | source)
XLA Modules:
  0.0 207.4 jit_solution(12956607961838816314)
XLA Ops:
  7.2 0.0 all-gather.9.cloned.1.call-start
  7.2 0.0 copy-start
  7.2 0.9 copy-done
  8.1 1.0 prepare.1
  9.1 10.6 %all_to_all.60 = bf16[4,160,256]{2,1,0:T(8,128)(2,1)} all-to-all(bf16[4,160,256]{2,1,0:T(8,128)(2,1)S(1)} %get-tuple-element.20), channel_id=1, replica_groups=mesh['z'=8,'core'=2,'x'=4,'y'=8] {'x'}, dimensions={0} | all-to-all | bytes 655360 | tf_op jit(solution)/shard_map/all_to_all | solution.py:330
  19.8 0.0 all-gather.9.cloned.1.call-update
  19.8 24.3 %all_to_all.61.got_ref = bf16[8,160,256]{2,1,0:T(8,128)(2,1)S(1)} all-to-all(bf16[8,160,256]{2,1,0:T(8,128)(2,1)S(1)} %get-tuple-element.22), channel_id=1, replica_groups=mesh['z'=8,'core'=2,'x'=4,'y'=8] {'y'}, dimensions={0} | all-to-all | bytes 1310720 | tf_op jit(solution)/shard_map/all_to_all | solution.py:333
  44.1 1.3 broadcast_in_dim.2
  45.4 3.6 %all-to-all-start.2 = ((bf16[4,8,96,256]{3,2,1,0:T(8,128)(2,1)}), bf16[4,8,96,256]{3,2,1,0:T(8,128)(2,1)S(1)}, u32[]{:S(2)}, u32[]{:S(2)}) async-start(bf16[4,8,96,256]{3,2,1,0:T(8,128)(2,1)} %broadcast_in_dim.2), calls=%async_computation.2 | async-start | bytes 3145728 | tf_op jit(solution)/shard_map/all_to_all | solution.py:335
  49.0 0.0 all-gather.5.cloned.1.call-start
  49.1 3.1 %multiply_reduce_fusion = f32[256]{0:T(256)S(1)} fusion(bf16[256,8192]{1,0:T(8,128)(2,1)} %data_ref.3), kind=kLoop, calls=%fused_computation | loop fusion | flops 6291200 | bytes 4195328 | tf_op jit(solution)/shard_map/reduce_sum | solution.py:337
  52.2 10.9 %all-to-all-done.2.second_ref = bf16[4,8,96,256]{3,2,1,0:T(8,128)(2,1)S(1)} async-done(((bf16[4,8,96,256]{3,2,1,0:T(8,128)(2,1)}), bf16[4,8,96,256]{3,2,1,0:T(8,128)(2,1)S(1)}, u32[]{:S(2)}, u32[]{:S(2)}) %all-to-all-start.2) | async-done | bytes 1572896 | tf_op jit(solution)/shard_map/all_to_all | solution.py:335
  63.1 6.5 %all-gather.9.cloned.1.call-done = bf16[32,160,256]{2,1,0:T(8,128)(2,1)} async-done(((bf16[4,160,256]{2,1,0:T(8,128)(2,1)}), bf16[32,160,256]{2,1,0:T(8,128)(2,1)}) %all-gather.9.cloned.1.call-update) | async-done | bytes 2621456 | tf_op jit(solution)/shard_map/all_gather | solution.py:331
  69.6 5.0 %inner.1 = (f32[256,256]{1,0:T(8,128)S(1)}, f32[256,256]{1,0:T(8,128)}, f32[32,4,128]{2,1,0:T(4,128)S(1)}, bf16[8,64,256]{2,1,0:T(8,128)(2,1)}) custom-call(bf16[8,4,160,256]{3,2,1,0:T(8,128)(2,1)} %bitcast.6, bf16[4,8,96,256]{3,2,1,0:T(8,128)(2,1)S(1)} %all-to-all-done.2.second_ref, bf16[256,8192]{1,0:T(8,128)(2,1)} %data_ref.3, ...), custom_call_target="tpu_custom_call" | custom-call | tf_op jit(solution)/shard_map/inner/pallas_call | solution.py:25
  74.5 0.0 all-gather.5.cloned.1.call-update
  74.6 0.0 all-gather.7.cloned.1.call-start
  74.6 13.6 %all_to_all.62.got_ref.began_ref = f32[32,4,128]{2,1,0:T(4,128)S(1)} all-to-all(f32[32,4,128]{2,1,0:T(4,128)S(1)} %get-tuple-element.24), channel_id=1, replica_groups=mesh['z'=8,'core'=2,'x'=4,'y'=8] {'x','y'}, dimensions={0} | all-to-all | bytes 131072 | tf_op jit(solution)/shard_map/all_to_all | solution.py:369
  88.2 0.0 all-gather.7.cloned.1.call-update
  88.2 0.2 half_cols.3
  88.5 22.1 %all_to_all.63.got_ref = f32[16,2,128]{2,1,0:T(2,128)S(1)} all-to-all(f32[16,2,128]{2,1,0:T(2,128)S(1)} %half_cols.3), channel_id=1, replica_groups=mesh['z'=8,'core'=2,'x'=4,'y'=8] {'z','core'}, dimensions={0} | all-to-all | bytes 32768 | tf_op jit(solution)/shard_map/all_to_all | solution.py:377
  110.6 0.3 half_rows.3
  110.9 11.7 %all_to_all.64.got_ref = f32[32,2,128]{2,1,0:T(2,128)S(1)} all-to-all(f32[32,2,128]{2,1,0:T(2,128)S(1)} %half_rows.3), channel_id=1, replica_groups=mesh['z'=8,'core'=2,'x'=4,'y'=8] {'x','y'}, dimensions={0} | all-to-all | bytes 65536 | tf_op jit(solution)/shard_map/all_to_all | solution.py:369
  122.6 0.0 all-gather.5.cloned.1.call-done.block_ref
  122.6 1.8 first_wide.1
  124.4 15.2 %all_to_all.65.got_ref = f32[16,16,128]{2,1,0:T(8,128)S(1)} all-to-all(f32[16,16,128]{2,1,0:T(8,128)S(1)} %get-tuple-element.27), channel_id=1, replica_groups=mesh['z'=8,'core'=2,'x'=4,'y'=8] {'z','core'}, dimensions={0} | all-to-all | bytes 262144 | tf_op jit(solution)/shard_map/all_to_all | solution.py:377
  139.6 0.6 half_rows.4
  140.2 7.9 %all_to_all.66.got_ref = f32[4,2,128]{2,1,0:T(2,128)S(1)} all-to-all(f32[4,2,128]{2,1,0:T(2,128)S(1)} %half_rows.4), channel_id=1, replica_groups=mesh['z'=8,'core'=2,'x'=4,'y'=8] {'x'}, dimensions={0} | all-to-all | bytes 8192 | tf_op jit(solution)/shard_map/all_to_all | solution.py:369
  148.2 0.8 half_cols.4
  148.9 14.2 %all_to_all.67.got_ref = f32[16,16,128]{2,1,0:T(8,128)S(1)} all-to-all(f32[16,16,128]{2,1,0:T(8,128)S(1)} %half_cols.4), channel_id=1, replica_groups=mesh['z'=8,'core'=2,'x'=4,'y'=8] {'z','core'}, dimensions={0} | all-to-all | bytes 262144 | tf_op jit(solution)/shard_map/all_to_all | solution.py:377
  163.1 0.6 half_rows.5
  163.7 6.5 %all_to_all.68.got_ref = f32[4,2,128]{2,1,0:T(2,128)S(1)} all-to-all(f32[4,2,128]{2,1,0:T(2,128)S(1)} %half_rows.5), channel_id=1, replica_groups=mesh['z'=8,'core'=2,'x'=4,'y'=8] {'x'}, dimensions={0} | all-to-all | bytes 8192 | tf_op jit(solution)/shard_map/all_to_all | solution.py:369
  170.2 0.7 half_cols.5
  171.0 12.9 %all_to_all.69.got_ref = f32[16,16,128]{2,1,0:T(8,128)S(1)} all-to-all(f32[16,16,128]{2,1,0:T(8,128)S(1)} %half_cols.5), channel_id=1, replica_groups=mesh['z'=8,'core'=2,'x'=4,'y'=8] {'z','core'}, dimensions={0} | all-to-all | bytes 262144 | tf_op jit(solution)/shard_map/all_to_all | solution.py:377
  183.9 0.0 all-gather.7.cloned.1.call-done.data_ref
  183.9 3.5 %final_terms.1 = (bf16[4,272,256]{2,1,0:T(8,128)(2,1)S(1)}, f32[16,128]{1,0:T(8,128)S(1)}) custom-call(f32[16,16,128]{2,1,0:T(8,128)S(1)} %all_to_all.69.got_ref, f32[256,2048]{1,0:T(8,128)S(1)} %get-tuple-element.28.block_ref.wide_ref, bf16[8,4,256,256]{3,2,1,0:T(8,128)(2,1)} %all-gather.7.cloned.1.call-done.data_ref), custom_call_target="tpu_custom_call" | custom-call | tf_op jit(solution)/shard_map/final_terms/pallas_call | solution.py:25
  187.4 12.5 %all_to_all.70.got_ref = bf16[4,272,256]{2,1,0:T(8,128)(2,1)S(1)} all-to-all(bf16[4,272,256]{2,1,0:T(8,128)(2,1)S(1)} %get-tuple-element.31), channel_id=1, replica_groups=mesh['z'=8,'core'=2,'x'=4,'y'=8] {'x'}, dimensions={0} | all-to-all | bytes 1114112 | tf_op jit(solution)/shard_map/all_to_all | solution.py:383
  199.9 0.9 combine.1
  (2 shorter events, 0.0 us)
Async XLA Ops:
  7.2 62.4 %all-gather.9.cloned.1.call-start = ((), (), s32[]{:S(2)}) async-start(), calls=%async_computation.14 | async-start | bytes 2949120 | tf_op jit(solution)/shard_map/all_gather | solution.py:331
  7.2 0.9 copy-start
  45.4 17.7 %all-to-all-start.2 = ((bf16[4,8,96,256]{3,2,1,0:T(8,128)(2,1)}), bf16[4,8,96,256]{3,2,1,0:T(8,128)(2,1)S(1)}, u32[]{:S(2)}, u32[]{:S(2)}) async-start(bf16[4,8,96,256]{3,2,1,0:T(8,128)(2,1)} %broadcast_in_dim.2), calls=%async_computation.2 | async-start | bytes 3145728 | tf_op jit(solution)/shard_map/all_to_all | solution.py:335
  49.0 73.6 %all-gather.5.cloned.1.call-start = ((), (), s32[]{:S(2)}) async-start(), calls=%async_computation.12 | async-start | bytes 2359296 | tf_op jit(solution)/shard_map/all_gather | solution.py:365
  74.6 109.3 %all-gather.7.cloned.1.call-start = ((), (), s32[]{:S(2)}) async-start(), calls=%async_computation.13 | async-start | bytes 4456448 | tf_op jit(solution)/shard_map/all_gather | solution.py:372
Sparse Core Ops, SparseCore 0:
  19.9 49.6 all-gather.8
  74.7 42.5 all-gather.4
  119.5 50.7 all-gather.6

commit v12 on v11

--- a/solution.py
+++ b/solution.py
@@ -187,33 +187,31 @@
 
 
 def first_wide_kernel(log_rows, got_ref, block_ref, out_ref, held_ref, sems):
-    parts = sems.shape[0]
-    places = out_ref.shape[1] // parts
-    width = places * LANES
+    parts, rows, width = block_ref.shape
+    places = width // LANES
     copies = [
-        pltpu.make_async_copy(
-            block_ref.at[:, k * width : (k + 1) * width], held_ref.at[:, k * width : (k + 1) * width], sems.at[k]
-        )
+        pltpu.make_async_copy(block_ref.at[k], held_ref.at[:, k * width : (k + 1) * width], sems.at[k])
         for k in range(parts)
     ]
     for copy in copies:
         copy.start()
-    pot = column_pot(got_ref, block_ref.shape[0] // LANES, log_rows)
+    pot = column_pot(got_ref, rows // LANES, log_rows)
     for k in range(parts):
         copies[k].wait()
         send_cols(held_ref, pot, out_ref, range(k * places, (k + 1) * places))
 
 
-def first_wide(got, block, members, log_rows):
+def first_wide(got, blocks, members, log_rows):
+    parts, rows, width = blocks.shape
     return call(
         functools.partial(first_wide_kernel, log_rows),
         "first_wide",
-        (shape((members, block.shape[1] // LANES, LANES)), shape(block.shape)),
+        (shape((members, parts * width // LANES, LANES)), shape((rows, parts * width))),
         [VMEM, HBM],
         (VMEM, VMEM),
         got,
-        block,
-        scratch_shapes=[pltpu.SemaphoreType.DMA((4,))],
+        blocks,
+        scratch_shapes=[pltpu.SemaphoreType.DMA((parts,))],
         vmem=51,
     )
 
@@ -223,9 +221,10 @@
 
 
 def final_kernel(log_cols, got_ref, wide_ref, data_ref, out_ref, pot_ref, weights, held, terms, sems):
-    ny, nx, cols, width = data_ref.shape
+    nrow, ny, nx, share, _ = data_ref.shape
+    cols = nrow * share
     rows = wide_ref.shape[0]
-    copies = [pltpu.make_async_copy(data_ref.at[y], held.at[y], sems.at[y]) for y in range(ny)]
+    copies = [pltpu.make_async_copy(data_ref.at[:, y], held.at[y], sems.at[y]) for y in range(ny)]
     for copy in copies:
         copy.start()
     pot = -(log_cols + joined(got_ref[...]))
@@ -249,19 +248,19 @@
     for copy in copies[:half]:
         copy.wait()
     for x in range(nx):
-        right = jnp.concatenate([held[y, x] for y in range(half)], axis=0)
+        right = jnp.concatenate([held[y, r, x] for y in range(half) for r in range(nrow)], axis=0)
         terms[x] = jnp.dot(weights[:, : half * cols], right, preferred_element_type=F32)
     for copy in copies[half:]:
         copy.wait()
     for x in range(nx):
-        right = jnp.concatenate([held[y, x] for y in range(half, ny)], axis=0)
+        right = jnp.concatenate([held[y, r, x] for y in range(half, ny) for r in range(nrow)], axis=0)
         term = terms[x] + jnp.dot(weights[:, half * cols :], right, preferred_element_type=F32)
         out_ref[x, :rows, :] = (term * inverse).astype(BF16)
         out_ref[x, rows:, :] = extra
 
 
 def final_terms(got, wide, data, log_cols):
-    ny, nx, cols, width = data.shape
+    nrow, ny, nx, share, width = data.shape
     rows = wide.shape[0]
     return call(
         functools.partial(final_kernel, log_cols),
@@ -274,7 +273,7 @@
         data,
         scratch_shapes=[
             pltpu.VMEM(wide.shape, BF16),
-            pltpu.VMEM(data.shape, BF16),
+            pltpu.VMEM((ny, nrow, nx, share, width), BF16),
             pltpu.VMEM((nx, rows, width), F32),
             pltpu.SemaphoreType.DMA((ny,)),
         ],
@@ -362,14 +361,14 @@
         ],
         vmem=50,
     )
-    wide = lax.all_gather(copied, "y", axis=1, tiled=True)
+    wide = lax.all_gather(copied, "y")
 
     began = None
     for step in range(ITERS):
         got = lax.all_to_all(sent, "x" if step > WIDE_FROM else COL, 0, 0)
         if step == 0:
             began, piece = lax.optimization_barrier((got, piece))
-            mine = lax.all_gather(piece.reshape(ny, nx, share, width), ROW, axis=2, tiled=True)
+            mine = lax.all_gather(piece.reshape(ny, nx, share, width), ROW)
         if step == WIDE_FROM:
             sent, wide = first_wide(got, wide, nrow, log_rows)
         else:

time: 208 us -> 208 us (level)
  no operation moved by 1% of the time
where the time goes in v12:
time: 208 us
  blocking collectives  152 us (73%)
  waiting for transfers between devices  17.4 us (8%)
  Pallas kernels  15.6 us (8%)
  between operations  13.8 us (7%)
  starting transfers between devices  3.68 us (2%)
  other arithmetic  3.14 us (2%)
  local copies, waits for them, and re-layouts  2.27 us (1%)
    all_to_all x4, blocking collectives, shards(): got = lax.all_to_all(sent, ROW, 0, 0)  64.6 us
    all_to_all x4, blocking collectives, shards(): got = lax.all_to_all(sent, 'x' if step > WIDE_FROM else COL, 0, 0)  39.7 us
    all_to_all x1, blocking collectives, shards(): got = lax.all_to_all(by_y, 'y', 0, 0)  24.3 us
    pallas_call x11, Pallas kernels, call(): pl.pallas_call(kernel, out_shape=out_shape, in_specs=in_specs, out_specs=...  15.6 us
    all_to_all x1, blocking collectives, shards(): got = lax.all_to_all(terms, 'x', 0, 0)  12.6 us
    all_to_all x1, waiting for transfers between devices, shards(): second = lax.all_to_all(second, 'x', 0, 0)  10.9 us
    all_to_all x1, blocking collectives, shards(): part = lax.all_to_all(by_x, 'x', 0, 0)  10.6 us
    all_gather x1, waiting for transfers between devices, shards(): first = lax.all_gather(part, 'y')  6.48 us
  transfers between devices with their start and end apart: 4, of which 2 were waited for; matrix products, arithmetic and copies ran while one was open for 2% of the time, Pallas kernels for 2%

profile of v12, /device:TPU:1, one launch (start us, length us, event | category | flops | bytes accessed | tf_op | source)
XLA Modules:
  0.0 207.7 jit_solution(14407138185434016688)
XLA Ops:
  7.2 0.0 all-gather.8.cloned.1.call-start
  7.2 0.0 copy-start
  7.2 0.9 copy-done
  8.1 1.0 prepare.1
  9.1 10.6 %all_to_all.60 = bf16[4,160,256]{2,1,0:T(8,128)(2,1)} all-to-all(bf16[4,160,256]{2,1,0:T(8,128)(2,1)S(1)} %get-tuple-element.20), channel_id=1, replica_groups=mesh['z'=8,'core'=2,'x'=4,'y'=8] {'x'}, dimensions={0} | all-to-all | bytes 655360 | tf_op jit(solution)/shard_map/all_to_all | solution.py:329
  19.8 0.0 all-gather.8.cloned.1.call-update
  19.8 24.3 %all_to_all.61.got_ref = bf16[8,160,256]{2,1,0:T(8,128)(2,1)S(1)} all-to-all(bf16[8,160,256]{2,1,0:T(8,128)(2,1)S(1)} %get-tuple-element.22), channel_id=1, replica_groups=mesh['z'=8,'core'=2,'x'=4,'y'=8] {'y'}, dimensions={0} | all-to-all | bytes 1310720 | tf_op jit(solution)/shard_map/all_to_all | solution.py:332
  44.1 1.3 broadcast_in_dim.2
  45.4 3.6 %all-to-all-start.2 = ((bf16[4,8,96,256]{3,2,1,0:T(8,128)(2,1)}), bf16[4,8,96,256]{3,2,1,0:T(8,128)(2,1)S(1)}, u32[]{:S(2)}, u32[]{:S(2)}) async-start(bf16[4,8,96,256]{3,2,1,0:T(8,128)(2,1)} %broadcast_in_dim.2), calls=%async_computation.2 | async-start | bytes 3145728 | tf_op jit(solution)/shard_map/all_to_all | solution.py:334
  49.0 0.0 all-gather.10.cloned.1.call-start
  49.1 3.1 %multiply_reduce_fusion = f32[256]{0:T(256)S(1)} fusion(bf16[256,8192]{1,0:T(8,128)(2,1)} %data_ref.3), kind=kLoop, calls=%fused_computation | loop fusion | flops 6291200 | bytes 4195328 | tf_op jit(solution)/shard_map/reduce_sum | solution.py:336
  52.2 10.9 %all-to-all-done.2.second_ref = bf16[4,8,96,256]{3,2,1,0:T(8,128)(2,1)S(1)} async-done(((bf16[4,8,96,256]{3,2,1,0:T(8,128)(2,1)}), bf16[4,8,96,256]{3,2,1,0:T(8,128)(2,1)S(1)}, u32[]{:S(2)}, u32[]{:S(2)}) %all-to-all-start.2) | async-done | bytes 1572896 | tf_op jit(solution)/shard_map/all_to_all | solution.py:334
  63.1 6.5 %all-gather.8.cloned.1.call-done = bf16[32,160,256]{2,1,0:T(8,128)(2,1)} async-done(((bf16[4,160,256]{2,1,0:T(8,128)(2,1)}), bf16[32,160,256]{2,1,0:T(8,128)(2,1)}) %all-gather.8.cloned.1.call-update) | async-done | bytes 2621456 | tf_op jit(solution)/shard_map/all_gather | solution.py:330
  69.6 5.0 %inner.1 = (f32[256,256]{1,0:T(8,128)S(1)}, f32[256,256]{1,0:T(8,128)}, f32[32,4,128]{2,1,0:T(4,128)S(1)}, bf16[8,64,256]{2,1,0:T(8,128)(2,1)}) custom-call(bf16[8,4,160,256]{3,2,1,0:T(8,128)(2,1)} %bitcast.7, bf16[4,8,96,256]{3,2,1,0:T(8,128)(2,1)S(1)} %all-to-all-done.2.second_ref, bf16[256,8192]{1,0:T(8,128)(2,1)} %data_ref.3, ...), custom_call_target="tpu_custom_call" | custom-call | tf_op jit(solution)/shard_map/inner/pallas_call | solution.py:25
  74.5 0.0 all-gather.10.cloned.1.call-update
  74.6 0.0 all-gather.6.cloned.1.call-start
  74.6 13.6 %all_to_all.62.got_ref.began_ref = f32[32,4,128]{2,1,0:T(4,128)S(1)} all-to-all(f32[32,4,128]{2,1,0:T(4,128)S(1)} %get-tuple-element.24), channel_id=1, replica_groups=mesh['z'=8,'core'=2,'x'=4,'y'=8] {'x','y'}, dimensions={0} | all-to-all | bytes 131072 | tf_op jit(solution)/shard_map/all_to_all | solution.py:368
  88.2 0.0 all-gather.6.cloned.1.call-update
  88.2 0.2 half_cols.3
  88.5 22.1 %all_to_all.63.got_ref = f32[16,2,128]{2,1,0:T(2,128)S(1)} all-to-all(f32[16,2,128]{2,1,0:T(2,128)S(1)} %half_cols.3), channel_id=1, replica_groups=mesh['z'=8,'core'=2,'x'=4,'y'=8] {'z','core'}, dimensions={0} | all-to-all | bytes 32768 | tf_op jit(solution)/shard_map/all_to_all | solution.py:376
  110.6 0.3 half_rows.3
  110.9 11.7 %all_to_all.64.got_ref = f32[32,2,128]{2,1,0:T(2,128)S(1)} all-to-all(f32[32,2,128]{2,1,0:T(2,128)S(1)} %half_rows.3), channel_id=1, replica_groups=mesh['z'=8,'core'=2,'x'=4,'y'=8] {'x','y'}, dimensions={0} | all-to-all | bytes 65536 | tf_op jit(solution)/shard_map/all_to_all | solution.py:368
  122.6 0.0 all-gather.10.cloned.1.call-done
  122.6 2.0 first_wide.1
  124.5 15.2 %all_to_all.65.got_ref = f32[16,16,128]{2,1,0:T(8,128)S(1)} all-to-all(f32[16,16,128]{2,1,0:T(8,128)S(1)} %get-tuple-element.27), channel_id=1, replica_groups=mesh['z'=8,'core'=2,'x'=4,'y'=8] {'z','core'}, dimensions={0} | all-to-all | bytes 262144 | tf_op jit(solution)/shard_map/all_to_all | solution.py:376
  139.7 0.6 half_rows.4
  140.3 7.9 %all_to_all.66.got_ref = f32[4,2,128]{2,1,0:T(2,128)S(1)} all-to-all(f32[4,2,128]{2,1,0:T(2,128)S(1)} %half_rows.4), channel_id=1, replica_groups=mesh['z'=8,'core'=2,'x'=4,'y'=8] {'x'}, dimensions={0} | all-to-all | bytes 8192 | tf_op jit(solution)/shard_map/all_to_all | solution.py:368
  148.3 0.8 half_cols.4
  149.0 14.1 %all_to_all.67.got_ref = f32[16,16,128]{2,1,0:T(8,128)S(1)} all-to-all(f32[16,16,128]{2,1,0:T(8,128)S(1)} %half_cols.4), channel_id=1, replica_groups=mesh['z'=8,'core'=2,'x'=4,'y'=8] {'z','core'}, dimensions={0} | all-to-all | bytes 262144 | tf_op jit(solution)/shard_map/all_to_all | solution.py:376
  163.2 0.6 half_rows.5
  163.7 6.5 %all_to_all.68.got_ref = f32[4,2,128]{2,1,0:T(2,128)S(1)} all-to-all(f32[4,2,128]{2,1,0:T(2,128)S(1)} %half_rows.5), channel_id=1, replica_groups=mesh['z'=8,'core'=2,'x'=4,'y'=8] {'x'}, dimensions={0} | all-to-all | bytes 8192 | tf_op jit(solution)/shard_map/all_to_all | solution.py:368
  170.2 0.7 half_cols.5
  171.0 13.2 %all_to_all.69.got_ref = f32[16,16,128]{2,1,0:T(8,128)S(1)} all-to-all(f32[16,16,128]{2,1,0:T(8,128)S(1)} %half_cols.5), channel_id=1, replica_groups=mesh['z'=8,'core'=2,'x'=4,'y'=8] {'z','core'}, dimensions={0} | all-to-all | bytes 262144 | tf_op jit(solution)/shard_map/all_to_all | solution.py:376
  184.2 0.0 all-gather.6.cloned.1.call-done.data_ref
  184.2 3.5 %final_terms.1 = (bf16[4,272,256]{2,1,0:T(8,128)(2,1)S(1)}, f32[16,128]{1,0:T(8,128)S(1)}) custom-call(f32[16,16,128]{2,1,0:T(8,128)S(1)} %all_to_all.69.got_ref, f32[256,2048]{1,0:T(8,128)S(1)} %get-tuple-element.28.block_ref.wide_ref, bf16[16,8,4,16,256]{4,3,2,1,0:T(8,128)(2,1)} %all-gather.6.cloned.1.call-done.data_ref), custom_call_target="tpu_custom_call" | custom-call | tf_op jit(solution)/shard_map/final_terms/pallas_call | solution.py:25
  187.7 12.6 %all_to_all.70.got_ref = bf16[4,272,256]{2,1,0:T(8,128)(2,1)S(1)} all-to-all(bf16[4,272,256]{2,1,0:T(8,128)(2,1)S(1)} %get-tuple-element.31), channel_id=1, replica_groups=mesh['z'=8,'core'=2,'x'=4,'y'=8] {'x'}, dimensions={0} | all-to-all | bytes 1114112 | tf_op jit(solution)/shard_map/all_to_all | solution.py:382
  200.2 0.9 combine.1
  (2 shorter events, 0.0 us)
Async XLA Ops:
  7.2 62.4 %all-gather.8.cloned.1.call-start = ((), (), s32[]{:S(2)}) async-start(), calls=%async_computation.13 | async-start | bytes 2949120 | tf_op jit(solution)/shard_map/all_gather | solution.py:330
  7.2 0.9 copy-start
  45.4 17.7 %all-to-all-start.2 = ((bf16[4,8,96,256]{3,2,1,0:T(8,128)(2,1)}), bf16[4,8,96,256]{3,2,1,0:T(8,128)(2,1)S(1)}, u32[]{:S(2)}, u32[]{:S(2)}) async-start(bf16[4,8,96,256]{3,2,1,0:T(8,128)(2,1)} %broadcast_in_dim.2), calls=%async_computation.2 | async-start | bytes 3145728 | tf_op jit(solution)/shard_map/all_to_all | solution.py:334
  49.0 73.6 %all-gather.10.cloned.1.call-start = ((), (), s32[]{:S(2)}) async-start(), calls=%async_computation.14 | async-start | bytes 2359296 | tf_op jit(solution)/shard_map/all_gather | solution.py:364
  74.6 109.6 %all-gather.6.cloned.1.call-start = ((), (), s32[]{:S(2)}) async-start(), calls=%async_computation.12 | async-start | bytes 4456448 | tf_op jit(solution)/shard_map/all_gather | solution.py:371
Sparse Core Ops, SparseCore 0:
  19.9 49.6 all-gather.7
  74.7 42.7 all-gather.9
  119.6 50.4 all-gather.5

commit v13 on v12

--- a/solution.py
+++ b/solution.py
@@ -13,7 +13,7 @@
 ROW = ("z", "core")
 COL = ("x", "y")
 LANES = 128
-FIRST_ROWS = 160
+FIRST_ROWS = 176
 WIDE_FROM = 1
 VMEM = pl.BlockSpec(memory_space=pltpu.VMEM)
 HBM = pl.BlockSpec(memory_space=pltpu.HBM)

time: 208 us -> 209 us (level)
  blocking collectives: 152 us -> 149 us
  waiting for transfers between devices: 17.4 us -> 20.1 us
    all_gather x1, waiting for transfers between devices: 6.48 us -> 11.2 us  [shards(): first = lax.all_gather(part, 'y')]
where the time goes in v13:
time: 209 us; the launch traced here: 208 us
  blocking collectives  149 us (71%)
  waiting for transfers between devices  20.1 us (10%)
  Pallas kernels  15.6 us (7%)
  between operations  13.8 us (7%)
  starting transfers between devices  3.66 us (2%)
  other arithmetic  3.14 us (2%)
  local copies, waits for them, and re-layouts  2.1 us (1%)
    all_to_all x4, blocking collectives, shards(): got = lax.all_to_all(sent, ROW, 0, 0)  62.5 us
    all_to_all x4, blocking collectives, shards(): got = lax.all_to_all(sent, 'x' if step > WIDE_FROM else COL, 0, 0)  40.4 us
    all_to_all x1, blocking collectives, shards(): got = lax.all_to_all(by_y, 'y', 0, 0)  23.1 us
    pallas_call x11, Pallas kernels, call(): pl.pallas_call(kernel, out_shape=out_shape, in_specs=in_specs, out_specs=...  15.6 us
    all_to_all x1, blocking collectives, shards(): got = lax.all_to_all(terms, 'x', 0, 0)  12.6 us
    all_gather x1, waiting for transfers between devices, shards(): first = lax.all_gather(part, 'y')  11.2 us
    all_to_all x1, blocking collectives, shards(): part = lax.all_to_all(by_x, 'x', 0, 0)  10.8 us
    all_to_all x1, waiting for transfers between devices, shards(): second = lax.all_to_all(second, 'x', 0, 0)  8.88 us
  transfers between devices with their start and end apart: 4, of which 2 were waited for; matrix products, arithmetic and copies ran while one was open for 2% of the time, Pallas kernels for 2%

profile of v13, /device:TPU:1, one launch (start us, length us, event | category | flops | bytes accessed | tf_op | source)
XLA Modules:
  0.0 207.9 jit_solution(6844056023814666295)
XLA Ops:
  7.2 0.0 all-gather.8.cloned.1.call-start
  7.2 0.0 copy-start
  7.2 0.9 copy-done
  8.1 1.0 prepare.1
  9.1 10.8 %all_to_all.60 = bf16[4,176,256]{2,1,0:T(8,128)(2,1)} all-to-all(bf16[4,176,256]{2,1,0:T(8,128)(2,1)S(1)} %get-tuple-element.20), channel_id=1, replica_groups=mesh['z'=8,'core'=2,'x'=4,'y'=8] {'x'}, dimensions={0} | all-to-all | bytes 720896 | tf_op jit(solution)/shard_map/all_to_all | solution.py:329
  19.9 0.0 all-gather.8.cloned.1.call-update
  19.9 23.1 %all_to_all.61.got_ref = bf16[8,144,256]{2,1,0:T(8,128)(2,1)S(1)} all-to-all(bf16[8,144,256]{2,1,0:T(8,128)(2,1)S(1)} %get-tuple-element.22), channel_id=1, replica_groups=mesh['z'=8,'core'=2,'x'=4,'y'=8] {'y'}, dimensions={0} | all-to-all | bytes 1179648 | tf_op jit(solution)/shard_map/all_to_all | solution.py:332
  43.0 1.2 broadcast_in_dim.2
  44.2 3.5 %all-to-all-start.2 = ((bf16[4,8,80,256]{3,2,1,0:T(8,128)(2,1)}), bf16[4,8,80,256]{3,2,1,0:T(8,128)(2,1)S(1)}, u32[]{:S(2)}, u32[]{:S(2)}) async-start(bf16[4,8,80,256]{3,2,1,0:T(8,128)(2,1)} %broadcast_in_dim.2), calls=%async_computation.2 | async-start | bytes 2621440 | tf_op jit(solution)/shard_map/all_to_all | solution.py:334
  47.8 0.0 all-gather.10.cloned.1.call-start
  47.8 3.1 %multiply_reduce_fusion = f32[256]{0:T(256)S(1)} fusion(bf16[256,8192]{1,0:T(8,128)(2,1)} %data_ref.3), kind=kLoop, calls=%fused_computation | loop fusion | flops 6291200 | bytes 4195328 | tf_op jit(solution)/shard_map/reduce_sum | solution.py:336
  51.0 8.9 %all-to-all-done.2.second_ref = bf16[4,8,80,256]{3,2,1,0:T(8,128)(2,1)S(1)} async-done(((bf16[4,8,80,256]{3,2,1,0:T(8,128)(2,1)}), bf16[4,8,80,256]{3,2,1,0:T(8,128)(2,1)S(1)}, u32[]{:S(2)}, u32[]{:S(2)}) %all-to-all-start.2) | async-done | bytes 1310752 | tf_op jit(solution)/shard_map/all_to_all | solution.py:334
  59.8 11.2 %all-gather.8.cloned.1.call-done = bf16[32,176,256]{2,1,0:T(8,128)(2,1)} async-done(((bf16[4,176,256]{2,1,0:T(8,128)(2,1)}), bf16[32,176,256]{2,1,0:T(8,128)(2,1)}) %all-gather.8.cloned.1.call-update) | async-done | bytes 2883600 | tf_op jit(solution)/shard_map/all_gather | solution.py:330
  71.1 5.0 %inner.1 = (f32[256,256]{1,0:T(8,128)S(1)}, f32[256,256]{1,0:T(8,128)}, f32[32,4,128]{2,1,0:T(4,128)S(1)}, bf16[8,64,256]{2,1,0:T(8,128)(2,1)}) custom-call(bf16[8,4,176,256]{3,2,1,0:T(8,128)(2,1)} %bitcast.7, bf16[4,8,80,256]{3,2,1,0:T(8,128)(2,1)S(1)} %all-to-all-done.2.second_ref, bf16[256,8192]{1,0:T(8,128)(2,1)} %data_ref.3, ...), custom_call_target="tpu_custom_call" | custom-call | tf_op jit(solution)/shard_map/inner/pallas_call | solution.py:25
  76.1 0.0 all-gather.10.cloned.1.call-update
  76.1 0.0 all-gather.6.cloned.1.call-start
  76.1 14.3 %all_to_all.62.got_ref.began_ref = f32[32,4,128]{2,1,0:T(4,128)S(1)} all-to-all(f32[32,4,128]{2,1,0:T(4,128)S(1)} %get-tuple-element.24), channel_id=1, replica_groups=mesh['z'=8,'core'=2,'x'=4,'y'=8] {'x','y'}, dimensions={0} | all-to-all | bytes 131072 | tf_op jit(solution)/shard_map/all_to_all | solution.py:368
  90.5 0.0 all-gather.6.cloned.1.call-update
  90.5 0.2 half_cols.3
  90.7 20.0 %all_to_all.63.got_ref = f32[16,2,128]{2,1,0:T(2,128)S(1)} all-to-all(f32[16,2,128]{2,1,0:T(2,128)S(1)} %half_cols.3), channel_id=1, replica_groups=mesh['z'=8,'core'=2,'x'=4,'y'=8] {'z','core'}, dimensions={0} | all-to-all | bytes 32768 | tf_op jit(solution)/shard_map/all_to_all | solution.py:376
  110.8 0.3 half_rows.3
  111.1 11.7 %all_to_all.64.got_ref = f32[32,2,128]{2,1,0:T(2,128)S(1)} all-to-all(f32[32,2,128]{2,1,0:T(2,128)S(1)} %half_rows.3), channel_id=1, replica_groups=mesh['z'=8,'core'=2,'x'=4,'y'=8] {'x','y'}, dimensions={0} | all-to-all | bytes 65536 | tf_op jit(solution)/shard_map/all_to_all | solution.py:368
  122.8 0.0 all-gather.10.cloned.1.call-done
  122.8 2.0 first_wide.1
  124.7 15.2 %all_to_all.65.got_ref = f32[16,16,128]{2,1,0:T(8,128)S(1)} all-to-all(f32[16,16,128]{2,1,0:T(8,128)S(1)} %get-tuple-element.27), channel_id=1, replica_groups=mesh['z'=8,'core'=2,'x'=4,'y'=8] {'z','core'}, dimensions={0} | all-to-all | bytes 262144 | tf_op jit(solution)/shard_map/all_to_all | solution.py:376
  139.9 0.6 half_rows.4
  140.5 7.9 %all_to_all.66.got_ref = f32[4,2,128]{2,1,0:T(2,128)S(1)} all-to-all(f32[4,2,128]{2,1,0:T(2,128)S(1)} %half_rows.4), channel_id=1, replica_groups=mesh['z'=8,'core'=2,'x'=4,'y'=8] {'x'}, dimensions={0} | all-to-all | bytes 8192 | tf_op jit(solution)/shard_map/all_to_all | solution.py:368
  148.5 0.8 half_cols.4
  149.2 14.1 %all_to_all.67.got_ref = f32[16,16,128]{2,1,0:T(8,128)S(1)} all-to-all(f32[16,16,128]{2,1,0:T(8,128)S(1)} %half_cols.4), channel_id=1, replica_groups=mesh['z'=8,'core'=2,'x'=4,'y'=8] {'z','core'}, dimensions={0} | all-to-all | bytes 262144 | tf_op jit(solution)/shard_map/all_to_all | solution.py:376
  163.4 0.6 half_rows.5
  164.0 6.5 %all_to_all.68.got_ref = f32[4,2,128]{2,1,0:T(2,128)S(1)} all-to-all(f32[4,2,128]{2,1,0:T(2,128)S(1)} %half_rows.5), channel_id=1, replica_groups=mesh['z'=8,'core'=2,'x'=4,'y'=8] {'x'}, dimensions={0} | all-to-all | bytes 8192 | tf_op jit(solution)/shard_map/all_to_all | solution.py:368
  170.4 0.7 half_cols.5
  171.2 13.2 %all_to_all.69.got_ref = f32[16,16,128]{2,1,0:T(8,128)S(1)} all-to-all(f32[16,16,128]{2,1,0:T(8,128)S(1)} %half_cols.5), channel_id=1, replica_groups=mesh['z'=8,'core'=2,'x'=4,'y'=8] {'z','core'}, dimensions={0} | all-to-all | bytes 262144 | tf_op jit(solution)/shard_map/all_to_all | solution.py:376
  184.4 0.0 all-gather.6.cloned.1.call-done.data_ref
  184.4 3.5 %final_terms.1 = (bf16[4,272,256]{2,1,0:T(8,128)(2,1)S(1)}, f32[16,128]{1,0:T(8,128)S(1)}) custom-call(f32[16,16,128]{2,1,0:T(8,128)S(1)} %all_to_all.69.got_ref, f32[256,2048]{1,0:T(8,128)S(1)} %get-tuple-element.28.block_ref.wide_ref, bf16[16,8,4,16,256]{4,3,2,1,0:T(8,128)(2,1)} %all-gather.6.cloned.1.call-done.data_ref), custom_call_target="tpu_custom_call" | custom-call | tf_op jit(solution)/shard_map/final_terms/pallas_call | solution.py:25
  187.9 12.6 %all_to_all.70.got_ref = bf16[4,272,256]{2,1,0:T(8,128)(2,1)S(1)} all-to-all(bf16[4,272,256]{2,1,0:T(8,128)(2,1)S(1)} %get-tuple-element.31), channel_id=1, replica_groups=mesh['z'=8,'core'=2,'x'=4,'y'=8] {'x'}, dimensions={0} | all-to-all | bytes 1114112 | tf_op jit(solution)/shard_map/all_to_all | solution.py:382
  200.4 0.9 combine.1
  (2 shorter events, 0.0 us)
Async XLA Ops:
  7.2 63.9 %all-gather.8.cloned.1.call-start = ((), (), s32[]{:S(2)}) async-start(), calls=%async_computation.13 | async-start | bytes 3244032 | tf_op jit(solution)/shard_map/all_gather | solution.py:330
  7.2 0.9 copy-start
  44.2 15.6 %all-to-all-start.2 = ((bf16[4,8,80,256]{3,2,1,0:T(8,128)(2,1)}), bf16[4,8,80,256]{3,2,1,0:T(8,128)(2,1)S(1)}, u32[]{:S(2)}, u32[]{:S(2)}) async-start(bf16[4,8,80,256]{3,2,1,0:T(8,128)(2,1)} %broadcast_in_dim.2), calls=%async_computation.2 | async-start | bytes 2621440 | tf_op jit(solution)/shard_map/all_to_all | solution.py:334
  47.8 75.0 %all-gather.10.cloned.1.call-start = ((), (), s32[]{:S(2)}) async-start(), calls=%async_computation.14 | async-start | bytes 2359296 | tf_op jit(solution)/shard_map/all_gather | solution.py:364
  76.1 108.3 %all-gather.6.cloned.1.call-start = ((), (), s32[]{:S(2)}) async-start(), calls=%async_computation.12 | async-start | bytes 4456448 | tf_op jit(solution)/shard_map/all_gather | solution.py:371
Sparse Core Ops, SparseCore 0:
  20.1 50.9 all-gather.7
  76.2 41.4 all-gather.9
  119.8 50.5 all-gather.5

commit v14 on v13

--- a/solution.py
+++ b/solution.py
@@ -78,6 +78,20 @@
             by_y_ref[y, low + x * share : low + (x + 1) * share] = block
 
 
+def load_kernel(scale, after_ref, data_ref, out_ref, pot_ref, sems):
+    parts = pot_ref.shape[0]
+    copies = [pltpu.make_async_copy(data_ref.at[lanes(k)], out_ref.at[lanes(k)], sems.at[k]) for k in range(parts)]
+    for copy in copies:
+        copy.start()
+    for k in range(parts):
+        copies[k].wait()
+        total = None
+        for f in range(out_ref.shape[1] // LANES):
+            block = out_ref[lanes(k), lanes(f)].astype(F32)
+            total = block * block if total is None else total + block * block
+        pot_ref[k : k + 1, :] = as_rows(jnp.sum(total, axis=1, keepdims=True))[:1] * scale
+
+
 def inner_kernel(
     scale,
     first_ref,
@@ -90,40 +104,23 @@
     copy_ref,
     send_ref,
     piece_ref,
-    rows_held,
-    held,
-    row_sems,
     sems,
 ):
     ny, nx, _, width = first_ref.shape
-    apart = pltpu.make_async_copy(got_ref.at[:, second_ref.shape[2] :], piece_ref, row_sems.at[nx])
+    apart = pltpu.make_async_copy(got_ref.at[:, second_ref.shape[2] :], piece_ref, sems.at[0])
     apart.start()
     wide = ny * width
-    copies = [
-        (
-            pltpu.make_async_copy(
-                data_ref.at[:, x * wide : (x + 1) * wide], held.at[:, x * wide : (x + 1) * wide], sems.at[x]
-            ),
-            pltpu.make_async_copy(first_ref.at[:, x], rows_held.at[:, x], row_sems.at[x]),
-        )
-        for x in range(nx)
-    ]
-    for pair in copies:
-        for copy in pair:
-            copy.start()
     total = None
     for x in range(nx):
-        for copy in copies[x]:
-            copy.wait()
         for y in range(ny):
-            left = jnp.concatenate([rows_held[y, x], second_ref[x, y]], axis=0)
+            left = jnp.concatenate([first_ref[y, x], second_ref[x, y]], axis=0)
             at = x * wide + y * width
             one = lax.dot_general(
-                left, held[:, at : at + width], (((1,), (1,)), ((), ())), preferred_element_type=F32
+                left, data_ref[:, at : at + width], (((1,), (1,)), ((), ())), preferred_element_type=F32
             )
             total = one if total is None else total + one
     out_ref[...] = total * scale
-    out = pltpu.make_async_copy(out_ref, copy_ref, sems.at[nx])
+    out = pltpu.make_async_copy(out_ref, copy_ref, sems.at[1])
     out.start()
     local = local_rows(out_ref, pot_ref[...])
     chunks = local.shape[1] // LANES
@@ -333,8 +330,18 @@
     second = jnp.broadcast_to(got[None, :, :low], (nx, ny, low, width))
     second = lax.all_to_all(second, "x", 0, 0)
 
-    data_sq = jnp.sum(jnp.square(data.astype(F32)), axis=1)
-    begin_pot = (data_sq * (-1.0 / (features * EPSILON))).reshape(-1, LANES)
+    held, col_pot = call(
+        functools.partial(load_kernel, -1.0 / (features * EPSILON)),
+        "load",
+        (shape(data.shape, BF16), shape((cols // LANES, LANES))),
+        [HBM, HBM],
+        (VMEM, VMEM),
+        second,
+        data,
+        scratch_shapes=[pltpu.SemaphoreType.DMA((cols // LANES,))],
+        vmem=46,
+    )
+    begin_pot = col_pot
     scale = 2.0 / (features * EPSILON)
     scaled, copied, sent, piece = call(
         functools.partial(inner_kernel, scale),
@@ -345,21 +352,15 @@
             shape((ncol, 2 * chunks, LANES)),
             shape((ny, nx * share, width), BF16),
         ),
-        [HBM, VMEM, HBM, VMEM, VMEM, HBM],
+        [VMEM, VMEM, VMEM, VMEM, VMEM, HBM],
         (VMEM, HBM, VMEM, HBM),
         first,
         second,
-        data,
+        held,
         begin_pot,
         noise_sq,
         got,
-        scratch_shapes=[
-            pltpu.VMEM(first.shape, BF16),
-            pltpu.VMEM(data.shape, BF16),
-            pltpu.SemaphoreType.DMA((nx + 1,)),
-            pltpu.SemaphoreType.DMA((nx + 1,)),
-        ],
-        vmem=50,
+        scratch_shapes=[pltpu.SemaphoreType.DMA((2,))],
     )
     wide = lax.all_gather(copied, "y")
 

time: 209 us -> 210 us (level)
  blocking collectives: 149 us -> 164 us
  waiting for transfers between devices: 20.1 us -> 8.67 us
  local copies, waits for them, and re-layouts: 2.1 us -> 6.96 us
  starting transfers between devices: 3.66 us -> 0.12 us
  other arithmetic: 3.14 us -> 0 us
    all_to_all x0 -> x1, blocking collectives: none -> 14.5 us  [shards(): second = lax.all_to_all(second, 'x', 0, 0)]
    all_to_all x1 -> x0, waiting for transfers between devices: 8.88 us -> none  [shards(): second = lax.all_to_all(second, 'x', 0, 0)]
    unnamed x2 -> x8, local copies, waits for them, and re-layouts: 0.9 us -> 6.85 us
    all_to_all x1 -> x0, starting transfers between devices: 3.54 us -> none  [shards(): second = lax.all_to_all(second, 'x', 0, 0)]
    reduce_sum x1 -> x0, other arithmetic: 3.14 us -> none  [shards(): data_sq = jnp.sum(jnp.square(data.astype(F32)), axis=1)]
    all_gather x1, waiting for transfers between devices: 11.2 us -> 8.62 us  [shards(): first = lax.all_gather(part, 'y')]
    pallas_call x11 -> x12, Pallas kernels: 15.6 us -> 15.5 us  [call(): pl.pallas_call(kernel, out_shape=out_shape, in_specs=in_specs, out_specs=...]
  transfers between devices with their start and end apart: 4 -> 3, of which waited for: 2 -> 1; matrix products, arithmetic and copies ran while one was open for 2% -> 0% of each run, Pallas kernels for 2% -> 4%
where the time goes in v14:
time: 210 us; the launch traced here: 209 us
  blocking collectives  164 us (78%)
  Pallas kernels  15.5 us (7%)
  between operations  13.8 us (7%)
  waiting for transfers between devices  8.67 us (4%)
  local copies, waits for them, and re-layouts  6.96 us (3%)
    all_to_all x4, blocking collectives, shards(): got = lax.all_to_all(sent, ROW, 0, 0)  62.8 us
    all_to_all x4, blocking collectives, shards(): got = lax.all_to_all(sent, 'x' if step > WIDE_FROM else COL, 0, 0)  40.4 us
    all_to_all x1, blocking collectives, shards(): got = lax.all_to_all(by_y, 'y', 0, 0)  23.1 us
    pallas_call x12, Pallas kernels, call(): pl.pallas_call(kernel, out_shape=out_shape, in_specs=in_specs, out_specs=...  15.5 us
    all_to_all x1, blocking collectives, shards(): second = lax.all_to_all(second, 'x', 0, 0)  14.5 us
    all_to_all x1, blocking collectives, shards(): got = lax.all_to_all(terms, 'x', 0, 0)  12.6 us
    all_to_all x1, blocking collectives, shards(): part = lax.all_to_all(by_x, 'x', 0, 0)  10.8 us
    all_gather x1, waiting for transfers between devices, shards(): first = lax.all_gather(part, 'y')  8.62 us
  transfers between devices with their start and end apart: 3, of which 1 were waited for; matrix products, arithmetic and copies ran while one was open for 0% of the time, Pallas kernels for 4%

profile of v14, /device:TPU:1, one launch (start us, length us, event | category | flops | bytes accessed | tf_op | source)
XLA Modules:
  0.0 209.3 jit_solution(6663759535884008989)
XLA Ops:
  7.2 0.0 all-gather.8.cloned.1.call-start
  7.2 0.0 copy-start.3
  7.2 0.9 copy-done.3
  8.1 1.0 prepare.1
  9.1 10.8 %all_to_all.60 = bf16[4,176,256]{2,1,0:T(8,128)(2,1)} all-to-all(bf16[4,176,256]{2,1,0:T(8,128)(2,1)S(1)} %get-tuple-element.22), channel_id=1, replica_groups=mesh['z'=8,'core'=2,'x'=4,'y'=8] {'x'}, dimensions={0} | all-to-all | bytes 720896 | tf_op jit(solution)/shard_map/all_to_all | solution.py:326
  19.9 0.0 all-gather.8.cloned.1.call-update
  19.9 0.0 all-gather.10.cloned.1.call-start
  20.0 23.1 %all_to_all.61.got_ref = bf16[8,144,256]{2,1,0:T(8,128)(2,1)S(1)} all-to-all(bf16[8,144,256]{2,1,0:T(8,128)(2,1)S(1)} %get-tuple-element.24), channel_id=1, replica_groups=mesh['z'=8,'core'=2,'x'=4,'y'=8] {'y'}, dimensions={0} | all-to-all | bytes 1179648 | tf_op jit(solution)/shard_map/all_to_all | solution.py:329
  43.1 0.1 broadcast_in_dim.2
  43.2 14.5 %all_to_all.62.after_ref.second_ref = bf16[4,8,80,256]{3,2,1,0:T(8,128)(2,1)S(1)} all-to-all(bf16[4,8,80,256]{3,2,1,0:T(8,128)(2,1)S(1)} %broadcast_in_dim.2), channel_id=1, replica_groups=mesh['z'=8,'core'=2,'x'=4,'y'=8] {'x'}, dimensions={0} | all-to-all | bytes 2621440 | tf_op jit(solution)/shard_map/all_to_all | solution.py:331
  57.7 2.8 %load.1 = (bf16[256,8192]{1,0:T(8,128)(2,1)S(1)}, f32[2,128]{1,0:T(2,128)S(1)}) custom-call(bf16[4,8,80,256]{3,2,1,0:T(8,128)(2,1)S(1)} %all_to_all.62.after_ref.second_ref, bf16[256,8192]{1,0:T(8,128)(2,1)} %data_ref.3), custom_call_target="tpu_custom_call" | custom-call | tf_op jit(solution)/shard_map/load/pallas_call | solution.py:25
  60.5 0.0 copy-start
  60.5 1.9 copy-done
  62.5 8.6 %all-gather.8.cloned.1.call-done = bf16[32,176,256]{2,1,0:T(8,128)(2,1)} async-done(((bf16[4,176,256]{2,1,0:T(8,128)(2,1)}), bf16[32,176,256]{2,1,0:T(8,128)(2,1)}) %all-gather.8.cloned.1.call-update) | async-done | bytes 2883600 | tf_op jit(solution)/shard_map/all_gather | solution.py:327
  71.1 0.0 copy-start.1
  71.1 2.2 %copy-done.1 = bf16[256,8192]{1,0:T(8,128)(2,1)S(1)} copy-done((bf16[256,8192]{1,0:T(8,128)(2,1)S(1)}, bf16[256,8192]{1,0:T(8,128)(2,1)}, u32[]{:S(2)}) %copy-start.1) | copy-done | bytes 4194328
  73.3 0.0 copy-start.2
  73.3 1.8 copy-done.2
  75.1 2.2 %inner.1 = (f32[256,256]{1,0:T(8,128)S(1)}, f32[256,256]{1,0:T(8,128)}, f32[32,4,128]{2,1,0:T(4,128)S(1)}, bf16[8,64,256]{2,1,0:T(8,128)(2,1)}) custom-call(bf16[8,4,176,256]{3,2,1,0:T(8,128)(2,1)S(1)} %bitcast.5, bf16[4,8,80,256]{3,2,1,0:T(8,128)(2,1)S(1)} %all_to_all.62.after_ref.second_ref, bf16[256,8192]{1,0:T(8,128)(2,1)S(1)} %copy-done.1, ...), custom_call_target="tpu_custom_call" | custom-call | tf_op jit(solution)/shard_map/inner/pallas_call | solution.py:25
  77.3 0.0 all-gather.10.cloned.1.call-update
  77.4 0.0 all-gather.6.cloned.1.call-start
  77.4 14.3 %all_to_all.63.got_ref.began_ref = f32[32,4,128]{2,1,0:T(4,128)S(1)} all-to-all(f32[32,4,128]{2,1,0:T(4,128)S(1)} %get-tuple-element.28), channel_id=1, replica_groups=mesh['z'=8,'core'=2,'x'=4,'y'=8] {'x','y'}, dimensions={0} | all-to-all | bytes 131072 | tf_op jit(solution)/shard_map/all_to_all | solution.py:369
  91.7 0.0 all-gather.6.cloned.1.call-update
  91.8 0.2 half_cols.3
  92.0 20.1 %all_to_all.64.got_ref = f32[16,2,128]{2,1,0:T(2,128)S(1)} all-to-all(f32[16,2,128]{2,1,0:T(2,128)S(1)} %half_cols.3), channel_id=1, replica_groups=mesh['z'=8,'core'=2,'x'=4,'y'=8] {'z','core'}, dimensions={0} | all-to-all | bytes 32768 | tf_op jit(solution)/shard_map/all_to_all | solution.py:377
  112.1 0.3 half_rows.3
  112.4 11.7 %all_to_all.65.got_ref = f32[32,2,128]{2,1,0:T(2,128)S(1)} all-to-all(f32[32,2,128]{2,1,0:T(2,128)S(1)} %half_rows.3), channel_id=1, replica_groups=mesh['z'=8,'core'=2,'x'=4,'y'=8] {'x','y'}, dimensions={0} | all-to-all | bytes 65536 | tf_op jit(solution)/shard_map/all_to_all | solution.py:369
  124.1 0.0 all-gather.10.cloned.1.call-done
  124.1 1.9 first_wide.1
  126.0 15.2 %all_to_all.66.got_ref = f32[16,16,128]{2,1,0:T(8,128)S(1)} all-to-all(f32[16,16,128]{2,1,0:T(8,128)S(1)} %get-tuple-element.31), channel_id=1, replica_groups=mesh['z'=8,'core'=2,'x'=4,'y'=8] {'z','core'}, dimensions={0} | all-to-all | bytes 262144 | tf_op jit(solution)/shard_map/all_to_all | solution.py:377
  141.2 0.6 half_rows.4
  141.8 7.9 %all_to_all.67.got_ref = f32[4,2,128]{2,1,0:T(2,128)S(1)} all-to-all(f32[4,2,128]{2,1,0:T(2,128)S(1)} %half_rows.4), channel_id=1, replica_groups=mesh['z'=8,'core'=2,'x'=4,'y'=8] {'x'}, dimensions={0} | all-to-all | bytes 8192 | tf_op jit(solution)/shard_map/all_to_all | solution.py:369
  149.7 0.7 half_cols.4
  150.5 14.4 %all_to_all.68.got_ref = f32[16,16,128]{2,1,0:T(8,128)S(1)} all-to-all(f32[16,16,128]{2,1,0:T(8,128)S(1)} %half_cols.4), channel_id=1, replica_groups=mesh['z'=8,'core'=2,'x'=4,'y'=8] {'z','core'}, dimensions={0} | all-to-all | bytes 262144 | tf_op jit(solution)/shard_map/all_to_all | solution.py:377
  164.8 0.6 half_rows.5
  165.4 6.5 %all_to_all.69.got_ref = f32[4,2,128]{2,1,0:T(2,128)S(1)} all-to-all(f32[4,2,128]{2,1,0:T(2,128)S(1)} %half_rows.5), channel_id=1, replica_groups=mesh['z'=8,'core'=2,'x'=4,'y'=8] {'x'}, dimensions={0} | all-to-all | bytes 8192 | tf_op jit(solution)/shard_map/all_to_all | solution.py:369
  171.9 0.7 half_cols.5
  172.6 13.2 %all_to_all.70.got_ref = f32[16,16,128]{2,1,0:T(8,128)S(1)} all-to-all(f32[16,16,128]{2,1,0:T(8,128)S(1)} %half_cols.5), channel_id=1, replica_groups=mesh['z'=8,'core'=2,'x'=4,'y'=8] {'z','core'}, dimensions={0} | all-to-all | bytes 262144 | tf_op jit(solution)/shard_map/all_to_all | solution.py:377
  185.8 0.0 all-gather.6.cloned.1.call-done.data_ref
  185.8 3.5 %final_terms.1 = (bf16[4,272,256]{2,1,0:T(8,128)(2,1)S(1)}, f32[16,128]{1,0:T(8,128)S(1)}) custom-call(f32[16,16,128]{2,1,0:T(8,128)S(1)} %all_to_all.70.got_ref, f32[256,2048]{1,0:T(8,128)S(1)} %get-tuple-element.32.block_ref.wide_ref, bf16[16,8,4,16,256]{4,3,2,1,0:T(8,128)(2,1)} %all-gather.6.cloned.1.call-done.data_ref), custom_call_target="tpu_custom_call" | custom-call | tf_op jit(solution)/shard_map/final_terms/pallas_call | solution.py:25
  189.3 12.6 %all_to_all.71.got_ref = bf16[4,272,256]{2,1,0:T(8,128)(2,1)S(1)} all-to-all(bf16[4,272,256]{2,1,0:T(8,128)(2,1)S(1)} %get-tuple-element.35), channel_id=1, replica_groups=mesh['z'=8,'core'=2,'x'=4,'y'=8] {'x'}, dimensions={0} | all-to-all | bytes 1114112 | tf_op jit(solution)/shard_map/all_to_all | solution.py:383
  201.9 0.9 combine.1
  (1 shorter events, 0.0 us)
Async XLA Ops:
  7.2 63.9 %all-gather.8.cloned.1.call-start = ((), (), s32[]{:S(2)}) async-start(), calls=%async_computation.13 | async-start | bytes 3244032 | tf_op jit(solution)/shard_map/all_gather | solution.py:327
  7.2 0.9 copy-start.3
  19.9 104.1 %all-gather.10.cloned.1.call-start = ((), (), s32[]{:S(2)}) async-start(), calls=%async_computation.14 | async-start | bytes 2359296 | tf_op jit(solution)/shard_map/all_gather | solution.py:365
  60.5 2.0 copy-start
  71.1 2.2 %copy-start.1 = (bf16[256,8192]{1,0:T(8,128)(2,1)S(1)}, bf16[256,8192]{1,0:T(8,128)(2,1)}, u32[]{:S(2)}) copy-start(bf16[256,8192]{1,0:T(8,128)(2,1)} %copy-done) | copy-start | bytes 12582916
  73.3 1.8 copy-start.2
  77.4 108.4 %all-gather.6.cloned.1.call-start = ((), (), s32[]{:S(2)}) async-start(), calls=%async_computation.12 | async-start | bytes 4456448 | tf_op jit(solution)/shard_map/all_gather | solution.py:372
Sparse Core Ops, SparseCore 0:
  20.1 51.0 all-gather.7
  77.5 41.2 all-gather.9
  120.9 50.8 all-gather.5

commit v15 on v14

--- a/solution.py
+++ b/solution.py
@@ -78,16 +78,17 @@
             by_y_ref[y, low + x * share : low + (x + 1) * share] = block
 
 
-def load_kernel(scale, after_ref, data_ref, out_ref, pot_ref, sems):
+def load_kernel(scale, after_ref, data_ref, upper_ref, lower_ref, pot_ref, sems):
     parts = pot_ref.shape[0]
-    copies = [pltpu.make_async_copy(data_ref.at[lanes(k)], out_ref.at[lanes(k)], sems.at[k]) for k in range(parts)]
+    outs = (upper_ref, lower_ref)
+    copies = [pltpu.make_async_copy(data_ref.at[lanes(k)], outs[k], sems.at[k]) for k in range(parts)]
     for copy in copies:
         copy.start()
     for k in range(parts):
         copies[k].wait()
         total = None
-        for f in range(out_ref.shape[1] // LANES):
-            block = out_ref[lanes(k), lanes(f)].astype(F32)
+        for f in range(upper_ref.shape[1] // LANES):
+            block = outs[k][:, lanes(f)].astype(F32)
             total = block * block if total is None else total + block * block
         pot_ref[k : k + 1, :] = as_rows(jnp.sum(total, axis=1, keepdims=True))[:1] * scale
 
@@ -96,7 +97,8 @@
     scale,
     first_ref,
     second_ref,
-    data_ref,
+    upper_ref,
+    lower_ref,
     pot_ref,
     sq_ref,
     got_ref,
@@ -116,7 +118,7 @@
             left = jnp.concatenate([first_ref[y, x], second_ref[x, y]], axis=0)
             at = x * wide + y * width
             one = lax.dot_general(
-                left, data_ref[:, at : at + width], (((1,), (1,)), ((), ())), preferred_element_type=F32
+                left, jnp.concatenate([upper_ref[:, at : at + width], lower_ref[:, at : at + width]], axis=0), (((1,), (1,)), ((), ())), preferred_element_type=F32
             )
             total = one if total is None else total + one
     out_ref[...] = total * scale
@@ -330,12 +332,12 @@
     second = jnp.broadcast_to(got[None, :, :low], (nx, ny, low, width))
     second = lax.all_to_all(second, "x", 0, 0)
 
-    held, col_pot = call(
+    upper, lower, col_pot = call(
         functools.partial(load_kernel, -1.0 / (features * EPSILON)),
         "load",
-        (shape(data.shape, BF16), shape((cols // LANES, LANES))),
+        (shape((LANES, features), BF16), shape((LANES, features), BF16), shape((cols // LANES, LANES))),
         [HBM, HBM],
-        (VMEM, VMEM),
+        (VMEM, VMEM, VMEM),
         second,
         data,
         scratch_shapes=[pltpu.SemaphoreType.DMA((cols // LANES,))],
@@ -352,11 +354,12 @@
             shape((ncol, 2 * chunks, LANES)),
             shape((ny, nx * share, width), BF16),
         ),
-        [VMEM, VMEM, VMEM, VMEM, VMEM, HBM],
+        [VMEM, VMEM, VMEM, VMEM, VMEM, VMEM, HBM],
         (VMEM, HBM, VMEM, HBM),
         first,
         second,
-        held,
+        upper,
+        lower,
         begin_pot,
         noise_sq,
         got,

time: 210 us -> 211 us (level)
    unnamed x8 -> x12, local copies, waits for them, and re-layouts: 6.85 us -> 8.6 us
where the time goes in v15:
time: 211 us; the launch traced here: 210 us
  blocking collectives  164 us (78%)
  Pallas kernels  15.5 us (7%)
  between operations  13.8 us (7%)
  local copies, waits for them, and re-layouts  8.72 us (4%)
  waiting for transfers between devices  7.91 us (4%)
    all_to_all x4, blocking collectives, shards(): got = lax.all_to_all(sent, ROW, 0, 0)  62.8 us
    all_to_all x4, blocking collectives, shards(): got = lax.all_to_all(sent, 'x' if step > WIDE_FROM else COL, 0, 0)  40.4 us
    all_to_all x1, blocking collectives, shards(): got = lax.all_to_all(by_y, 'y', 0, 0)  23.1 us
    pallas_call x12, Pallas kernels, call(): pl.pallas_call(kernel, out_shape=out_shape, in_specs=in_specs, out_specs=...  15.5 us
    all_to_all x1, blocking collectives, shards(): second = lax.all_to_all(second, 'x', 0, 0)  14.5 us
    all_to_all x1, blocking collectives, shards(): got = lax.all_to_all(terms, 'x', 0, 0)  12.6 us
    all_to_all x1, blocking collectives, shards(): part = lax.all_to_all(by_x, 'x', 0, 0)  10.8 us
    unnamed x12, local copies, waits for them, and re-layouts  8.6 us
  transfers between devices with their start and end apart: 3, of which 1 were waited for; matrix products, arithmetic and copies ran while one was open for 0% of the time, Pallas kernels for 4%

profile of v15, /device:TPU:1, one launch (start us, length us, event | category | flops | bytes accessed | tf_op | source)
XLA Modules:
  0.0 210.3 jit_solution(12786135786106207841)
XLA Ops:
  7.2 0.0 all-gather.8.cloned.1.call-start
  7.2 0.0 copy-start.5
  7.2 0.9 copy-done.5
  8.1 1.0 prepare.1
  9.1 10.8 %all_to_all.60 = bf16[4,176,256]{2,1,0:T(8,128)(2,1)} all-to-all(bf16[4,176,256]{2,1,0:T(8,128)(2,1)S(1)} %get-tuple-element.23), channel_id=1, replica_groups=mesh['z'=8,'core'=2,'x'=4,'y'=8] {'x'}, dimensions={0} | all-to-all | bytes 720896 | tf_op jit(solution)/shard_map/all_to_all | solution.py:328
  19.9 0.0 all-gather.8.cloned.1.call-update
  19.9 0.0 all-gather.10.cloned.1.call-start
  20.0 23.1 %all_to_all.61.got_ref = bf16[8,144,256]{2,1,0:T(8,128)(2,1)S(1)} all-to-all(bf16[8,144,256]{2,1,0:T(8,128)(2,1)S(1)} %get-tuple-element.25), channel_id=1, replica_groups=mesh['z'=8,'core'=2,'x'=4,'y'=8] {'y'}, dimensions={0} | all-to-all | bytes 1179648 | tf_op jit(solution)/shard_map/all_to_all | solution.py:331
  43.1 0.1 broadcast_in_dim.2
  43.2 14.5 %all_to_all.62.after_ref.second_ref = bf16[4,8,80,256]{3,2,1,0:T(8,128)(2,1)S(1)} all-to-all(bf16[4,8,80,256]{3,2,1,0:T(8,128)(2,1)S(1)} %broadcast_in_dim.2), channel_id=1, replica_groups=mesh['z'=8,'core'=2,'x'=4,'y'=8] {'x'}, dimensions={0} | all-to-all | bytes 2621440 | tf_op jit(solution)/shard_map/all_to_all | solution.py:333
  57.7 2.8 %load.1 = (bf16[128,8192]{1,0:T(8,128)(2,1)S(1)}, bf16[128,8192]{1,0:T(8,128)(2,1)S(1)}, f32[2,128]{1,0:T(2,128)S(1)}) custom-call(bf16[4,8,80,256]{3,2,1,0:T(8,128)(2,1)S(1)} %all_to_all.62.after_ref.second_ref, bf16[256,8192]{1,0:T(8,128)(2,1)} %data_ref.3), custom_call_target="tpu_custom_call" | custom-call | tf_op jit(solution)/shard_map/load/pallas_call | solution.py:25
  60.5 0.0 copy-start.1
  60.5 1.3 copy-done.1
  61.9 0.0 copy-start.3
  61.9 1.4 copy-done.3
  63.3 7.9 %all-gather.8.cloned.1.call-done = bf16[32,176,256]{2,1,0:T(8,128)(2,1)} async-done(((bf16[4,176,256]{2,1,0:T(8,128)(2,1)}), bf16[32,176,256]{2,1,0:T(8,128)(2,1)}) %all-gather.8.cloned.1.call-update) | async-done | bytes 2883600 | tf_op jit(solution)/shard_map/all_gather | solution.py:329
  71.1 0.0 copy-start
  71.1 1.8 copy-done
  72.9 0.0 copy-start.2
  72.9 1.6 copy-done.2
  74.5 0.0 copy-start.4
  74.5 1.6 copy-done.4
  76.1 2.2 %inner.1 = (f32[256,256]{1,0:T(8,128)S(1)}, f32[256,256]{1,0:T(8,128)}, f32[32,4,128]{2,1,0:T(4,128)S(1)}, bf16[8,64,256]{2,1,0:T(8,128)(2,1)}) custom-call(bf16[8,4,176,256]{3,2,1,0:T(8,128)(2,1)S(1)} %bitcast.5, bf16[4,8,80,256]{3,2,1,0:T(8,128)(2,1)S(1)} %all_to_all.62.after_ref.second_ref, bf16[128,8192]{1,0:T(8,128)(2,1)S(1)} %copy-done.2, ...), custom_call_target="tpu_custom_call" | custom-call | tf_op jit(solution)/shard_map/inner/pallas_call | solution.py:25
  78.3 0.0 all-gather.10.cloned.1.call-update
  78.3 0.0 all-gather.6.cloned.1.call-start
  78.4 14.3 %all_to_all.63.got_ref.began_ref = f32[32,4,128]{2,1,0:T(4,128)S(1)} all-to-all(f32[32,4,128]{2,1,0:T(4,128)S(1)} %get-tuple-element.30), channel_id=1, replica_groups=mesh['z'=8,'core'=2,'x'=4,'y'=8] {'x','y'}, dimensions={0} | all-to-all | bytes 131072 | tf_op jit(solution)/shard_map/all_to_all | solution.py:372
  92.7 0.0 all-gather.6.cloned.1.call-update
  92.8 0.2 half_cols.3
  93.0 20.1 %all_to_all.64.got_ref = f32[16,2,128]{2,1,0:T(2,128)S(1)} all-to-all(f32[16,2,128]{2,1,0:T(2,128)S(1)} %half_cols.3), channel_id=1, replica_groups=mesh['z'=8,'core'=2,'x'=4,'y'=8] {'z','core'}, dimensions={0} | all-to-all | bytes 32768 | tf_op jit(solution)/shard_map/all_to_all | solution.py:380
  113.1 0.3 half_rows.3
  113.4 11.7 %all_to_all.65.got_ref = f32[32,2,128]{2,1,0:T(2,128)S(1)} all-to-all(f32[32,2,128]{2,1,0:T(2,128)S(1)} %half_rows.3), channel_id=1, replica_groups=mesh['z'=8,'core'=2,'x'=4,'y'=8] {'x','y'}, dimensions={0} | all-to-all | bytes 65536 | tf_op jit(solution)/shard_map/all_to_all | solution.py:372
  125.1 0.0 all-gather.10.cloned.1.call-done
  125.1 1.9 first_wide.1
  127.0 15.2 %all_to_all.66.got_ref = f32[16,16,128]{2,1,0:T(8,128)S(1)} all-to-all(f32[16,16,128]{2,1,0:T(8,128)S(1)} %get-tuple-element.33), channel_id=1, replica_groups=mesh['z'=8,'core'=2,'x'=4,'y'=8] {'z','core'}, dimensions={0} | all-to-all | bytes 262144 | tf_op jit(solution)/shard_map/all_to_all | solution.py:380
  142.2 0.6 half_rows.4
  142.8 7.9 %all_to_all.67.got_ref = f32[4,2,128]{2,1,0:T(2,128)S(1)} all-to-all(f32[4,2,128]{2,1,0:T(2,128)S(1)} %half_rows.4), channel_id=1, replica_groups=mesh['z'=8,'core'=2,'x'=4,'y'=8] {'x'}, dimensions={0} | all-to-all | bytes 8192 | tf_op jit(solution)/shard_map/all_to_all | solution.py:372
  150.7 0.7 half_cols.4
  151.4 14.4 %all_to_all.68.got_ref = f32[16,16,128]{2,1,0:T(8,128)S(1)} all-to-all(f32[16,16,128]{2,1,0:T(8,128)S(1)} %half_cols.4), channel_id=1, replica_groups=mesh['z'=8,'core'=2,'x'=4,'y'=8] {'z','core'}, dimensions={0} | all-to-all | bytes 262144 | tf_op jit(solution)/shard_map/all_to_all | solution.py:380
  165.8 0.6 half_rows.5
  166.4 6.5 %all_to_all.69.got_ref = f32[4,2,128]{2,1,0:T(2,128)S(1)} all-to-all(f32[4,2,128]{2,1,0:T(2,128)S(1)} %half_rows.5), channel_id=1, replica_groups=mesh['z'=8,'core'=2,'x'=4,'y'=8] {'x'}, dimensions={0} | all-to-all | bytes 8192 | tf_op jit(solution)/shard_map/all_to_all | solution.py:372
  172.9 0.7 half_cols.5
  173.6 13.2 %all_to_all.70.got_ref = f32[16,16,128]{2,1,0:T(8,128)S(1)} all-to-all(f32[16,16,128]{2,1,0:T(8,128)S(1)} %half_cols.5), channel_id=1, replica_groups=mesh['z'=8,'core'=2,'x'=4,'y'=8] {'z','core'}, dimensions={0} | all-to-all | bytes 262144 | tf_op jit(solution)/shard_map/all_to_all | solution.py:380
  186.8 0.0 all-gather.6.cloned.1.call-done.data_ref
  186.8 3.5 %final_terms.1 = (bf16[4,272,256]{2,1,0:T(8,128)(2,1)S(1)}, f32[16,128]{1,0:T(8,128)S(1)}) custom-call(f32[16,16,128]{2,1,0:T(8,128)S(1)} %all_to_all.70.got_ref, f32[256,2048]{1,0:T(8,128)S(1)} %get-tuple-element.34.block_ref.wide_ref, bf16[16,8,4,16,256]{4,3,2,1,0:T(8,128)(2,1)} %all-gather.6.cloned.1.call-done.data_ref), custom_call_target="tpu_custom_call" | custom-call | tf_op jit(solution)/shard_map/final_terms/pallas_call | solution.py:25
  190.3 12.6 %all_to_all.71.got_ref = bf16[4,272,256]{2,1,0:T(8,128)(2,1)S(1)} all-to-all(bf16[4,272,256]{2,1,0:T(8,128)(2,1)S(1)} %get-tuple-element.37), channel_id=1, replica_groups=mesh['z'=8,'core'=2,'x'=4,'y'=8] {'x'}, dimensions={0} | all-to-all | bytes 1114112 | tf_op jit(solution)/shard_map/all_to_all | solution.py:386
  202.8 0.9 combine.1
  (1 shorter events, 0.0 us)
Async XLA Ops:
  7.2 63.9 %all-gather.8.cloned.1.call-start = ((), (), s32[]{:S(2)}) async-start(), calls=%async_computation.13 | async-start | bytes 3244032 | tf_op jit(solution)/shard_map/all_gather | solution.py:329
  7.2 0.9 copy-start.5
  19.9 105.1 %all-gather.10.cloned.1.call-start = ((), (), s32[]{:S(2)}) async-start(), calls=%async_computation.14 | async-start | bytes 2359296 | tf_op jit(solution)/shard_map/all_gather | solution.py:368
  60.5 1.3 copy-start.1
  61.9 1.4 copy-start.3
  71.1 1.8 copy-start
  72.9 1.6 copy-start.2
  74.5 1.6 copy-start.4
  78.3 108.4 %all-gather.6.cloned.1.call-start = ((), (), s32[]{:S(2)}) async-start(), calls=%async_computation.12 | async-start | bytes 4456448 | tf_op jit(solution)/shard_map/all_gather | solution.py:375
Sparse Core Ops, SparseCore 0:
  20.1 51.0 all-gather.7
  78.5 41.2 all-gather.9
  121.9 50.8 all-gather.5
